TPU v7x, 32 devices: a whole 2x2x4 slice. The times are simulated.
32 devices in a mesh: dp: 2 (over x), blk: 16 (over z, y, core).
Axes of the slice: x: 2, y: 2, z: 4, core: 2. Of those that a mesh axis runs over, the one named last changes fastest.
Arguments:
- tokens: bfloat16 [16384, 768], P(('dp', 'blk')), may hold values from -6 to 6
- w_qkv: bfloat16 [768, 2304], replicated, may hold values from -0.21875 to 0.21875
- b_query: bfloat16 [768], replicated, may hold values from -1.796875 to 1.796875
- b_value: bfloat16 [768], replicated, may hold values from -1.796875 to 1.796875
- w_out: bfloat16 [768, 768], replicated, may hold values from -2.5 to 2.5
- b_out: bfloat16 [768], replicated, may hold values from -1.796875 to 1.796875
- gain_one: bfloat16 [768], replicated, may hold values from 0.5 to 1.5
- shift_one: bfloat16 [768], replicated, may hold values from -1.796875 to 1.796875
- w_up: bfloat16 [768, 3072], replicated, may hold values from -0.21875 to 0.21875
- b_up: bfloat16 [3072], replicated, may hold values from -1.796875 to 1.796875
- w_down: bfloat16 [3072, 768], replicated, may hold values from -0.109375 to 0.109375
- b_down: bfloat16 [768], replicated, may hold values from -1.796875 to 1.796875
- gain_two: bfloat16 [768], replicated, may hold values from 0.5 to 1.5
- shift_two: bfloat16 [768], replicated, may hold values from -1.796875 to 1.796875
- cluster_perm: int32 [2, 12, 8192], P('dp', None, 'blk'), may hold values from 0 to 8191, as said below
- cluster_pairs: int32 [2, 12, 64, 2], P('dp'), may hold values from 0 to 63, as said below
- cotangent: bfloat16 [16384, 768], P(('dp', 'blk')), may hold values from -6 to 6
Outputs:
- layer_out: bfloat16 [16384, 768], P(('dp', 'blk'))
- grad_tokens: bfloat16 [16384, 768], P(('dp', 'blk'))
- grad_w_qkv: float32 [768, 2304], replicated
- grad_b_query: float32 [768], replicated
- grad_b_value: float32 [768], replicated
- grad_w_out: float32 [768, 768], replicated
- grad_b_out: float32 [768], replicated
- grad_gain_one: float32 [768], replicated
- grad_shift_one: float32 [768], replicated
- grad_w_up: float32 [768, 3072], replicated
- grad_b_up: float32 [3072], replicated
- grad_w_down: float32 [3072, 768], replicated
- grad_b_down: float32 [768], replicated
- grad_gain_two: float32 [768], replicated
- grad_shift_two: float32 [768], replicated
Inputs may be any that keep to these rules, and one draw needn't show every extreme that they name: `cluster_perm`: for each item and head, a permutation of the item's 8192 positions that maps every aligned block of 512 positions onto itself; cluster c of the head is the 128 positions listed at places c * 128 to (c + 1) * 128 - 1. `cluster_pairs`: entry [i, h, c, p] names key-value cluster number p of query cluster c of head h in item i. The clusters of a device are, in each head, the 4 clusters of the positions it holds. Of the 96 entries of one device's query clusters (all heads and all p), at most 7 name clusters of one and the same device, and exactly 7 name clusters of some device.
All inputs are finite; a program needn't handle non-finite values.
Results may differ from a plain program's by a relative error of at most 0.015.
Values may be sent and summed in bfloat16 or wider, within the bound.
No kernel may reach another device: no remote copies, remote signals or barrier semaphores. Data moves between devices by JAX's collectives and lax.ppermute only.
A program may use at most 192 MiB of HBM per device.

v0:
```python
from functools import partial

import jax
import jax.numpy as jnp
from jax import lax
from jax.sharding import PartitionSpec as P

D = 768
HEADS = 12
HEAD_DIM = 64
CLUS = 128
PAIRS = 2


def layer_norm(values, scaling, offset):
    average = jnp.mean(values, -1, keepdims=True)
    centred = values - average
    variance = jnp.mean(centred * centred, -1, keepdims=True)
    return centred * lax.rsqrt(variance + 1e-06) * scaling + offset


def column_sums(matrix):
    return jnp.sum(matrix.astype(jnp.float32), axis=0)


def flatten_all(members, multiple):
    flattened = jnp.concatenate([member.reshape(-1) for member in members])
    padding = -flattened.shape[0] % multiple
    return jnp.pad(flattened, (0, padding))


def split_all(flattened, members):
    pieces_out = []
    offset = 0
    for member in members:
        length = member.size
        pieces_out.append(flattened[offset : offset + length].reshape(member.shape))
        offset = offset + length
    return pieces_out


def per_device(
    tokens,
    w_qkv,
    b_query,
    b_value,
    w_out,
    b_out,
    gain_one,
    shift_one,
    w_up,
    b_up,
    w_down,
    b_down,
    gain_two,
    shift_two,
    cluster_perm,
    cluster_pairs,
    cotangent,
):
    count_blk = lax.axis_size("blk")
    my_index = lax.axis_index("blk")
    rows_dev = tokens.shape[0]
    per_dev = rows_dev // CLUS
    requests = per_dev * HEADS * PAIRS
    capacity = max(2, (requests + count_blk - 1) // count_blk + 1)
    score_scale = HEAD_DIM ** (-0.5)
    pair_width = 2 * HEAD_DIM
    local_order = cluster_perm[0] - my_index * rows_dev
    inverse = jnp.argsort(local_order, axis=1)

    def sort_heads(tensor):
        shaped = tensor.reshape(rows_dev, HEADS, -1).transpose(1, 0, 2)
        return jnp.take_along_axis(shaped, local_order[:, :, None], axis=1)

    def unsort_heads(tensor):
        placed = jnp.take_along_axis(tensor, inverse[:, :, None], axis=1)
        return placed.transpose(1, 0, 2).reshape(rows_dev, -1)

    projected = jnp.dot(tokens, w_qkv, preferred_element_type=jnp.float32)
    queries = (projected[:, :D] + b_query.astype(jnp.float32)).astype(jnp.bfloat16)
    keys_all = projected[:, D : 2 * D].astype(jnp.bfloat16)
    values = (projected[:, 2 * D :] + b_value.astype(jnp.float32)).astype(jnp.bfloat16)
    q_sorted = sort_heads(queries).reshape(HEADS, per_dev, CLUS, HEAD_DIM)
    joined = jnp.concatenate(
        [keys_all.reshape(rows_dev, HEADS, HEAD_DIM), values.reshape(rows_dev, HEADS, HEAD_DIM)],
        axis=2,
    )
    kv_blocks = sort_heads(joined.reshape(rows_dev, HEADS * pair_width)).reshape(
        HEADS * per_dev, CLUS, pair_width
    )
    wanted = (
        cluster_pairs[0]
        .reshape(HEADS, count_blk, per_dev, PAIRS)
        .transpose(1, 0, 2, 3)
        .reshape(count_blk, requests)
    )
    source = wanted // per_dev
    within = wanted % per_dev
    positions = jnp.arange(requests, dtype=jnp.int32)
    earlier = positions[None, :] < positions[:, None]
    same_source = source[:, :, None] == source[:, None, :]
    slot_rank = jnp.sum(same_source & earlier[None], axis=2)
    head_of = positions // (per_dev * PAIRS)
    block_id = head_of[None, :] * per_dev + within
    matches = (source == my_index)[:, :, None] & (
        slot_rank[:, :, None] == jnp.arange(capacity, dtype=jnp.int32)[None, None, :]
    )
    filled = jnp.any(matches, axis=1)
    chosen = jnp.sum(jnp.where(matches, block_id[:, :, None], 0), axis=1)
    fetch_index = source[my_index] * capacity + slot_rank[my_index]
    segment = jnp.where(filled, chosen, HEADS * per_dev).reshape(-1)
    outgoing = kv_blocks[chosen]
    outgoing = jnp.where(filled[:, :, None, None], outgoing, jnp.zeros_like(outgoing))
    arrived = lax.all_to_all(outgoing, "blk", split_axis=0, concat_axis=0, tiled=True)
    pairs_kv = arrived.reshape(count_blk * capacity, CLUS, pair_width)[fetch_index].reshape(
        HEADS, per_dev, PAIRS * CLUS, pair_width
    )
    pair_keys = pairs_kv[..., :HEAD_DIM]
    pair_values = pairs_kv[..., HEAD_DIM:]
    scores = (
        jnp.einsum("hcqd,hckd->hcqk", q_sorted, pair_keys, preferred_element_type=jnp.float32)
        * score_scale
    )
    row_top = jnp.max(scores, -1, keepdims=True)
    exponent = jnp.exp(scores - row_top)
    row_total = jnp.sum(exponent, -1, keepdims=True)
    attention = exponent / row_total
    log_total = row_top + jnp.log(row_total)
    mixture = jnp.einsum(
        "hcqk,hckd->hcqd",
        attention.astype(jnp.bfloat16),
        pair_values,
        preferred_element_type=jnp.float32,
    )
    attn = unsort_heads(mixture.astype(jnp.bfloat16).reshape(HEADS, rows_dev, HEAD_DIM))
    branch = jnp.dot(attn, w_out, preferred_element_type=jnp.float32) + b_out.astype(jnp.float32)
    resid = tokens.astype(jnp.float32) + branch
    normed, norm_one_back = jax.vjp(
        layer_norm, resid, gain_one.astype(jnp.float32), shift_one.astype(jnp.float32)
    )
    normed_low = normed.astype(jnp.bfloat16)
    inner_pre = jnp.dot(normed_low, w_up, preferred_element_type=jnp.float32) + b_up.astype(
        jnp.float32
    )
    active_full, gelu_back = jax.vjp(partial(jax.nn.gelu, approximate=False), inner_pre)
    active = active_full.astype(jnp.bfloat16)
    second = jnp.dot(active, w_down, preferred_element_type=jnp.float32) + b_down.astype(
        jnp.float32
    )
    result_full, norm_two_back = jax.vjp(
        layer_norm, normed + second, gain_two.astype(jnp.float32), shift_two.astype(jnp.float32)
    )
    layer_out = result_full.astype(jnp.bfloat16)
    grad_sum_two, grad_gain_two, grad_shift_two = norm_two_back(cotangent.astype(jnp.float32))
    grad_second = grad_sum_two.astype(jnp.bfloat16)
    grad_w_down = jnp.dot(active.T, grad_second, preferred_element_type=jnp.float32)
    grad_b_down = column_sums(grad_second)
    (grad_inner_full,) = gelu_back(
        jnp.dot(grad_second, w_down.T, preferred_element_type=jnp.float32)
    )
    grad_inner = grad_inner_full.astype(jnp.bfloat16)
    grad_w_up = jnp.dot(normed_low.T, grad_inner, preferred_element_type=jnp.float32)
    grad_b_up = column_sums(grad_inner)
    grad_normed = grad_sum_two + jnp.dot(grad_inner, w_up.T, preferred_element_type=jnp.float32)
    grad_resid, grad_gain_one, grad_shift_one = norm_one_back(grad_normed)
    grad_branch = grad_resid.astype(jnp.bfloat16)
    grad_w_out = jnp.dot(attn.T, grad_branch, preferred_element_type=jnp.float32)
    grad_b_out = column_sums(grad_branch)
    grad_attn = jnp.dot(grad_branch, w_out.T, preferred_element_type=jnp.float32).astype(
        jnp.bfloat16
    )
    grad_mixture = sort_heads(grad_attn).reshape(HEADS, per_dev, CLUS, HEAD_DIM)
    scores_again = (
        jnp.einsum("hcqd,hckd->hcqk", q_sorted, pair_keys, preferred_element_type=jnp.float32)
        * score_scale
    )
    attention_again = jnp.exp(scores_again - log_total)
    grad_probs = jnp.einsum(
        "hcqd,hckd->hcqk", grad_mixture, pair_values, preferred_element_type=jnp.float32
    )
    grad_values = jnp.einsum(
        "hcqk,hcqd->hckd",
        attention_again.astype(jnp.bfloat16),
        grad_mixture,
        preferred_element_type=jnp.float32,
    )
    grad_scores = (
        attention_again * (grad_probs - jnp.sum(grad_probs * attention_again, -1, keepdims=True))
    ).astype(jnp.bfloat16)
    grad_query = (
        jnp.einsum("hcqk,hckd->hcqd", grad_scores, pair_keys, preferred_element_type=jnp.float32)
        * score_scale
    ).astype(jnp.bfloat16)
    grad_keys = (
        jnp.einsum("hcqk,hcqd->hckd", grad_scores, q_sorted, preferred_element_type=jnp.float32)
        * score_scale
    )
    grad_pair = jnp.concatenate([grad_keys, grad_values], axis=3).reshape(
        requests, CLUS, pair_width
    )
    returned = (
        jnp.zeros((count_blk * capacity, CLUS, pair_width), jnp.float32)
        .at[fetch_index]
        .set(grad_pair)
    )
    returned_grads = lax.all_to_all(
        returned.reshape(count_blk, capacity, CLUS, pair_width).astype(jnp.bfloat16),
        "blk",
        split_axis=0,
        concat_axis=0,
        tiled=True,
    ).astype(jnp.float32)
    summed = jax.ops.segment_sum(
        returned_grads.reshape(count_blk * capacity, CLUS, pair_width),
        segment,
        num_segments=HEADS * per_dev + 1,
    )[: HEADS * per_dev]
    grad_kv_rows = unsort_heads(summed.reshape(HEADS, rows_dev, pair_width)).reshape(
        rows_dev, HEADS, pair_width
    )
    grad_k = grad_kv_rows[:, :, :HEAD_DIM].reshape(rows_dev, D).astype(jnp.bfloat16)
    grad_v = grad_kv_rows[:, :, HEAD_DIM:].reshape(rows_dev, D).astype(jnp.bfloat16)
    grad_q = unsort_heads(grad_query.reshape(HEADS, rows_dev, HEAD_DIM))
    grad_proj = jnp.concatenate([grad_q, grad_k, grad_v], axis=1)
    grad_w_qkv = jnp.dot(tokens.T, grad_proj, preferred_element_type=jnp.float32)
    grad_b_query = column_sums(grad_q)
    grad_b_value = column_sums(grad_v)
    grad_tokens = (
        grad_resid + jnp.dot(grad_proj, w_qkv.T, preferred_element_type=jnp.float32)
    ).astype(jnp.bfloat16)
    gradients = (
        grad_w_qkv,
        grad_b_query,
        grad_b_value,
        grad_w_out,
        grad_b_out,
        grad_gain_one,
        grad_shift_one,
        grad_w_up,
        grad_b_up,
        grad_w_down,
        grad_b_down,
        grad_gain_two,
        grad_shift_two,
    )
    flattened = flatten_all(gradients, lax.axis_size("dp") * count_blk)
    shares = lax.psum_scatter(flattened, ("dp", "blk"), scatter_dimension=0, tiled=True)
    totals_flat = lax.all_gather(
        shares.astype(jnp.bfloat16), ("dp", "blk"), axis=0, tiled=True
    ).astype(shares.dtype)
    totals = split_all(totals_flat, gradients)
    return (
        layer_out,
        grad_tokens,
        totals[0],
        totals[1],
        totals[2],
        totals[3],
        totals[4],
        totals[5],
        totals[6],
        totals[7],
        totals[8],
        totals[9],
        totals[10],
        totals[11],
        totals[12],
    )


def solution(mesh):
    return jax.shard_map(
        per_device,
        mesh=mesh,
        in_specs=(
            P(("dp", "blk"), None),
            P(),
            P(),
            P(),
            P(),
            P(),
            P(),
            P(),
            P(),
            P(),
            P(),
            P(),
            P(),
            P(),
            P("dp", None, "blk"),
            P("dp", None, None, None),
            P(("dp", "blk"), None),
        ),
        out_specs=(
            P(("dp", "blk"), None),
            P(("dp", "blk"), None),
            P(),
            P(),
            P(),
            P(),
            P(),
            P(),
            P(),
            P(),
            P(),
            P(),
            P(),
            P(),
            P(),
        ),
        check_vma=False,
    )
```

profile of v0, /device:TPU:0, one launch (start us, length us, event | category | flops | bytes accessed | tf_op | source)
XLA Modules:
  0.0 1955.3 jit_solution(2782621795003412746)
XLA Ops:
  44.4 105.0 %gather_fusion.2 = bf16[6144,128]{1,0:T(8,128)(2,1)} fusion(bf16[12,512,128]{2,1,0:T(8,128)(2,1)} %maximum_bitcast_fusion, s32[6144]{0:T(1024)} %bitcast.134), kind=kCustom, calls=%fused_computation.6 | custom fusion | bytes 3194880 | tf_op jit(solution)/shard_map/jit(take_along_axis)/gather | solution.py:74
  177.7 105.1 %gather_fusion.4 = bf16[6144,64]{1,0:T(8,128)(2,1)} fusion(bf16[12,512,64]{2,1,0:T(8,128)(2,1)} %bitcast.143, s32[6144]{0:T(1024)} %bitcast.135), kind=kCustom, calls=%fused_computation.clone | custom fusion | bytes 1622016 | tf_op jit(solution)/shard_map/jit(take_along_axis)/gather | solution.py:74
  319.2 105.0 %gather_fusion.5 = bf16[6144,64]{1,0:T(8,128)(2,1)} fusion(bf16[12,512,64]{2,1,0:T(8,128)(2,1)} %bitcast.144, s32[6144]{0:T(1024)} %reshape.561), kind=kCustom, calls=%fused_computation.1.clone | custom fusion | bytes 1622016 | tf_op jit(solution)/shard_map/jit(take_along_axis)/gather | solution.py:77
  431.0 20.0 %multiply_convert_fusion.1 = (bf16[512,3072]{1,0:T(8,128)(2,1)S(1)}, f32[512,3072]{1,0:T(8,128)}, f32[512,3072]{1,0:T(8,128)}) fusion(f32[3072]{0:T(1024)S(1)} %copy-done.32, bf16[768,3072]{1,0:T(8,128)(2,1)} %param.27, f32[512,768]{1,0:T(8,128)S(1)} %get-tuple-element.60, f32[768]{0:T(1024)S(1)} %copy-done.40, f32[768]{0:T(1024)S(1)} %copy-done.29, ...), kind=kOutput, calls=%fused_computation.18 | convolution fusion | flops 2521694208 | bytes 22042624 | tf_op jit(solution)/shard_map/dot_general | solution.py:143
  457.9 9.7 convert_reduce_fusion
  483.4 105.0 %gather_fusion.6 = bf16[6144,64]{1,0:T(8,128)(2,1)} fusion(bf16[12,512,64]{2,1,0:T(8,128)(2,1)} %bitcast.140, s32[6144]{0:T(1024)} %bitcast.136), kind=kCustom, calls=%fused_computation.2.clone | custom fusion | bytes 1622016 | tf_op jit(solution)/shard_map/jit(take_along_axis)/gather | solution.py:74
  591.8 7.5 multiply_reduce_fusion
  620.9 17.4 scatter_fusion
  662.0 105.0 %gather_fusion.7 = bf16[6144,64]{1,0:T(8,128)(2,1)} fusion(bf16[12,512,64]{2,1,0:T(8,128)(2,1)} %bitcast.141, s32[6144]{0:T(1024)} %reshape.561), kind=kCustom, calls=%fused_computation.3.clone | custom fusion | bytes 1622016 | tf_op jit(solution)/shard_map/jit(take_along_axis)/gather | solution.py:77
  796.3 10.8 reshape.475
  815.2 22.8 %scatter_fusion.1 = f32[49,128,128]{2,1,0:T(8,128)} fusion(f32[49,128,128]{2,1,0:T(8,128)} %broadcast_in_dim.118, s32[112]{0:T(128)S(1)} %copy-done.44, f32[112,128,128]{2,1,0:T(8,128)} %bitcast_convert_fusion), kind=kCustom, calls=%fused_computation.9 | custom fusion | flops 1835008 | bytes 22020544 | tf_op jit(solution)/shard_map/scatter-add | solution.py:214
  841.3 105.0 %gather_fusion.3 = bf16[6144,128]{1,0:T(8,128)(2,1)} fusion(bf16[12,512,128]{2,1,0:T(8,128)(2,1)} %bitcast.142, s32[6144]{0:T(1024)} %bitcast.137), kind=kCustom, calls=%fused_computation.7 | custom fusion | bytes 3194880 | tf_op jit(solution)/shard_map/jit(take_along_axis)/gather | solution.py:77
  957.4 8.0 copy.178
  965.4 7.9 reshape.472
  981.7 21.3 %dynamic-update-slice.4 = f32[7087104]{0:T(1024)} dynamic-update-slice(f32[7087104]{0:T(1024)} %constant_dynamic-update-slice_fusion.7, f32[589824]{0:T(1024)} %reshape.473, s32[]{} %constant.295) | dynamic-update-slice | bytes 4718596
  1006.8 80.6 %dynamic-update-slice.8 = f32[7087104]{0:T(1024)} dynamic-update-slice(f32[7087104]{0:T(1024)} %constant_dynamic-update-slice_fusion.4, f32[2359296]{0:T(1024)} %bitcast.149, s32[]{} %constant.299) | dynamic-update-slice | bytes 18874372
  1088.8 80.4 %dynamic-update-slice.10 = f32[7087104]{0:T(1024)} dynamic-update-slice(f32[7087104]{0:T(1024)} %constant_dynamic-update-slice_fusion.3, f32[2359296]{0:T(1024)} %reshape.475, s32[]{} %constant.301) | dynamic-update-slice | bytes 18874372
  1173.1 457.1 %all-reduce.6 = bf16[7087104]{0:T(1024)(128)(2,1)} all-reduce(f32[7087104]{0:T(1024)} %constant_dynamic-update-slice_fusion), channel_id=2, replica_groups=mesh['dp'=2,'blk'=16] {'dp','blk'}, use_global_device_ids=true, to_apply=%region_26.28.clone | all-reduce | flops 7087104 | bytes 42522624
  1637.5 7.7 dynamic-update-slice
  1650.9 243.2 %all-reduce.5.cloned.1.call-done = bf16[7087104]{0:T(1024)(128)(2,1)} async-done(((bf16[7087104]{0:T(1024)(128)(2,1)}), bf16[7087104]{0:T(1024)(128)(2,1)}) %all-reduce.5.cloned.1.call-update) | async-done | bytes 14174224
  1894.2 10.0 fusion.60
  1904.2 10.9 reshape.476
  1915.1 11.3 slice.115
  1930.9 8.2 slice.104
  (251 shorter events, 275.2 us)
Async XLA Ops:
  19.6 8.5 copy-start.30
  162.1 135.7 %all-to-all-start = ((bf16[16,7,128,128]{3,2,1,0:T(8,128)(2,1)}), bf16[16,7,128,128]{3,2,1,0:T(8,128)(2,1)}, u32[]{:S(2)}, u32[]{:S(2)}) async-start(bf16[16,7,128,128]{3,2,1,0:T(8,128)(2,1)} %broadcast_select_fusion), calls=%async_computation | async-start | bytes 7340032 | tf_op jit(solution)/shard_map/all_to_all | solution.py:115
  169.6 124.7 %sort.19.cloned.1.call-start = ((), (), s32[]{:S(2)}) async-start(), calls=%async_computation.3 | async-start | bytes 196640 | tf_op jit(solution)/shard_map/jit(argsort)/sort | solution.py:70
  177.7 112.1 %copy-start.37 = (bf16[3072]{0:T(1024)(128)(2,1)S(1)}, bf16[3072]{0:T(1024)(128)(2,1)}, u32[]{:S(2)}) copy-start(bf16[3072]{0:T(1024)(128)(2,1)} %param.28) | copy-start | bytes 18436
  427.8 23.2 %slice-start.2 = ((s8[4718592]{0:T(1024)(128)(4,1)}), s8[4194304]{0:T(1024)(128)(4,1)S(1)}, s32[]{:S(2)}) async-start(s8[4718592]{0:T(1024)(128)(4,1)} %bitcast.184), calls=%async_computation.7 | async-start | bytes 8388608
  430.6 42.8 %copy-start.6 = (f32[512,768]{1,0:T(8,128)}, f32[512,768]{1,0:T(8,128)S(1)}, u32[]{:S(2)}) copy-start(f32[512,768]{1,0:T(8,128)S(1)} %get-tuple-element.60) | copy-start | bytes 4718596
  430.6 42.8 %copy-start.22 = (f32[512]{0:T(512)}, f32[512]{0:T(512)S(1)}, u32[]{:S(2)}) copy-start(f32[512]{0:T(512)S(1)} %broadcast_multiply_fusion.1) | copy-start | bytes 6148
  431.0 42.4 %copy-start.34 = (f32[512]{0:T(512)}, f32[512]{0:T(512)S(1)}, u32[]{:S(2)}) copy-start(f32[512]{0:T(512)S(1)} %fusion.45) | copy-start | bytes 6148
  431.0 20.0 %copy-start.41 = (f32[768]{0:T(1024)S(1)}, f32[768]{0:T(1024)}, u32[]{:S(2)}) copy-start(f32[768]{0:T(1024)} %convert_element_type.137) | copy-start | bytes 9220
  431.0 20.0 %slice-start.3 = ((s8[4718592]{0:T(1024)(128)(4,1)}), s8[524288]{0:T(1024)(128)(4,1)S(1)}, s32[]{:S(2)}) async-start(s8[4718592]{0:T(1024)(128)(4,1)} %bitcast.184), calls=%async_computation.8 | async-start | bytes 1048576
  455.5 12.2 slice-start.4
  457.9 9.7 copy-start.14
  457.9 9.8 slice-start.5
  591.7 11.3 slice-start
  591.7 11.3 slice-start.1
  644.1 163.0 %all-to-all-start.1 = ((bf16[16,7,128,128]{3,2,1,0:T(8,128)(2,1)}), bf16[16,7,128,128]{3,2,1,0:T(8,128)(2,1)}, u32[]{:S(2)}, u32[]{:S(2)}) async-start(bf16[16,7,128,128]{3,2,1,0:T(8,128)(2,1)} %bitcast.152), calls=%async_computation.1 | async-start | bytes 7340032 | tf_op jit(solution)/shard_map/all_to_all | solution.py:207
  650.3 1243.9 %all-reduce.5.cloned.1.call-start = ((), (), s32[]{:S(2)}) async-start(), calls=%async_computation.2 | async-start | bytes 28348416
  978.4 24.5 %copy-start.27 = (f32[768]{0:T(1024)S(1)}, f32[768]{0:T(1024)}, u32[]{:S(2)}) copy-start(f32[768]{0:T(1024)} %get-tuple-element.28) | copy-start | bytes 9220
  979.1 25.2 %copy-start.43 = (f32[768]{0:T(1024)S(1)}, f32[768]{0:T(1024)}, u32[]{:S(2)}) copy-start(f32[768]{0:T(1024)} %get-tuple-element.18) | copy-start | bytes 9220
  979.1 26.5 %copy-start.42 = (f32[768]{0:T(1024)S(1)}, f32[768]{0:T(1024)}, u32[]{:S(2)}) copy-start(f32[768]{0:T(1024)} %get-tuple-element.22) | copy-start | bytes 9220
  1006.8 80.6 %copy-start.31 = (f32[3072]{0:T(1024)S(1)}, f32[3072]{0:T(1024)}, u32[]{:S(2)}) copy-start(f32[3072]{0:T(1024)} %get-tuple-element.26) | copy-start | bytes 36868
  1088.8 80.4 %copy-start.26 = (f32[768]{0:T(1024)S(1)}, f32[768]{0:T(1024)}, u32[]{:S(2)}) copy-start(f32[768]{0:T(1024)} %get-tuple-element.24) | copy-start | bytes 9220
  1088.8 81.7 %copy-start.25 = (f32[768]{0:T(1024)S(1)}, f32[768]{0:T(1024)}, u32[]{:S(2)}) copy-start(f32[768]{0:T(1024)} %get-tuple-element.20) | copy-start | bytes 9220
  1088.8 83.1 %copy-start.24 = (f32[768]{0:T(1024)S(1)}, f32[768]{0:T(1024)}, u32[]{:S(2)}) copy-start(f32[768]{0:T(1024)} %get-tuple-element.23) | copy-start | bytes 9220
  (35 other events, 105.0 us)
Sparse Core Ops, SparseCore 0:
  173.4 3.2 sort.21.cloned.1.call-done
  1645.3 248.7 all-reduce.4
  (1 shorter events, 0.0 us)
where the time goes:
time: 1980 us; the launch traced here: 1960 us
  local copies, waits for them, and re-layouts  1040 us (53%)
  blocking collectives  457 us (23%)
  waiting for transfers between devices  243 us (12%)
  matrix products  96.5 us (5%)
  other arithmetic  92.3 us (5%)
    unnamed x1, blocking collectives  457 us
    gather x7, local copies, waits for them, and re-layouts, unsort_heads(): placed = jnp.take_along_axis(tensor, inverse[:, :, None], axis=1)  324 us
    gather x5, local copies, waits for them, and re-layouts, sort_heads(): return jnp.take_along_axis(shaped, local_order[:, :, None], axis=1)  320 us
    unnamed x2, waiting for transfers between devices  243 us
    unnamed x130, local copies, waits for them, and re-layouts  231 us
    slice x8, local copies, waits for them, and re-layouts, split_all(): pieces_out.append(flattened[offset:offset + length].reshape(member.shape))  43 us
  transfers between devices with their start and end apart: 3, of which 1 were waited for; matrix products, arithmetic and copies ran while one was open for 15% of the time, Pallas kernels for 0%

commit v1 on v0

v1 whole, which is shorter than its diff:
```python
from functools import partial

import jax
import jax.numpy as jnp
from jax import lax
from jax.sharding import PartitionSpec as P

D = 768
HEADS = 12
HEAD_DIM = 64
CLUS = 128
PAIRS = 2


def layer_norm(values, scaling, offset):
    average = jnp.mean(values, -1, keepdims=True)
    centred = values - average
    variance = jnp.mean(centred * centred, -1, keepdims=True)
    return centred * lax.rsqrt(variance + 1e-06) * scaling + offset


def column_sums(matrix):
    return jnp.sum(matrix.astype(jnp.float32), axis=0)


def swap(value, axis, distance):
    size = lax.axis_size(axis)
    return lax.ppermute(value, axis, [(i, i ^ distance) for i in range(size)])


def bit_of(axis, distance):
    return (lax.axis_index(axis) & distance) != 0


def routes(count_blk):
    dp = ("dp", 1)
    chip = [("blk", 2), ("blk", 4), ("blk", 8)]
    rest = []
    distance = 16
    while distance < count_blk:
        rest.append(("blk", distance))
        distance *= 2
    first = [dp, chip[0], chip[1], chip[2]]
    second = [chip[0], dp, chip[1], chip[2]]
    return first, second, rest


def add_low(left, right):
    return (left.astype(jnp.float32) + right.astype(jnp.float32)).astype(jnp.bfloat16)


def scatter_sum(value, route, rest):
    for axis, distance in route:
        half = value.shape[0] // 2
        low, high = value[:half], value[half:]
        bit = bit_of(axis, distance)
        given = swap(jnp.where(bit, low, high), axis, distance)
        value = add_low(jnp.where(bit, high, low), given)
    for axis, distance in rest:
        value = add_low(value, swap(value, axis, distance))
    return value


def gather_rows(value, route):
    for axis, distance in reversed(route):
        given = swap(value, axis, distance)
        bit = bit_of(axis, distance)
        value = jnp.where(
            bit, jnp.concatenate([given, value]), jnp.concatenate([value, given])
        )
    return value


def sum_everywhere(halves, count_blk):
    first, second, rest = routes(count_blk)
    core = lax.axis_index("blk") & 1
    mine = lax.dynamic_index_in_dim(halves, core, 0, keepdims=False)
    other = lax.dynamic_index_in_dim(halves, 1 - core, 0, keepdims=False)
    mine = add_low(mine, swap(other, "blk", 1))
    totals = [
        gather_rows(scatter_sum(mine[at], route, rest), route)
        for at, route in enumerate((first, second))
    ]
    own = jnp.stack(totals)
    given = swap(own, "blk", 1)
    return jnp.where(core == 1, jnp.stack([given, own]), jnp.stack([own, given]))


def per_device(
    tokens,
    w_qkv,
    b_query,
    b_value,
    w_out,
    b_out,
    gain_one,
    shift_one,
    w_up,
    b_up,
    w_down,
    b_down,
    gain_two,
    shift_two,
    cluster_perm,
    cluster_pairs,
    cotangent,
):
    count_blk = lax.axis_size("blk")
    my_index = lax.axis_index("blk")
    rows_dev = tokens.shape[0]
    per_dev = rows_dev // CLUS
    requests = per_dev * HEADS * PAIRS
    capacity = max(2, (requests + count_blk - 1) // count_blk + 1)
    score_scale = HEAD_DIM ** (-0.5)
    pair_width = 2 * HEAD_DIM
    local_order = cluster_perm[0] - my_index * rows_dev
    places = jnp.arange(rows_dev, dtype=jnp.int32)
    onehot = (local_order[:, :, None] == places[None, None, :]).astype(jnp.bfloat16)

    def sort_heads(tensor):
        shaped = tensor.reshape(rows_dev, HEADS, -1)
        return jnp.einsum(
            "hji,ihd->hjd", onehot, shaped, preferred_element_type=jnp.float32
        ).astype(jnp.bfloat16)

    def unsort_heads(tensor):
        return (
            jnp.einsum("hji,hjd->ihd", onehot, tensor, preferred_element_type=jnp.float32)
            .astype(jnp.bfloat16)
            .reshape(rows_dev, -1)
        )

    projected = jnp.dot(tokens, w_qkv, preferred_element_type=jnp.float32)
    queries = (projected[:, :D] + b_query.astype(jnp.float32)).astype(jnp.bfloat16)
    keys_all = projected[:, D : 2 * D].astype(jnp.bfloat16)
    values = (projected[:, 2 * D :] + b_value.astype(jnp.float32)).astype(jnp.bfloat16)
    q_sorted = sort_heads(queries).reshape(HEADS, per_dev, CLUS, HEAD_DIM)
    joined = jnp.concatenate(
        [keys_all.reshape(rows_dev, HEADS, HEAD_DIM), values.reshape(rows_dev, HEADS, HEAD_DIM)],
        axis=2,
    )
    kv_blocks = sort_heads(joined.reshape(rows_dev, HEADS * pair_width)).reshape(
        HEADS * per_dev, CLUS, pair_width
    )
    wanted = (
        cluster_pairs[0]
        .reshape(HEADS, count_blk, per_dev, PAIRS)
        .transpose(1, 0, 2, 3)
        .reshape(count_blk, requests)
    )
    positions = jnp.arange(requests, dtype=jnp.int32)
    before = positions[:, None] < positions[None, :]
    source = wanted // per_dev
    named = source == my_index
    rank = jnp.sum(named[:, :, None] & before[None], axis=1)
    head_of = positions // (per_dev * PAIRS)
    block_id = head_of[None, :] * per_dev + wanted % per_dev
    matches = named[:, :, None] & (
        rank[:, :, None] == jnp.arange(capacity, dtype=jnp.int32)[None, None, :]
    )
    filled = jnp.any(matches, axis=1)
    chosen = jnp.sum(jnp.where(matches, block_id[:, :, None], 0), axis=1)
    my_source = lax.dynamic_index_in_dim(wanted, my_index, 0, keepdims=False) // per_dev
    my_rank = jnp.sum((my_source[:, None] == my_source[None, :]) & before, axis=0)
    fetch_index = my_source * capacity + my_rank
    segment = jnp.where(filled, chosen, HEADS * per_dev).reshape(-1)
    outgoing = kv_blocks[chosen]
    arrived = lax.all_to_all(outgoing, "blk", split_axis=0, concat_axis=0, tiled=True)
    pairs_kv = arrived.reshape(count_blk * capacity, CLUS, pair_width)[fetch_index].reshape(
        HEADS, per_dev, PAIRS * CLUS, pair_width
    )
    pair_keys = pairs_kv[..., :HEAD_DIM]
    pair_values = pairs_kv[..., HEAD_DIM:]
    scores = (
        jnp.einsum("hcqd,hckd->hcqk", q_sorted, pair_keys, preferred_element_type=jnp.float32)
        * score_scale
    )
    row_top = jnp.max(scores, -1, keepdims=True)
    exponent = jnp.exp(scores - row_top)
    row_total = jnp.sum(exponent, -1, keepdims=True)
    attention = exponent / row_total
    attention_low = attention.astype(jnp.bfloat16)
    mixture = jnp.einsum(
        "hcqk,hckd->hcqd",
        attention_low,
        pair_values,
        preferred_element_type=jnp.float32,
    )
    attn = unsort_heads(mixture.astype(jnp.bfloat16).reshape(HEADS, rows_dev, HEAD_DIM))
    branch = jnp.dot(attn, w_out, preferred_element_type=jnp.float32) + b_out.astype(jnp.float32)
    resid = tokens.astype(jnp.float32) + branch
    normed, norm_one_back = jax.vjp(
        layer_norm, resid, gain_one.astype(jnp.float32), shift_one.astype(jnp.float32)
    )
    normed_low = normed.astype(jnp.bfloat16)
    inner_pre = jnp.dot(normed_low, w_up, preferred_element_type=jnp.float32) + b_up.astype(
        jnp.float32
    )
    active_full, gelu_back = jax.vjp(partial(jax.nn.gelu, approximate=False), inner_pre)
    active = active_full.astype(jnp.bfloat16)
    second = jnp.dot(active, w_down, preferred_element_type=jnp.float32) + b_down.astype(
        jnp.float32
    )
    result_full, norm_two_back = jax.vjp(
        layer_norm, normed + second, gain_two.astype(jnp.float32), shift_two.astype(jnp.float32)
    )
    layer_out = result_full.astype(jnp.bfloat16)
    grad_sum_two, grad_gain_two, grad_shift_two = norm_two_back(cotangent.astype(jnp.float32))
    grad_second = grad_sum_two.astype(jnp.bfloat16)
    grad_b_down = column_sums(grad_second)
    (grad_inner_full,) = gelu_back(
        jnp.dot(grad_second, w_down.T, preferred_element_type=jnp.float32)
    )
    grad_inner = grad_inner_full.astype(jnp.bfloat16)
    grad_b_up = column_sums(grad_inner)
    grad_normed = grad_sum_two + jnp.dot(grad_inner, w_up.T, preferred_element_type=jnp.float32)
    grad_resid, grad_gain_one, grad_shift_one = norm_one_back(grad_normed)
    grad_branch = grad_resid.astype(jnp.bfloat16)
    grad_b_out = column_sums(grad_branch)
    grad_attn = jnp.dot(grad_branch, w_out.T, preferred_element_type=jnp.float32).astype(
        jnp.bfloat16
    )
    grad_mixture = sort_heads(grad_attn).reshape(HEADS, per_dev, CLUS, HEAD_DIM)
    grad_probs = jnp.einsum(
        "hcqd,hckd->hcqk", grad_mixture, pair_values, preferred_element_type=jnp.float32
    )
    grad_values = jnp.einsum(
        "hcqk,hcqd->hckd",
        attention_low,
        grad_mixture,
        preferred_element_type=jnp.float32,
    )
    grad_scores = (
        attention * (grad_probs - jnp.sum(grad_probs * attention, -1, keepdims=True))
    ).astype(jnp.bfloat16)
    grad_query = (
        jnp.einsum("hcqk,hckd->hcqd", grad_scores, pair_keys, preferred_element_type=jnp.float32)
        * score_scale
    ).astype(jnp.bfloat16)
    grad_keys = (
        jnp.einsum("hcqk,hcqd->hckd", grad_scores, q_sorted, preferred_element_type=jnp.float32)
        * score_scale
    )
    grad_pair = jnp.concatenate([grad_keys, grad_values], axis=3).reshape(
        requests, CLUS, pair_width
    ).astype(jnp.bfloat16)
    returned = (
        jnp.zeros((count_blk * capacity, CLUS, pair_width), jnp.bfloat16)
        .at[fetch_index]
        .set(grad_pair)
    )
    returned_grads = lax.all_to_all(
        returned.reshape(count_blk, capacity, CLUS, pair_width),
        "blk",
        split_axis=0,
        concat_axis=0,
        tiled=True,
    ).astype(jnp.float32)
    grad_w_down = jnp.dot(active.T, grad_second, preferred_element_type=jnp.float32)
    grad_w_up = jnp.dot(normed_low.T, grad_inner, preferred_element_type=jnp.float32)
    grad_w_out = jnp.dot(attn.T, grad_branch, preferred_element_type=jnp.float32)
    grad_q = unsort_heads(grad_query.reshape(HEADS, rows_dev, HEAD_DIM))
    grad_w_q = jnp.dot(tokens.T, grad_q, preferred_element_type=jnp.float32)

    sum_down = sum_everywhere(
        grad_w_down.astype(jnp.bfloat16).reshape(2, 2, D, D), count_blk
    ).reshape(4 * D, D)
    sum_up = (
        sum_everywhere(
            jnp.stack(jnp.split(grad_w_up.astype(jnp.bfloat16), 4, axis=1)).reshape(2, 2, D, D),
            count_blk,
        )
        .reshape(4, D, D)
        .transpose(1, 0, 2)
        .reshape(D, 4 * D)
    )

    def two_matrices(first, second):
        both = jnp.stack([first, second]).astype(jnp.bfloat16)
        halves = both.reshape(2, D, 2, D // 2).transpose(2, 0, 1, 3)
        total = sum_everywhere(halves, count_blk)
        return total.transpose(1, 2, 0, 3).reshape(2, D, D)

    sum_q, sum_out = two_matrices(grad_w_q, grad_w_out)

    summed = jax.ops.segment_sum(
        returned_grads.reshape(count_blk * capacity, CLUS, pair_width),
        segment,
        num_segments=HEADS * per_dev + 1,
    )[: HEADS * per_dev].astype(jnp.bfloat16)
    grad_kv_rows = unsort_heads(summed.reshape(HEADS, rows_dev, pair_width)).reshape(
        rows_dev, HEADS, pair_width
    )
    grad_k = grad_kv_rows[:, :, :HEAD_DIM].reshape(rows_dev, D)
    grad_v = grad_kv_rows[:, :, HEAD_DIM:].reshape(rows_dev, D)
    grad_w_k = jnp.dot(tokens.T, grad_k, preferred_element_type=jnp.float32)
    grad_w_v = jnp.dot(tokens.T, grad_v, preferred_element_type=jnp.float32)
    sum_k, sum_v = two_matrices(grad_w_k, grad_w_v)
    grad_b_query = column_sums(grad_q)
    grad_b_value = jnp.sum(grad_values, axis=(1, 2)).reshape(D)
    vectors = (
        grad_b_query,
        grad_b_value,
        grad_b_out,
        grad_gain_one,
        grad_shift_one,
        grad_b_up,
        grad_b_down,
        grad_gain_two,
        grad_shift_two,
    )
    totals = lax.psum(jnp.concatenate(vectors), ("dp", "blk"))
    pieces = []
    offset = 0
    for vector in vectors:
        pieces.append(totals[offset : offset + vector.shape[0]])
        offset += vector.shape[0]
    sum_qkv = jnp.concatenate([sum_q, sum_k, sum_v], axis=1)
    grad_proj = jnp.concatenate([grad_q, grad_k, grad_v], axis=1)
    grad_tokens = (
        grad_resid + jnp.dot(grad_proj, w_qkv.T, preferred_element_type=jnp.float32)
    ).astype(jnp.bfloat16)
    return (
        layer_out,
        grad_tokens,
        sum_qkv.astype(jnp.float32),
        pieces[0],
        pieces[1],
        sum_out.astype(jnp.float32),
        pieces[2],
        pieces[3],
        pieces[4],
        sum_up.astype(jnp.float32),
        pieces[5],
        sum_down.astype(jnp.float32),
        pieces[6],
        pieces[7],
        pieces[8],
    )


def solution(mesh):
    whole = P()
    rows = P(("dp", "blk"), None)
    return jax.shard_map(
        per_device,
        mesh=mesh,
        in_specs=(
            (rows,)
            + (whole,) * 13
            + (P("dp", None, "blk"), P("dp", None, None, None), rows)
        ),
        out_specs=(rows, rows) + (whole,) * 13,
        check_vma=False,
    )
```

time: 1980 us -> 729 us (0.37)
  local copies, waits for them, and re-layouts: 1040 us -> 148 us
  blocking collectives: 457 us -> 39.1 us
  starting transfers between devices: 13.6 us -> 90.1 us
  waiting for transfers between devices: 243 us -> 178 us
  matrix products: 96.5 us -> 142 us
  other arithmetic: 92.3 us -> 121 us
    gather x12 -> x0, local copies, waits for them, and re-layouts: 644 us -> none  [the longest x7 324 us: unsort_heads(): placed = jnp.take_along_axis(tensor, inverse[:, :, None], axis=1)]
    unnamed x1 -> x0, blocking collectives: 457 us -> none
    unnamed x2 -> x0, waiting for transfers between devices: 243 us -> none
    unnamed x130 -> x155, local copies, waits for them, and re-layouts: 231 us -> 43.3 us
    ppermute x0 -> x72, waiting for transfers between devices: none -> 129 us  [swap(): return lax.ppermute(value, axis, [(i, i ^ distance) for i in range(size)])]
    ppermute x0 -> x72, starting transfers between devices: none -> 64.8 us  [swap(): return lax.ppermute(value, axis, [(i, i ^ distance) for i in range(size)])]
    dot_general x3 -> x11, matrix products: 14.8 us -> 71 us  [the longest x1 19.7 us: per_device(): jnp.einsum('hcqk,hckd->hcqd', attention_low, pair_values, preferred_eleme...]
    all_to_all x1, waiting for transfers between devices: 0.01 us -> 49.5 us  [per_device(): lax.all_to_all(outgoing, 'blk', split_axis=0, concat_axis=0, tiled=True)]
  transfers between devices with their start and end apart: 3 -> 74, of which waited for: 1 -> 45; matrix products, arithmetic and copies ran while one was open for 15% -> 27% of each run, Pallas kernels for 0% -> 0%
where the time goes in v1:
time: 729 us; the launch traced here: 721 us
  waiting for transfers between devices  178 us (24%)
  local copies, waits for them, and re-layouts  148 us (20%)
  matrix products  142 us (19%)
  other arithmetic  121 us (17%)
  starting transfers between devices  90.1 us (12%)
  blocking collectives  39.1 us (5%)
    ppermute x72, waiting for transfers between devices, swap(): return lax.ppermute(value, axis, [(i, i ^ distance) for i in range(size)])  129 us
    ppermute x72, starting transfers between devices, swap(): return lax.ppermute(value, axis, [(i, i ^ distance) for i in range(size)])  64.8 us
    all_to_all x1, waiting for transfers between devices, per_device(): lax.all_to_all(outgoing, 'blk', split_axis=0, concat_axis=0, tiled=True)  49.5 us
    unnamed x155, local copies, waits for them, and re-layouts  43.3 us
    psum x1, blocking collectives, per_device(): totals = lax.psum(jnp.concatenate(vectors), ('dp', 'blk'))  39.1 us
    scatter-add x1, other arithmetic, per_device(): jax.ops.segment_sum(returned_grads.reshape(count_blk * capacity, CLUS, pa...  22.8 us
    dot_general x1, matrix products, per_device(): jnp.dot(normed_low, w_up, preferred_element_type=jnp.float32)  20.2 us
    dot_general x1, matrix products, per_device(): jnp.einsum('hcqk,hckd->hcqd', attention_low, pair_values, preferred_eleme...  19.7 us
  transfers between devices with their start and end apart: 74, of which 45 were waited for; matrix products, arithmetic and copies ran while one was open for 27% of the time, Pallas kernels for 0%

profile of v1, /device:TPU:0, one launch (start us, length us, event | category | flops | bytes accessed | tf_op | source)
XLA Modules:
  0.0 720.7 jit_solution(17603939748317308919)
XLA Ops:
  29.7 5.4 fusion.45
  39.5 7.7 %all-to-all-start = ((bf16[16,7,128,128]{3,2,1,0:T(8,128)(2,1)}), bf16[16,7,128,128]{3,2,1,0:T(8,128)(2,1)}, u32[]{:S(2)}, u32[]{:S(2)}) async-start(bf16[16,7,128,128]{3,2,1,0:T(8,128)(2,1)} %bitcast.256), calls=%async_computation | async-start | bytes 7340032 | tf_op jit(solution)/shard_map/all_to_all | solution.py:168
  66.2 49.5 %all-to-all-done = bf16[16,7,128,128]{3,2,1,0:T(8,128)(2,1)} async-done(((bf16[16,7,128,128]{3,2,1,0:T(8,128)(2,1)}), bf16[16,7,128,128]{3,2,1,0:T(8,128)(2,1)}, u32[]{:S(2)}, u32[]{:S(2)}) %all-to-all-start) | async-done | bytes 3670048 | tf_op jit(solution)/shard_map/all_to_all | solution.py:168
  128.8 19.7 %fusion.72 = bf16[12,4,8,8,128]{4,3,2,1,0:T(8,128)(2,1)} fusion(bf16[12,4,256,128]{3,2,1,0:T(8,128)(2,1)} %bitcast.249, f32[12,4,128]{2,1,0:T(4,128)} %get-tuple-element.142, f32[12,4,128,256]{3,2,1,0:T(8,128)} %copy-done.2), kind=kOutput, calls=%fused_computation.143 | convolution fusion | flops 209590528 | bytes 16539648 | tf_op jit(solution)/shard_map/hcqk,hckd->hcqd/dot_general | solution.py:183
  154.1 20.2 %multiply_convert_fusion.1 = (bf16[512,3072]{1,0:T(8,128)(2,1)S(1)}, f32[512,3072]{1,0:T(8,128)}, f32[512,3072]{1,0:T(8,128)}) fusion(f32[3072]{0:T(1024)S(1)} %copy-done.37, bf16[768,3072]{1,0:T(8,128)(2,1)} %param.25, f32[512,768]{1,0:T(8,128)S(1)} %get-tuple-element.145, f32[768]{0:T(1024)S(1)} %copy-done.42, f32[768]{0:T(1024)S(1)} %copy-done.33, ...), kind=kOutput, calls=%fused_computation.18 | convolution fusion | flops 2521694208 | bytes 22042624 | tf_op jit(solution)/shard_map/dot_general | solution.py:196
  180.5 9.9 %convert_reduce_fusion = (f32[3072]{0:T(1024)}, bf16[512,3072]{1,0:T(8,128)(2,1)}) fusion(f32[512,3072]{1,0:T(8,128)} %get-tuple-element.94, f32[512,3072]{1,0:T(8,128)} %get-tuple-element.146, f32[3072]{0:T(1024)S(1)} %copy-done.37, bf16[512,768]{1,0:T(8,128)(2,1)S(1)} %get-tuple-element.84, bf16[3072,768]{1,0:T(8,128)(2,1)S(1)} %bitcast.305), kind=kOutput, calls=%fused_computation.14 | convolution fusion | flops 2442654720 | bytes 21258240 | tf_op jit(solution)/shard_map/dot_general | solution.py:212
  190.4 5.6 multiply_reduce_fusion.2
  207.8 17.5 %fusion.145 = (f32[12,64]{1,0:T(8,128)}, bf16[12,4,256,64]{2,3,1,0:T(8,128)(2,1)}) fusion(f32[12,4,128]{2,1,0:T(4,128)} %get-tuple-element.142, f32[12,4,128,256]{3,2,1,0:T(8,128)} %copy-done.2, bf16[12,8,4,8,128]{4,3,2,1,0:T(8,128)(2,1)} %fusion.80), kind=kOutput, calls=%fused_computation.357 | convolution fusion | flops 210769408 | bytes 8678400 | tf_op jit(solution)/shard_map/hcqk,hcqd->hckd/dot_general | solution.py:227
  225.3 7.4 %multiply_reduce_fusion = (f32[12,4,128]{2,1,0:T(4,128)S(1)}, f32[12,4,128,256]{3,2,1,0:T(8,128)S(1)}) fusion(f32[12,4,128,256]{3,2,1,0:T(8,128)} %get-tuple-element.143, f32[12,4,128]{2,1,0:T(4,128)} %get-tuple-element.142, bf16[12,4,256,128]{3,2,1,0:T(8,128)(2,1)} %bitcast.250, bf16[12,8,4,8,128]{4,3,2,1,0:T(8,128)(2,1)} %fusion.80), kind=kOutput, calls=%fused_computation.16 | convolution fusion | flops 206039040 | bytes 16564224 | tf_op jit(solution)/shard_map/hcqd,hckd->hcqk/dot_general | solution.py:224
  253.6 14.6 %scatter_fusion = bf16[112,128,128]{2,1,0:T(8,128)(2,1)} fusion(bf16[112,128,128]{2,1,0:T(8,128)(2,1)} %broadcast_in_dim.33, s32[96]{0:T(128)S(1)} %copy-done.50, bf16[96,128,128]{2,1,0:T(8,128)(2,1)} %bitcast.257), kind=kCustom, calls=%fused_computation.2 | custom fusion | bytes 9437568 | tf_op jit(solution)/shard_map/scatter | solution.py:250
  268.2 17.6 %all-to-all-start.1 = ((bf16[16,7,128,128]{3,2,1,0:T(8,128)(2,1)}), bf16[16,7,128,128]{3,2,1,0:T(8,128)(2,1)}, u32[]{:S(2)}, u32[]{:S(2)}) async-start(bf16[16,7,128,128]{3,2,1,0:T(8,128)(2,1)} %bitcast.247), calls=%async_computation.1 | async-start | bytes 7340032 | tf_op jit(solution)/shard_map/all_to_all | solution.py:252
  334.8 5.7 collective-permute-done.9
  348.0 9.9 %collective-permute-done.2 = bf16[192,384]{1,0:T(8,128)(2,1)S(1)} collective-permute-done((bf16[192,384]{1,0:T(8,128)(2,1)S(1)}, bf16[192,384]{1,0:T(8,128)(2,1)S(1)}, u32[]{:S(2)}, u32[]{:S(2)}) %collective-permute-start.2) | collective-permute-done | bytes 147488 | tf_op jit(solution)/shard_map/ppermute | solution.py:28
  362.7 8.7 %collective-permute-done.12 = bf16[48,384]{1,0:T(8,128)(2,1)S(1)} collective-permute-done((bf16[48,384]{1,0:T(8,128)(2,1)S(1)}, bf16[48,384]{1,0:T(8,128)(2,1)S(1)}, u32[]{:S(2)}, u32[]{:S(2)}) %collective-permute-start.12) | collective-permute-done | bytes 36896 | tf_op jit(solution)/shard_map/ppermute | solution.py:28
  386.5 39.1 %psum.7 = f32[9216]{0:T(1024)} all-reduce(f32[9216]{0:T(1024)} %constant_dynamic-update-slice_fusion), channel_id=1, replica_groups=mesh['dp'=2,'blk'=16] {'dp','blk'}, use_global_device_ids=true, to_apply=%region_26.27 | all-reduce | flops 9216 | bytes 73728 | tf_op jit(solution)/shard_map/psum | solution.py:312
  449.6 9.7 %collective-permute-done.37 = bf16[384,768]{1,0:T(8,128)(2,1)S(1)} collective-permute-done((bf16[384,768]{1,0:T(8,128)(2,1)S(1)}, bf16[384,768]{1,0:T(8,128)(2,1)S(1)}, u32[]{:S(2)}, u32[]{:S(2)}) %collective-permute-start.37) | collective-permute-done | bytes 589856 | tf_op jit(solution)/shard_map/ppermute | solution.py:28
  462.3 9.6 %collective-permute-done.55 = bf16[384,768]{1,0:T(8,128)(2,1)S(1)} collective-permute-done((bf16[384,768]{1,0:T(8,128)(2,1)S(1)}, bf16[384,768]{1,0:T(8,128)(2,1)S(1)}, u32[]{:S(2)}, u32[]{:S(2)}) %collective-permute-start.55) | collective-permute-done | bytes 589856 | tf_op jit(solution)/shard_map/ppermute | solution.py:28
  489.7 5.0 collective-permute-done.65
  535.4 6.0 bitcast_convert_fusion.2
  543.5 22.8 %scatter_fusion.1 = f32[49,128,128]{2,1,0:T(8,128)} fusion(f32[49,128,128]{2,1,0:T(8,128)} %broadcast_in_dim.32, s32[112]{0:T(128)S(1)} %copy-done.48, f32[112,128,128]{2,1,0:T(8,128)} %bitcast_convert_fusion.2), kind=kCustom, calls=%fused_computation.3 | custom fusion | flops 1835008 | bytes 22020544 | tf_op jit(solution)/shard_map/scatter-add | solution.py:286
  604.9 9.1 %collective-permute-done.62 = bf16[384,768]{1,0:T(8,128)(2,1)S(1)} collective-permute-done((bf16[384,768]{1,0:T(8,128)(2,1)S(1)}, bf16[384,768]{1,0:T(8,128)(2,1)S(1)}, u32[]{:S(2)}, u32[]{:S(2)}) %collective-permute-start.62) | collective-permute-done | bytes 589856 | tf_op jit(solution)/shard_map/ppermute | solution.py:28
  671.3 13.4 %copy.180 = f32[4,768,768]{2,0,1:T(4,128)} copy(f32[4,768,768]{2,1,0:T(8,128)} %bitcast_convert_fusion.1) | data formatting | bytes 18874368 | tf_op jit(solution)/shard_map/convert_element_type | solution.py:333
  684.7 9.8 %copy.192 = f32[96,8,4,768]{3,1,2,0:T(8,128)} copy(f32[96,8,4,768]{3,2,1,0:T(4,128)} %bitcast.246) | data formatting | bytes 18874368
  712.5 8.0 %copy.181 = f32[768,2304]{1,0:T(8,128)} copy(f32[768,2304]{0,1:T(8,128)} %maximum_convert_fusion) | data formatting | bytes 14155776
  (502 shorter events, 386.4 us)
Async XLA Ops:
  39.5 76.3 %all-to-all-start = ((bf16[16,7,128,128]{3,2,1,0:T(8,128)(2,1)}), bf16[16,7,128,128]{3,2,1,0:T(8,128)(2,1)}, u32[]{:S(2)}, u32[]{:S(2)}) async-start(bf16[16,7,128,128]{3,2,1,0:T(8,128)(2,1)} %bitcast.256), calls=%async_computation | async-start | bytes 7340032 | tf_op jit(solution)/shard_map/all_to_all | solution.py:168
  268.2 267.2 %all-to-all-start.1 = ((bf16[16,7,128,128]{3,2,1,0:T(8,128)(2,1)}), bf16[16,7,128,128]{3,2,1,0:T(8,128)(2,1)}, u32[]{:S(2)}, u32[]{:S(2)}) async-start(bf16[16,7,128,128]{3,2,1,0:T(8,128)(2,1)} %bitcast.247), calls=%async_computation.1 | async-start | bytes 7340032 | tf_op jit(solution)/shard_map/all_to_all | solution.py:252
  300.6 23.2 %collective-permute-start = (bf16[2,768,384]{2,1,0:T(8,128)(2,1)}, bf16[2,768,384]{2,1,0:T(8,128)(2,1)}, u32[]{:S(2)}, u32[]{:S(2)}) collective-permute-start(bf16[2,768,384]{2,1,0:T(8,128)(2,1)} %fusion.88), channel_id=1, source_target_pairs={{0,1},{1,0},{2,3},{3,2},{4,5},{5,4},{6,7},{7,6},{8,9},{9,8},{10,11... | collective-permute-start | bytes 3538952 | tf_op jit(solution)/shard_map/ppermute | solution.py:28
  309.9 129.9 %collective-permute-start.36 = (bf16[2,768,768]{2,1,0:T(8,128)(2,1)}, bf16[2,768,768]{2,1,0:T(8,128)(2,1)}, u32[]{:S(2)}, u32[]{:S(2)}) collective-permute-start(bf16[2,768,768]{2,1,0:T(8,128)(2,1)} %dynamic-slice_bitcast_fusion.1), channel_id=1, source_target_pairs={{0,1},{1,0},{2,3},{3,2},{4,5},{5,4},{6,7},{7,6},{8,9},{9,8},{10,11... | collective-permute-start | bytes 7077896 | tf_op jit(solution)/shard_map/ppermute | solution.py:28
  317.1 128.0 %collective-permute-start.54 = (bf16[2,768,768]{2,1,0:T(8,128)(2,1)}, bf16[2,768,768]{2,1,0:T(8,128)(2,1)}, u32[]{:S(2)}, u32[]{:S(2)}) collective-permute-start(bf16[2,768,768]{2,1,0:T(8,128)(2,1)} %dynamic-slice_bitcast_fusion), channel_id=1, source_target_pairs={{0,1},{1,0},{2,3},{3,2},{4,5},{5,4},{6,7},{7,6},{8,9},{9,8},{10,11... | collective-permute-start | bytes 7077896 | tf_op jit(solution)/shard_map/ppermute | solution.py:28
  342.4 15.6 %collective-permute-start.2 = (bf16[192,384]{1,0:T(8,128)(2,1)S(1)}, bf16[192,384]{1,0:T(8,128)(2,1)S(1)}, u32[]{:S(2)}, u32[]{:S(2)}) collective-permute-start(bf16[192,384]{1,0:T(8,128)(2,1)S(1)} %broadcast_select_fusion.11), channel_id=1, source_target_pairs={{0,2},{1,3},{2,0},{3,1},{4,6},{5,7},{6,4},{7,5},{8,10},{9,11},{10,... | collective-permute-start | bytes 442376 | tf_op jit(solution)/shard_map/ppermute | solution.py:28
  381.5 45.4 %collective-permute-start.15 = (bf16[192,384]{1,0:T(8,128)(2,1)}, bf16[192,384]{1,0:T(8,128)(2,1)}, u32[]{:S(2)}, u32[]{:S(2)}) collective-permute-start(bf16[192,384]{1,0:T(8,128)(2,1)} %maximum_select_fusion.25), channel_id=1, source_target_pairs={{0,16},{16,0},{1,17},{17,1},{2,18},{18,2},{3,19},{19,3},{4,20},{20... | collective-permute-start | bytes 442376 | tf_op jit(solution)/shard_map/ppermute | solution.py:28
  383.7 46.7 %collective-permute-start.7 = (bf16[192,384]{1,0:T(8,128)(2,1)}, bf16[192,384]{1,0:T(8,128)(2,1)}, u32[]{:S(2)}, u32[]{:S(2)}) collective-permute-start(bf16[192,384]{1,0:T(8,128)(2,1)} %maximum_select_fusion.24), channel_id=1, source_target_pairs={{0,2},{1,3},{2,0},{3,1},{4,6},{5,7},{6,4},{7,5},{8,10},{9,11},{10,... | collective-permute-start | bytes 442376 | tf_op jit(solution)/shard_map/ppermute | solution.py:28
  439.8 58.2 %collective-permute-start.17 = (bf16[2,768,384]{2,1,0:T(8,128)(2,1)S(1)}, bf16[2,768,384]{2,1,0:T(8,128)(2,1)S(1)}, u32[]{:S(2)}, u32[]{:S(2)}) collective-permute-start(bf16[2,768,384]{2,1,0:T(8,128)(2,1)S(1)} %get-tuple-element.122), channel_id=1, source_target_pairs={{0,1},{1,0},{2,3},{3,2},{4,5},{5,4},{6,7},{7,6},{8,9},{9,8},{10,11... | collective-permute-start | bytes 3538952 | tf_op jit(solution)/shard_map/ppermute | solution.py:28
  443.1 16.2 %collective-permute-start.37 = (bf16[384,768]{1,0:T(8,128)(2,1)S(1)}, bf16[384,768]{1,0:T(8,128)(2,1)S(1)}, u32[]{:S(2)}, u32[]{:S(2)}) collective-permute-start(bf16[384,768]{1,0:T(8,128)(2,1)S(1)} %get-tuple-element.113), channel_id=1, source_target_pairs={{0,16},{16,0},{1,17},{17,1},{2,18},{18,2},{3,19},{19,3},{4,20},{20... | collective-permute-start | bytes 1769480 | tf_op jit(solution)/shard_map/ppermute | solution.py:28
  443.7 16.2 %collective-permute-start.45 = (bf16[384,768]{1,0:T(8,128)(2,1)S(1)}, bf16[384,768]{1,0:T(8,128)(2,1)S(1)}, u32[]{:S(2)}, u32[]{:S(2)}) collective-permute-start(bf16[384,768]{1,0:T(8,128)(2,1)S(1)} %get-tuple-element.114), channel_id=1, source_target_pairs={{0,2},{1,3},{2,0},{3,1},{4,6},{5,7},{6,4},{7,5},{8,10},{9,11},{10,... | collective-permute-start | bytes 1769480 | tf_op jit(solution)/shard_map/ppermute | solution.py:28
  447.5 24.4 %collective-permute-start.55 = (bf16[384,768]{1,0:T(8,128)(2,1)S(1)}, bf16[384,768]{1,0:T(8,128)(2,1)S(1)}, u32[]{:S(2)}, u32[]{:S(2)}) collective-permute-start(bf16[384,768]{1,0:T(8,128)(2,1)S(1)} %get-tuple-element.107), channel_id=1, source_target_pairs={{0,16},{16,0},{1,17},{17,1},{2,18},{18,2},{3,19},{19,3},{4,20},{20... | collective-permute-start | bytes 1769480 | tf_op jit(solution)/shard_map/ppermute | solution.py:28
  447.9 24.7 %collective-permute-start.63 = (bf16[384,768]{1,0:T(8,128)(2,1)S(1)}, bf16[384,768]{1,0:T(8,128)(2,1)S(1)}, u32[]{:S(2)}, u32[]{:S(2)}) collective-permute-start(bf16[384,768]{1,0:T(8,128)(2,1)S(1)} %get-tuple-element.108), channel_id=1, source_target_pairs={{0,2},{1,3},{2,0},{3,1},{4,6},{5,7},{6,4},{7,5},{8,10},{9,11},{10,... | collective-permute-start | bytes 1769480 | tf_op jit(solution)/shard_map/ppermute | solution.py:28
  460.4 17.9 %collective-permute-start.46 = (bf16[192,768]{1,0:T(8,128)(2,1)S(1)}, bf16[192,768]{1,0:T(8,128)(2,1)S(1)}, u32[]{:S(2)}, u32[]{:S(2)}) collective-permute-start(bf16[192,768]{1,0:T(8,128)(2,1)S(1)} %broadcast_select_fusion.1), channel_id=1, source_target_pairs={{0,16},{16,0},{1,17},{17,1},{2,18},{18,2},{3,19},{19,3},{4,20},{20... | collective-permute-start | bytes 884744 | tf_op jit(solution)/shard_map/ppermute | solution.py:28
  461.9 17.6 %collective-permute-start.38 = (bf16[192,768]{1,0:T(8,128)(2,1)S(1)}, bf16[192,768]{1,0:T(8,128)(2,1)S(1)}, u32[]{:S(2)}, u32[]{:S(2)}) collective-permute-start(bf16[192,768]{1,0:T(8,128)(2,1)S(1)} %broadcast_select_fusion.3), channel_id=1, source_target_pairs={{0,2},{1,3},{2,0},{3,1},{4,6},{5,7},{6,4},{7,5},{8,10},{9,11},{10,... | collective-permute-start | bytes 884744 | tf_op jit(solution)/shard_map/ppermute | solution.py:28
  528.3 68.5 %collective-permute-start.61 = (bf16[192,768]{1,0:T(8,128)(2,1)}, bf16[192,768]{1,0:T(8,128)(2,1)}, u32[]{:S(2)}, u32[]{:S(2)}) collective-permute-start(bf16[192,768]{1,0:T(8,128)(2,1)} %maximum_select_fusion.22), channel_id=1, source_target_pairs={{0,2},{1,3},{2,0},{3,1},{4,6},{5,7},{6,4},{7,5},{8,10},{9,11},{10,... | collective-permute-start | bytes 884744 | tf_op jit(solution)/shard_map/ppermute | solution.py:28
  529.3 69.3 %collective-permute-start.52 = (bf16[384,768]{1,0:T(8,128)(2,1)}, bf16[384,768]{1,0:T(8,128)(2,1)}, u32[]{:S(2)}, u32[]{:S(2)}) collective-permute-start(bf16[384,768]{1,0:T(8,128)(2,1)} %maximum_select_fusion.13), channel_id=1, source_target_pairs={{0,2},{1,3},{2,0},{3,1},{4,6},{5,7},{6,4},{7,5},{8,10},{9,11},{10,... | collective-permute-start | bytes 1769480 | tf_op jit(solution)/shard_map/ppermute | solution.py:28
  532.4 68.2 %collective-permute-start.44 = (bf16[384,768]{1,0:T(8,128)(2,1)}, bf16[384,768]{1,0:T(8,128)(2,1)}, u32[]{:S(2)}, u32[]{:S(2)}) collective-permute-start(bf16[384,768]{1,0:T(8,128)(2,1)} %maximum_select_fusion.12), channel_id=1, source_target_pairs={{0,16},{16,0},{1,17},{17,1},{2,18},{18,2},{3,19},{19,3},{4,20},{20... | collective-permute-start | bytes 1769480 | tf_op jit(solution)/shard_map/ppermute | solution.py:28
  533.7 69.3 %collective-permute-start.70 = (bf16[384,768]{1,0:T(8,128)(2,1)}, bf16[384,768]{1,0:T(8,128)(2,1)}, u32[]{:S(2)}, u32[]{:S(2)}) collective-permute-start(bf16[384,768]{1,0:T(8,128)(2,1)} %maximum_select_fusion.15), channel_id=1, source_target_pairs={{0,2},{1,3},{2,0},{3,1},{4,6},{5,7},{6,4},{7,5},{8,10},{9,11},{10,... | collective-permute-start | bytes 1769480 | tf_op jit(solution)/shard_map/ppermute | solution.py:28
  586.3 28.7 %collective-permute-start.18 = (bf16[2,768,384]{2,1,0:T(8,128)(2,1)}, bf16[2,768,384]{2,1,0:T(8,128)(2,1)}, u32[]{:S(2)}, u32[]{:S(2)}) collective-permute-start(bf16[2,768,384]{2,1,0:T(8,128)(2,1)} %fusion.84), channel_id=1, source_target_pairs={{0,1},{1,0},{2,3},{3,2},{4,5},{5,4},{6,7},{7,6},{8,9},{9,8},{10,11... | collective-permute-start | bytes 3538952 | tf_op jit(solution)/shard_map/ppermute | solution.py:28
  598.3 15.8 %collective-permute-start.62 = (bf16[384,768]{1,0:T(8,128)(2,1)S(1)}, bf16[384,768]{1,0:T(8,128)(2,1)S(1)}, u32[]{:S(2)}, u32[]{:S(2)}) collective-permute-start(bf16[384,768]{1,0:T(8,128)(2,1)S(1)} %maximum_select_fusion.14), channel_id=1, source_target_pairs={{0,16},{16,0},{1,17},{17,1},{2,18},{18,2},{3,19},{19,3},{4,20},{20... | collective-permute-start | bytes 1769480 | tf_op jit(solution)/shard_map/ppermute | solution.py:28
  602.7 52.1 %collective-permute-start.53 = (bf16[2,768,768]{2,1,0:T(8,128)(2,1)S(1)}, bf16[2,768,768]{2,1,0:T(8,128)(2,1)S(1)}, u32[]{:S(2)}, u32[]{:S(2)}) collective-permute-start(bf16[2,768,768]{2,1,0:T(8,128)(2,1)S(1)} %get-tuple-element.109), channel_id=1, source_target_pairs={{0,1},{1,0},{2,3},{3,2},{4,5},{5,4},{6,7},{7,6},{8,9},{9,8},{10,11... | collective-permute-start | bytes 7077896 | tf_op jit(solution)/shard_map/ppermute | solution.py:28
  614.9 53.6 %collective-permute-start.71 = (bf16[2,768,768]{2,1,0:T(8,128)(2,1)S(1)}, bf16[2,768,768]{2,1,0:T(8,128)(2,1)S(1)}, u32[]{:S(2)}, u32[]{:S(2)}) collective-permute-start(bf16[2,768,768]{2,1,0:T(8,128)(2,1)S(1)} %get-tuple-element.103), channel_id=1, source_target_pairs={{0,1},{1,0},{2,3},{3,2},{4,5},{5,4},{6,7},{7,6},{8,9},{9,8},{10,11... | collective-permute-start | bytes 7077896 | tf_op jit(solution)/shard_map/ppermute | solution.py:28
  668.5 30.8 %collective-permute-start.35 = (bf16[2,768,384]{2,1,0:T(8,128)(2,1)}, bf16[2,768,384]{2,1,0:T(8,128)(2,1)}, u32[]{:S(2)}, u32[]{:S(2)}) collective-permute-start(bf16[2,768,384]{2,1,0:T(8,128)(2,1)} %get-tuple-element.128), channel_id=1, source_target_pairs={{0,1},{1,0},{2,3},{3,2},{4,5},{5,4},{6,7},{7,6},{8,9},{9,8},{10,11... | collective-permute-start | bytes 3538952 | tf_op jit(solution)/shard_map/ppermute | solution.py:28
  (121 other events, 833.3 us)

commit v2 on v1

v2 whole, which is shorter than its diff:
```python
from functools import partial

import jax
import jax.numpy as jnp
from jax import lax
from jax.experimental import pallas as pl
from jax.experimental.pallas import tpu as pltpu
from jax.sharding import PartitionSpec as P

D = 768
HEADS = 12
HEAD_DIM = 64
CLUS = 128
PAIRS = 2
LANES = 128

F32 = jnp.float32
LOW = jnp.bfloat16


def nn(left, right):
    return jnp.dot(left, right, preferred_element_type=F32)


def nt(left, right):
    return lax.dot_general(left, right, (((1,), (1,)), ((), ())), preferred_element_type=F32)


def tn(left, right):
    return lax.dot_general(left, right, (((0,), (0,)), ((), ())), preferred_element_type=F32)


def left_half(shape):
    return lax.broadcasted_iota(jnp.int32, shape, 1) < HEAD_DIM


def pick(hot):
    return jnp.where(hot, 1.0, 0.0).astype(LOW)


def params(megabytes=60):
    return pltpu.CompilerParams(vmem_limit_bytes=megabytes << 20)


def kv_kernel(chosen, tok, w_key, w_value, b_value, order, out, blocks, sem):
    rows = tok.shape[0]
    per_dev = rows // CLUS
    place = lax.broadcasted_iota(jnp.int32, (rows, rows), 1)
    left = left_half((rows, 2 * HEAD_DIM))
    inputs = tok[...]
    for quad in range(HEADS // 4):
        four = slice(quad * 4 * HEAD_DIM, (quad + 1) * 4 * HEAD_DIM)
        keys = nn(inputs, w_key[:, four])
        values = nn(inputs, w_value[:, four]) + b_value[:, four].astype(F32)
        for pair in range(2):
            two = slice(pair * 2 * HEAD_DIM, (pair + 1) * 2 * HEAD_DIM)
            key_two = keys[:, two]
            value_two = pltpu.roll(values[:, two], HEAD_DIM, 1)
            for odd in range(2):
                head = quad * 4 + pair * 2 + odd
                joined = jnp.where(left, value_two, key_two) if odd else jnp.where(left, key_two, value_two)
                hot = pick(order[:, head : head + 1] == place)
                ranked = nn(hot, joined.astype(LOW)).astype(LOW)
                blocks[head * per_dev : (head + 1) * per_dev] = ranked.reshape(per_dev, CLUS, 2 * HEAD_DIM)
    devices, capacity = chosen.shape

    @pl.loop(0, devices)
    def _(device):
        for slot in range(capacity):
            pltpu.make_async_copy(
                blocks.at[chosen[device, slot]], out.at[device * capacity + slot], sem
            ).start()

    pltpu.make_async_copy(out, out, sem).wait()


def q_kernel(tok, w_query, b_query, order, out):
    rows = tok.shape[0]
    place = lax.broadcasted_iota(jnp.int32, (rows, rows), 1)
    left = left_half((rows, 2 * HEAD_DIM))
    inputs = tok[...]
    for quad in range(HEADS // 4):
        four = slice(quad * 4 * HEAD_DIM, (quad + 1) * 4 * HEAD_DIM)
        queries = nn(inputs, w_query[:, four]) + b_query[:, four].astype(F32)
        queries = (queries.astype(LOW).astype(F32) * HEAD_DIM ** (-0.5)).astype(LOW)
        for pair in range(2):
            two = queries[:, pair * 2 * HEAD_DIM : (pair + 1) * 2 * HEAD_DIM]
            for odd in range(2):
                head = quad * 4 + pair * 2 + odd
                hot = pick(order[:, head : head + 1] == place)
                ranked = nn(hot, two)
                kept = jnp.where(left, 0.0, ranked) if odd else jnp.where(left, ranked, 0.0)
                out[head] = kept.astype(LOW)


ROW_TILE = 128
WIDE = 768


def mid_kernel(
    fetch, queries, arrived, order, inverse, tok, cot, vecs, b_up, w_out_hbm, w_up_hbm, w_down_hbm,
    back, dq_out, attn_out, z_out, active_out, du_out, df_out, db_out, dh1_out, layer_out, sums,
    kv, probs, attn, mixed, w_out, w_up, w_down, hidden, z_full, n_one, r_one, z_low, active, slope,
    dh2, df, db, d_out, dh1, final, dq, kv_sem, w_sem, out_sem, back_sem,
):
    rows = tok.shape[0]
    per_dev = rows // CLUS
    pair_width = 2 * HEAD_DIM
    requests = fetch.shape[0]
    each = 2 * per_dev * PAIRS
    width = w_up.shape[1]
    tiles = rows // ROW_TILE
    left = left_half((CLUS, pair_width))
    left_rows = left_half((rows, pair_width))
    down = lax.broadcasted_iota(jnp.int32, (rows, rows), 0)

    @pl.loop(0, HEADS // 2)
    def _(group):
        for step in range(each):
            entry = group * each + step
            pltpu.make_async_copy(arrived.at[fetch[entry]], kv.at[entry], kv_sem.at[group]).start()

    loads = [
        pltpu.make_async_copy(source, target, w_sem.at[at])
        for at, (source, target) in enumerate(
            ((w_out_hbm, w_out), (w_up_hbm, w_up), (w_down_hbm, w_down))
        )
    ]
    for load in loads:
        load.start()
    stores = []

    def store(source, target):
        copy = pltpu.make_async_copy(source, target, out_sem.at[len(stores)])
        copy.start()
        stores.append(copy)

    @pl.loop(0, HEADS // 2)
    def _(group):
        span = kv.at[pl.ds(group * each, each)]
        pltpu.make_async_copy(span, span, kv_sem.at[group]).wait()
        for odd in range(2):
            head = 2 * group + odd
            for cluster in range(per_dev):
                unit = head * per_dev + cluster
                query = queries[head, cluster * CLUS : (cluster + 1) * CLUS, :]
                pair = kv[pl.ds(unit * PAIRS, PAIRS)].reshape(PAIRS * CLUS, pair_width)
                scores = nt(query, pair)
                exponent = jnp.exp(scores - jnp.max(scores, -1, keepdims=True))
                low = (exponent / jnp.sum(exponent, -1, keepdims=True)).astype(LOW)
                probs[unit] = low
                mixed[odd, cluster * CLUS : (cluster + 1) * CLUS, :] = nn(low, pair).astype(LOW)
        even = nn(pick(down == order[2 * group]), mixed[0])
        other = nn(pick(down == order[2 * group + 1]), mixed[1])
        both = pltpu.roll(jnp.where(left_rows, other, even), HEAD_DIM, 1)
        attn[:, pl.ds(pl.multiple_of(group * pair_width, pair_width), pair_width)] = both.astype(LOW)

    store(attn, attn_out)
    loads[0].wait()
    hidden[...] = nn(attn[...], w_out[...])

    @pl.loop(0, tiles)
    def _(tile):
        at = pl.ds(pl.multiple_of(tile * ROW_TILE, ROW_TILE), ROW_TILE)
        value = hidden[at, :] + (vecs[0:1, :] + tok[at, :].astype(F32))
        centred = value - jnp.mean(value, -1, keepdims=True)
        scale = lax.rsqrt(jnp.mean(centred * centred, -1, keepdims=True) + 1e-06)
        unit = centred * scale
        z = unit * vecs[1:2, :] + vecs[2:3, :]
        n_one[at, :] = unit
        r_one[at, :] = scale
        z_low[at, :] = z.astype(LOW)
        z_full[at, :] = z
        hidden[at, :] = z + vecs[3:4, :]

    store(z_low, z_out)
    loads[1].wait()
    loads[2].wait()

    @pl.loop(0, width // WIDE)
    def _(step):
        at = pl.ds(pl.multiple_of(step * WIDE, WIDE), WIDE)
        inner = nn(z_low[...], w_up[:, at]) + b_up[:, at]
        normal = 0.5 * (1.0 + lax.erf(inner * 0.7071067811865476))
        density = jnp.exp(inner * inner * -0.5) * 0.3989422804014327
        active[:, at] = (inner * normal).astype(LOW)
        slope[:, at] = (normal + inner * density).astype(LOW)
        hidden[...] += nn(active[:, at], w_down[at, :])

    store(active, active_out)
    sums[...] = jnp.zeros_like(sums)

    @pl.loop(0, tiles)
    def _(tile):
        at = pl.ds(pl.multiple_of(tile * ROW_TILE, ROW_TILE), ROW_TILE)
        value = hidden[at, :]
        centred = value - jnp.mean(value, -1, keepdims=True)
        scale = lax.rsqrt(jnp.mean(centred * centred, -1, keepdims=True) + 1e-06)
        unit = centred * scale
        final[at, :] = (unit * vecs[4:5, :] + vecs[5:6, :]).astype(LOW)
        grad = cot[at, :].astype(F32)
        lifted = grad * vecs[4:5, :]
        back_grad = scale * (
            lifted - jnp.mean(lifted, -1, keepdims=True) - unit * jnp.mean(lifted * unit, -1, keepdims=True)
        )
        dh2[at, :] = back_grad
        low = back_grad.astype(LOW)
        df[at, :] = low
        sums[0:1, :] += jnp.sum(grad * unit, axis=0, keepdims=True)
        sums[1:2, :] += jnp.sum(grad, axis=0, keepdims=True)
        sums[2:3, :] += jnp.sum(low.astype(F32), axis=0, keepdims=True)

    store(final, layer_out)
    store(df, df_out)
    ones = jnp.ones((8, rows), LOW)

    @pl.loop(0, width // WIDE)
    def _(step):
        at = pl.ds(pl.multiple_of(step * WIDE, WIDE), WIDE)
        grad = (nt(df[...], w_down[at, :]) * slope[:, at].astype(F32)).astype(LOW)
        slope[:, at] = grad
        sums[pl.ds(8 + step, 1), :] = nn(ones, grad)[0:1]
        dh2[...] += nt(grad, w_up[:, at])

    store(slope, du_out)

    @pl.loop(0, tiles)
    def _(tile):
        at = pl.ds(pl.multiple_of(tile * ROW_TILE, ROW_TILE), ROW_TILE)
        grad = dh2[at, :]
        unit = n_one[at, :]
        lifted = grad * vecs[1:2, :]
        back_grad = r_one[at, :] * (
            lifted - jnp.mean(lifted, -1, keepdims=True) - unit * jnp.mean(lifted * unit, -1, keepdims=True)
        )
        dh1[at, :] = back_grad
        low = back_grad.astype(LOW)
        db[at, :] = low
        sums[3:4, :] += jnp.sum(grad * unit, axis=0, keepdims=True)
        sums[4:5, :] += jnp.sum(grad, axis=0, keepdims=True)
        sums[5:6, :] += jnp.sum(low.astype(F32), axis=0, keepdims=True)

    store(dh1, dh1_out)
    store(db, db_out)
    d_out[...] = nt(db[...], w_out[...]).astype(LOW)

    @pl.loop(0, HEADS // 2)
    def _(group):
        lanes = pl.ds(pl.multiple_of(group * pair_width, pair_width), pair_width)
        tile = d_out[:, lanes]
        bias = []
        q_total = jnp.zeros((1, pair_width), F32)
        for odd in range(2):
            head = 2 * group + odd
            turned = pltpu.roll(nn(pick(down == inverse[head]), tile), HEAD_DIM, 1)
            grads = (jnp.where(left_rows, turned, 0.0) if odd else jnp.where(left_rows, 0.0, turned)).astype(LOW)
            total = jnp.zeros((1, pair_width), F32)
            for cluster in range(per_dev):
                unit = head * per_dev + cluster
                query = queries[head, cluster * CLUS : (cluster + 1) * CLUS, :]
                grad = grads[cluster * CLUS : (cluster + 1) * CLUS]
                pair = kv[pl.ds(unit * PAIRS, PAIRS)].reshape(PAIRS * CLUS, pair_width)
                low = probs[unit]
                wide = low.astype(F32)
                d_probs = nt(grad, pair)
                d_scores = (wide * (d_probs - jnp.sum(d_probs * wide, -1, keepdims=True))).astype(LOW)
                d_query = nn(d_scores, pair) * HEAD_DIM ** (-0.5)
                d_query = (jnp.where(left, 0.0, d_query) if odd else jnp.where(left, d_query, 0.0)).astype(LOW)
                dq[head, cluster * CLUS : (cluster + 1) * CLUS, :] = d_query
                q_total += jnp.sum(d_query.astype(F32), axis=0, keepdims=True)
                d_pair = tn(d_scores, query) + tn(low, grad)
                total += jnp.sum(d_pair, axis=0, keepdims=True)
                kv[pl.ds(unit * PAIRS, PAIRS)] = d_pair.astype(LOW).reshape(PAIRS, CLUS, pair_width)
                for part in range(PAIRS):
                    entry = unit * PAIRS + part
                    pltpu.make_async_copy(kv.at[entry], back.at[fetch[entry]], back_sem).start()
            bias.append(total)
        both = jnp.where(left_half((1, pair_width)), bias[1], bias[0])
        sums[7:8, lanes] = q_total
        sums[6:7, lanes] = pltpu.roll(jnp.broadcast_to(both, (8, pair_width)), HEAD_DIM, 1)[0:1]

    store(dq, dq_out)
    span = back.at[pl.ds(0, requests)]
    pltpu.make_async_copy(kv, span, back_sem).wait()
    for copy in stores:
        copy.wait()


CHUNKS = 16


def chunk_rows(at, size):
    return pl.ds(pl.multiple_of(at * size, size), size)


def place_chunks(source, target, info, sem, start=1):
    size = source.shape[0] // CHUNKS
    for chunk in range(CHUNKS):
        pltpu.make_async_copy(
            source.at[chunk * size : (chunk + 1) * size],
            target.at[chunk_rows(info[start + chunk], size)],
            sem,
        ).start()


def wait_chunks(source, target, sem):
    pltpu.make_async_copy(source, target, sem).wait()


def core_of(info, side):
    return info[0] if side else 1 - info[0]


def up_kernel(info, z_low, grad, give, keep, turned, buf, sem):
    half = keep.shape[1]
    turned[...] = z_low[...].T
    for side, out in ((0, give), (1, keep)):
        base = core_of(info, side) * half

        @pl.loop(0, half // WIDE)
        def _(step):
            at = pl.ds(pl.multiple_of(base + step * WIDE, WIDE), WIDE)
            to = pl.ds(pl.multiple_of(step * WIDE, WIDE), WIDE)
            buf[side, :, to] = nn(turned[...], grad[:, at]).astype(LOW)

        place_chunks(buf.at[side], out, info, sem.at[side])
    for side, out in ((0, give), (1, keep)):
        wait_chunks(buf.at[side], out, sem.at[side])


def down_kernel(info, active, grad, give, keep, buf, sem):
    size = keep.shape[0]
    for side, out in ((0, give), (1, keep)):
        for part in range(keep.shape[1] // size):
            block = core_of(info, side) * (keep.shape[1] // size) + part
            at = pl.ds(pl.multiple_of(block * size, size), size)
            buf[side, :, part * size : (part + 1) * size] = nn(active[:, at].T, grad[...]).astype(LOW)
        place_chunks(buf.at[side], out, info, sem.at[side])
    for side, out in ((0, give), (1, keep)):
        wait_chunks(buf.at[side], out, sem.at[side])


def out_q_kernel(info, attn, db, tok, dq, order, sums, give, keep, grad_q, attn_t, tok_t, buf, sem):
    rows = tok.shape[0]
    half = D // 2
    down = lax.broadcasted_iota(jnp.int32, (rows, rows), 0)
    for pair in range(HEADS // 2):
        total = nn(pick(down == order[2 * pair]), dq[2 * pair])
        total += nn(pick(down == order[2 * pair + 1]), dq[2 * pair + 1])
        lanes = slice(pair * 2 * HEAD_DIM, (pair + 1) * 2 * HEAD_DIM)
        grad_q[:, lanes] = total.astype(LOW)
    attn_t[...] = attn[...].T
    tok_t[...] = tok[...].T
    size = D // CHUNKS
    filler = jnp.zeros((size - D // LANES, LANES), F32)
    for vector in range(CHUNKS):
        rows_of = [sums[vector : vector + 1, row * LANES : (row + 1) * LANES] for row in range(D // LANES)]
        value = jnp.concatenate(rows_of + [filler]).astype(LOW)
        for side in range(2):
            buf[side, vector * size : (vector + 1) * size, D:] = value
    for side, out in ((0, give), (1, keep)):
        at = pl.ds(pl.multiple_of(core_of(info, side) * half, half), half)
        buf[side, :, :half] = nn(attn_t[...], db[:, at]).astype(LOW)
        buf[side, :, half:D] = nn(tok_t[...], grad_q[:, at]).astype(LOW)
        place_chunks(buf.at[side], out, info, sem.at[side], 65)
    for side, out in ((0, give), (1, keep)):
        wait_chunks(buf.at[side], out, sem.at[side])


def key_value_kernel(
    info, segment, returned, order, tok, key_give, key_keep, value_give, value_keep, grad_kv, total, tok_t, buf, sem
):
    rows = tok.shape[0]
    half = D // 2
    per_dev = rows // CLUS
    pair_width = 2 * HEAD_DIM
    down = lax.broadcasted_iota(jnp.int32, (rows, rows), 0)
    left = left_half((rows, pair_width))
    total[...] = jnp.zeros_like(total)

    @pl.loop(0, segment.shape[0])
    def _(slot):
        block = segment[slot]
        total[block] += returned[slot].astype(F32)

    for pair in range(HEADS // 2):
        placed = []
        for head in (2 * pair, 2 * pair + 1):
            summed = total[head * per_dev : (head + 1) * per_dev].reshape(rows, pair_width)
            placed.append(nn(pick(down == order[head]), summed.astype(LOW)))
        even, odd = placed
        grad_kv[:, pair * pair_width : (pair + 1) * pair_width] = jnp.where(left, even, odd).astype(LOW)
        values = pltpu.roll(jnp.where(left, odd, even), HEAD_DIM, 1)
        grad_kv[:, D + pair * pair_width : D + (pair + 1) * pair_width] = values.astype(LOW)
    tok_t[...] = tok[...].T
    outs = ((key_give, key_keep), (value_give, value_keep))
    for side in range(2):
        base = core_of(info, side) * half
        for part in range(2):
            at = pl.ds(pl.multiple_of(part * D + base, half), half)
            buf[part, side] = nn(tok_t[...], grad_kv[:, at]).astype(LOW)
            place_chunks(buf.at[part, side], outs[part][side], info, sem.at[part, side], 65 if part else 1)
    for side in range(2):
        for part in range(2):
            wait_chunks(buf.at[part, side], outs[part][side], sem.at[part, side])


def spread_start(info, start, pieces, targets, buf, sem):
    size = buf.shape[2]
    copies = []
    for at, piece in enumerate(pieces):
        core = core_of(info, 1 - at)
        for chunk in range(CHUNKS // 2):
            buf[at, chunk] = piece[chunk * size : (chunk + 1) * size].astype(F32)
            for lanes, target in targets(core, info[start + chunk], size, at == 0):
                copies.append(pltpu.make_async_copy(buf.at[at, chunk, : target.shape[0], lanes], target, sem))
                copies[-1].start()
    return copies


def spread(info, start, pieces, targets, buf, sem):
    for copy in spread_start(info, start, pieces, targets, buf, sem):
        copy.wait()


def up_targets(out, half):
    def targets(core, chunk, size, mine):
        rows = chunk_rows(chunk, size)
        yield pl.ds(0, half), out.at[rows, pl.ds(pl.multiple_of(core * half, half), half)]

    return targets


def down_targets(out, half):
    parts = half // D

    def targets(core, chunk, size, mine):
        rows = chunk_rows(chunk, size)
        for part in range(parts):
            yield pl.ds(part * D, D), out.at[core * parts + part, rows]

    return targets


def attention_targets(w_out, w_qkv, vectors, wide):
    half = D // 2

    def targets(core, chunk, size, mine):
        rows = chunk_rows(chunk, size)
        at = pl.ds(pl.multiple_of(core * half, half), half)
        yield pl.ds(0, half), w_out.at[rows, at]
        for part, lane in enumerate((half, D + LANES, D + LANES + half)):
            to = pl.ds(pl.multiple_of(part * D + core * half, half), half)
            yield pl.ds(lane, half), w_qkv.at[rows, to]
        if mine:
            yield pl.ds(D, LANES), vectors.at[chunk]

    return targets


def spread_kernel(start, route, count, info, mine, other, *refs):
    buf, sem = refs[-2:]
    spread(info, start, (mine, other), route(*refs[:count], mine.shape[1]), buf, sem)


def spread_last_kernel(info, *refs):
    pieces, outs, staged, bufs = refs[:6], refs[11:16], refs[16:22], refs[22:25]
    load_sem, sem = refs[25:]
    w_up, w_down, w_out, w_qkv, vectors = outs
    half = w_up.shape[1] // 2
    loads = []
    for at, (source, target) in enumerate(zip(pieces, staged)):
        loads.append(pltpu.make_async_copy(source, target, load_sem.at[at]))
        loads[-1].start()
    routes = (up_targets(w_up, half), down_targets(w_down, half), attention_targets(w_out, w_qkv, vectors, half))
    copies = []
    for at, (start, targets) in enumerate(zip((25, 41, 57), routes)):
        for load in loads[2 * at : 2 * at + 2]:
            load.wait()
        copies += spread_start(info, start, staged[2 * at : 2 * at + 2], targets, bufs[at], sem.at[at])
    for copy in copies:
        copy.wait()


X, Y, Z0, Z1 = ("dp", 1), ("blk", 2), ("blk", 4), ("blk", 8)
CORE = ("blk", 1)


def swap(value, bit):
    axis, distance = bit
    size = lax.axis_size(axis)
    return lax.ppermute(value, axis, [(i, i ^ distance) for i in range(size)])


def further_bits(count_blk):
    bits = []
    distance = 16
    while distance < count_blk:
        bits.append(("blk", distance))
        distance *= 2
    return bits


def chip_bits():
    return [(lax.axis_index(axis) // distance) % 2 for axis, distance in (X, Y, Z0, Z1)]


def chunk_places():
    x, y, z0, z1 = chip_bits()
    chip = x * 8 + y * 4 + z0 * 2 + z1
    core = lax.axis_index("blk") % 2
    every = jnp.arange(CHUNKS, dtype=jnp.int32)
    value = {X: 8, Y: 4, Z0: 2, Z1: 1}

    def from_order(order):
        at = sum(((every // 2**step) % 2) * value[bit] for step, bit in enumerate(order))
        return at ^ chip

    placed = every ^ chip
    x_y_swapped = placed % 4 + (placed // 8) * 4 + (placed // 4 % 2) * 8
    return jnp.concatenate(
        [core[None], placed]
        + [from_order(order) for order in (ORDER_X, ORDER_Y, ORDER_Z)]
        + [x_y_swapped]
    )


ORDER_X = (Z1, Z0, Y, X)
ORDER_Y = (Z1, X, Z0, Y)
ORDER_Z = (Z1, Y, X, Z0)


def sum_rows(terms, low, high):
    total = terms[0][low:high].astype(F32)
    for term in terms[1:]:
        total = total + term[low:high].astype(F32)
    return total


def scatter_start(terms, bits):
    rows = terms[-1].shape[0]
    for bit in bits:
        if len(terms) > 2:
            rows = terms[-1].shape[0]
        terms = terms + [swap(sum_rows(terms, rows // 2, rows).astype(LOW), bit)]
        rows //= 2
    return terms


def scatter_end(sets, bits, further):
    rows = sets[0][-1].shape[0]
    more = []

    def total(low, high):
        value = jnp.concatenate([sum_rows(terms, low, high) for terms in sets], axis=1)
        for term in more:
            value = value + term[low:high].astype(F32)
        return value.astype(LOW)

    for bit in bits:
        more.append(swap(total(rows // 2, rows), bit))
        rows //= 2
    value = total(0, rows)
    for bit in further:
        value = sum_rows([value, swap(value, bit)], 0, rows).astype(LOW)
    return value


def tie(values):
    return lax.optimization_barrier(tuple(values))


def gather_rows(values, orders):
    for step in range(len(orders[0]) - 1):
        values = tie(
            jnp.concatenate([value, swap(value, order[step])]) for value, order in zip(values, orders)
        )
    return values


def per_device(
    tokens,
    w_qkv,
    b_query,
    b_value,
    w_out,
    b_out,
    gain_one,
    shift_one,
    w_up,
    b_up,
    w_down,
    b_down,
    gain_two,
    shift_two,
    cluster_perm,
    cluster_pairs,
    cotangent,
):
    count_blk = lax.axis_size("blk")
    my_index = lax.axis_index("blk")
    rows = tokens.shape[0]
    per_dev = rows // CLUS
    blocks = HEADS * per_dev
    requests = blocks * PAIRS
    capacity = max(2, (requests + count_blk - 1) // count_blk + 1)
    slots = count_blk * capacity
    pair_width = 2 * HEAD_DIM
    ff = w_up.shape[1]
    local_order = cluster_perm[0] - my_index * rows
    order_cols = local_order.T
    order_rows = local_order[:, None, :]

    wanted = (
        cluster_pairs[0]
        .reshape(HEADS, count_blk, per_dev, PAIRS)
        .transpose(1, 0, 2, 3)
        .reshape(count_blk, requests)
    )
    positions = jnp.arange(requests, dtype=jnp.int32)
    before = positions[:, None] < positions[None, :]
    source = wanted // per_dev
    named = source == my_index
    rank = jnp.sum(named[:, :, None] & before[None], axis=1)
    head_of = positions // (per_dev * PAIRS)
    block_id = head_of[None, :] * per_dev + wanted % per_dev
    matches = named[:, :, None] & (
        rank[:, :, None] == jnp.arange(capacity, dtype=jnp.int32)[None, None, :]
    )
    chosen = jnp.sum(jnp.where(matches, block_id[:, :, None], 0), axis=1)

    smem = pl.BlockSpec(memory_space=pltpu.SMEM)
    vmem = pl.BlockSpec(memory_space=pltpu.VMEM)
    hbm = pl.BlockSpec(memory_space=pl.ANY)

    def column_block(at):
        return pl.BlockSpec((D, D), lambda step: (0, at))

    outgoing = pl.pallas_call(
        kv_kernel,
        grid=(1,),
        out_shape=jax.ShapeDtypeStruct((slots, CLUS, pair_width), LOW),
        in_specs=[smem, vmem, column_block(1), column_block(2), vmem, vmem],
        out_specs=hbm,
        scratch_shapes=[pltpu.VMEM((blocks, CLUS, pair_width), LOW), pltpu.SemaphoreType.DMA],
        compiler_params=params(),
        name="kv_kernel",
    )(chosen, tokens, w_qkv, w_qkv, b_value[None], order_cols)
    arrived = lax.all_to_all(
        outgoing.reshape(count_blk, capacity, CLUS, pair_width),
        "blk",
        split_axis=0,
        concat_axis=0,
        tiled=True,
    ).reshape(slots, CLUS, pair_width)

    info = chunk_places()
    queries = pl.pallas_call(
        q_kernel,
        grid=(1,),
        out_shape=jax.ShapeDtypeStruct((HEADS, rows, pair_width), LOW),
        in_specs=[vmem, column_block(0), vmem, vmem],
        out_specs=vmem,
        compiler_params=params(),
        name="q_kernel",
    )(tokens, w_qkv, b_query[None], order_cols)
    filled = jnp.any(matches, axis=1)
    segment = jnp.where(filled, chosen, blocks).reshape(-1)
    my_source = lax.dynamic_index_in_dim(wanted, my_index, 0, keepdims=False) // per_dev
    my_rank = jnp.sum((my_source[:, None] == my_source[None, :]) & before, axis=0)
    fetch = my_source * capacity + my_rank
    places = jnp.arange(rows, dtype=jnp.int32)
    inverse = jnp.sum(
        jnp.where(local_order[:, :, None] == places, places[None, :, None], 0), axis=1
    )[:, None, :]
    vecs = jnp.stack(
        [b_out, gain_one, shift_one, b_down, gain_two, shift_two, b_down, b_down]
    ).astype(F32)

    def low(*shape):
        return jax.ShapeDtypeStruct(shape, LOW)

    def full(*shape):
        return jax.ShapeDtypeStruct(shape, F32)

    (
        back, dq_sorted, attn, normed, active, grad_inner, grad_second, grad_branch, grad_resid,
        layer_out, sums,
    ) = pl.pallas_call(
        mid_kernel,
        out_shape=(
            low(slots, CLUS, pair_width), low(HEADS, rows, pair_width), low(rows, D), low(rows, D),
            low(rows, ff), low(rows, ff), low(rows, D), low(rows, D), full(rows, D), low(rows, D),
            full(16, D),
        ),
        in_specs=[smem, vmem, hbm, vmem, vmem, vmem, vmem, vmem, vmem, hbm, hbm, hbm],
        out_specs=(hbm,) * 10 + (vmem,),
        scratch_shapes=[
            pltpu.VMEM((requests, CLUS, pair_width), LOW),
            pltpu.VMEM((blocks, CLUS, PAIRS * CLUS), LOW),
            pltpu.VMEM((rows, D), LOW),
            pltpu.VMEM((2, rows, pair_width), LOW),
            pltpu.VMEM((D, D), LOW),
            pltpu.VMEM((D, ff), LOW),
            pltpu.VMEM((ff, D), LOW),
            pltpu.VMEM((rows, D), F32),
            pltpu.VMEM((rows, D), F32),
            pltpu.VMEM((rows, D), F32),
            pltpu.VMEM((rows, 1), F32),
            pltpu.VMEM((rows, D), LOW),
            pltpu.VMEM((rows, ff), LOW),
            pltpu.VMEM((rows, ff), LOW),
            pltpu.VMEM((rows, D), F32),
            pltpu.VMEM((rows, D), LOW),
            pltpu.VMEM((rows, D), LOW),
            pltpu.VMEM((rows, D), LOW),
            pltpu.VMEM((rows, D), F32),
            pltpu.VMEM((rows, D), LOW),
            pltpu.VMEM((HEADS, rows, pair_width), LOW),
            pltpu.SemaphoreType.DMA((HEADS // 2,)),
            pltpu.SemaphoreType.DMA((3,)),
            pltpu.SemaphoreType.DMA((9,)),
            pltpu.SemaphoreType.DMA,
        ],
        compiler_params=params(),
        name="mid_kernel",
    )(
        fetch, queries, arrived, order_rows, inverse, tokens, cotangent, vecs,
        b_up[None].astype(F32), w_out, w_up, w_down,
    )
    returned = lax.all_to_all(
        back.reshape(count_blk, capacity, CLUS, pair_width),
        "blk",
        split_axis=0,
        concat_axis=0,
        tiled=True,
    ).reshape(slots, CLUS, pair_width)

    further = further_bits(count_blk)

    def halves(kernel, operands, columns, scratch, more=(), name=None):
        return pl.pallas_call(
            kernel,
            out_shape=(low(D, columns), low(D, columns)) + more,
            in_specs=[smem] + [vmem] * (len(operands) - 1),
            out_specs=(hbm, hbm) + (vmem,) * len(more),
            scratch_shapes=scratch
            + [pltpu.VMEM((2, D, columns), LOW), pltpu.SemaphoreType.DMA((2,))],
            compiler_params=params(),
            cost_estimate=pl.CostEstimate(flops=1, bytes_accessed=1, transcendentals=0),
            name=name,
        )(*operands)

    half = D // 2
    turned = pltpu.VMEM((D, rows), LOW)
    up_give, up_keep = halves(
        up_kernel, (info, normed, grad_inner), ff // 2, [turned], name="up_kernel"
    )
    down_give, down_keep = halves(
        down_kernel, (info, active, grad_second), ff // 2, [], name="down_kernel"
    )
    oq_give, oq_keep, grad_q = halves(
        out_q_kernel,
        (info, attn, grad_branch, tokens, dq_sorted, order_rows, sums),
        D + LANES,
        [turned, turned],
        (low(rows, D),),
        name="out_q_kernel",
    )
    up = scatter_start([up_keep, swap(up_give, CORE)], (X, Y))
    down = scatter_start([down_keep, swap(down_give, CORE)], (X, Y))
    out_q = scatter_start([oq_keep, swap(oq_give, CORE)], (Y, X))

    returned, up[-1], down[-1], out_q[-1] = tie((returned, up[-1], down[-1], out_q[-1]))
    key_give, key_keep, value_give, value_keep, grad_kv = pl.pallas_call(
        key_value_kernel,
        out_shape=(low(D, half),) * 4 + (low(rows, 2 * D),),
        in_specs=[smem, smem, vmem, vmem, vmem],
        out_specs=(hbm,) * 4 + (vmem,),
        scratch_shapes=[
            pltpu.VMEM((blocks + 1, CLUS, pair_width), F32),
            turned,
            pltpu.VMEM((2, 2, D, half), LOW),
            pltpu.SemaphoreType.DMA((2, 2)),
        ],
        compiler_params=params(),
        name="key_value_kernel",
    )(info, segment, returned, order_rows, tokens)
    key = scatter_start([key_keep, swap(key_give, CORE)], (X, Y))
    value = scatter_start([value_keep, swap(value_give, CORE)], (Y, X))
    early = scatter_end([up, down, out_q], (Z0, Z1), further)
    late = scatter_end([key, value], (Z0, Z1), further)
    grad_proj = jnp.concatenate([grad_q, grad_kv], axis=1)
    grad_tokens = (grad_resid + nt(grad_proj, w_qkv)).astype(LOW)
    early, late, grad_tokens = tie((early, late, grad_tokens))
    wide = ff // 2
    up = early[:, :wide]
    down = early[:, wide : 2 * wide]
    rest = jnp.concatenate([early[:, 2 * wide :], late], axis=1)

    def spread_call(start, route, mine, other, outs):
        count = len(outs)
        return pl.pallas_call(
            partial(spread_kernel, start, route, count),
            out_shape=outs,
            in_specs=[smem, vmem, vmem],
            out_specs=(hbm,) * count,
            scratch_shapes=[
                pltpu.VMEM((2, CHUNKS // 2, D // CHUNKS, mine.shape[1]), F32),
                pltpu.SemaphoreType.DMA,
            ],
            compiler_params=params(),
            cost_estimate=pl.CostEstimate(flops=20_000_000_000, bytes_accessed=20_000_000, transcendentals=0),
            name=route.__name__,
        )(info, mine, other)

    orders = (ORDER_X, ORDER_Y, ORDER_Z)
    mine = gather_rows((up, down, rest), orders)
    last = [swap(value, order[-1]) for value, order in zip(mine, orders)]
    other = [swap(value, CORE) for value in mine]
    outs = []
    for at, (start, route, shapes) in enumerate(
        (
            (17, up_targets, (full(D, ff),)),
            (33, down_targets, (full(ff // D, D, D),)),
            (49, attention_targets, (full(D, D), full(D, 3 * D), full(CHUNKS, 8, LANES))),
        )
    ):
        outs += spread_call(start, route, mine[at], other[at], shapes)
    last_pieces = []
    for value in last:
        last_pieces += [value, swap(value, CORE)]
    sum_up, sum_down, sum_out, sum_qkv, vectors = pl.pallas_call(
        spread_last_kernel,
        out_shape=tuple(full(*out.shape) for out in outs),
        in_specs=[smem] + [hbm] * 11,
        out_specs=(hbm,) * 5,
        scratch_shapes=[pltpu.VMEM(piece.shape, LOW) for piece in last_pieces]
        + [
            pltpu.VMEM((2, CHUNKS // 2, D // CHUNKS, piece.shape[1]), F32)
            for piece in last_pieces[::2]
        ]
        + [
            pltpu.SemaphoreType.DMA((6,)),
            pltpu.SemaphoreType.DMA((3,)),
        ],
        input_output_aliases={7 + at: at for at in range(5)},
        compiler_params=params(),
        name="spread_last",
    )(info, *last_pieces, *outs)
    vectors = vectors[:, : D // LANES].reshape(CHUNKS, D)
    return (
        layer_out,
        grad_tokens,
        sum_qkv,
        vectors[7],
        vectors[6],
        sum_out,
        vectors[5],
        vectors[3],
        vectors[4],
        sum_up,
        vectors[8 : 8 + ff // D].reshape(ff),
        sum_down.reshape(ff, D),
        vectors[2],
        vectors[0],
        vectors[1],
    )


def solution(mesh):
    whole = P()
    rows = P(("dp", "blk"), None)
    return jax.shard_map(
        per_device,
        mesh=mesh,
        in_specs=(
            (rows,)
            + (whole,) * 13
            + (P("dp", None, "blk"), P("dp", None, None, None), rows)
        ),
        out_specs=(rows, rows) + (whole,) * 13,
        check_vma=False,
    )
```

time: 729 us -> 428 us (0.59)
  local copies, waits for them, and re-layouts: 148 us -> 10.2 us
  matrix products: 142 us -> 5.05 us
  Pallas kernels: 0 us -> 114 us
  other arithmetic: 121 us -> 24.2 us
  blocking collectives: 39.1 us -> 0 us
  starting transfers between devices: 90.1 us -> 62.5 us
  waiting for transfers between devices: 178 us -> 202 us
    dot_general x26 -> x1, matrix products: 142 us -> 5.05 us  [nt(): lax.dot_general(left, right, (((1,), (1,)), ((), ())), preferred_element_...]
    pallas_call x0 -> x11, Pallas kernels: none -> 114 us  [the longest x1 51.2 us: per_device(): pl.pallas_call(mid_kernel, out_shape=(low(slots, CLUS, pair_width), low(H...]
    unnamed x155 -> x52, local copies, waits for them, and re-layouts: 43.3 us -> 1.97 us
    psum x1 -> x0, blocking collectives: 39.1 us -> none  [per_device(): totals = lax.psum(jnp.concatenate(vectors), ('dp', 'blk'))]
    convert_element_type x47 -> x16, other arithmetic: 40.1 us -> 10.8 us  [the longest x10 9.35 us: scatter_start(): terms = terms + [swap(sum_rows(terms, rows // 2, rows).astype(LOW), bit)]]
    ppermute x72 -> x37, starting transfers between devices: 64.8 us -> 36.9 us  [swap(): return lax.ppermute(value, axis, [(i, i ^ distance) for i in range(size)])]
    convert_element_type x5 -> x0, local copies, waits for them, and re-layouts: 23.4 us -> none  [the longest x1 13.4 us: per_device(): sum_up.astype(jnp.float32)]
    scatter-add x1 -> x0, other arithmetic: 22.8 us -> none  [per_device(): jax.ops.segment_sum(returned_grads.reshape(count_blk * capacity, CLUS, pa...]
  transfers between devices with their start and end apart: 74 -> 39, of which waited for: 45 -> 21; matrix products, arithmetic and copies ran while one was open for 27% -> 7% of each run, Pallas kernels for 0% -> 9%
where the time goes in v2:
time: 428 us; the launch traced here: 421 us
  waiting for transfers between devices  202 us (47%)
  Pallas kernels  114 us (27%)
  starting transfers between devices  62.5 us (15%)
  other arithmetic  24.2 us (6%)
  local copies, waits for them, and re-layouts  10.2 us (2%)
  matrix products  5.05 us (1%)
    ppermute x37, waiting for transfers between devices, swap(): return lax.ppermute(value, axis, [(i, i ^ distance) for i in range(size)])  146 us
    all_to_all x1, waiting for transfers between devices, per_device(): lax.all_to_all(outgoing.reshape(count_blk, capacity, CLUS, pair_width), '...  56.9 us
    pallas_call x1, Pallas kernels, per_device(): pl.pallas_call(mid_kernel, out_shape=(low(slots, CLUS, pair_width), low(H...  51.2 us
    ppermute x37, starting transfers between devices, swap(): return lax.ppermute(value, axis, [(i, i ^ distance) for i in range(size)])  36.9 us
    pallas_call x3, Pallas kernels, halves(): pl.pallas_call(kernel, out_shape=(low(D, columns), low(D, columns)) + mor...  20.9 us
    all_to_all x1, starting transfers between devices, per_device(): lax.all_to_all(back.reshape(count_blk, capacity, CLUS, pair_width), 'blk'...  17.8 us
    pallas_call x3, Pallas kernels, spread_call(): pl.pallas_call(partial(spread_kernel, start, route, count), out_shape=out...  12 us
    pallas_call x1, Pallas kernels, per_device(): pl.pallas_call(key_value_kernel, out_shape=(low(D, half),) * 4 + (low(row...  9.56 us
  transfers between devices with their start and end apart: 39, of which 21 were waited for; matrix products, arithmetic and copies ran while one was open for 7% of the time, Pallas kernels for 9%

profile of v2, /device:TPU:0, one launch (start us, length us, event | category | flops | bytes accessed | tf_op | source)
XLA Modules:
  0.0 420.8 jit_solution(1467979266111839176)
XLA Ops:
  5.8 7.5 %kv_kernel.1 = bf16[112,128,128]{2,1,0:T(8,128)(2,1)} custom-call(s32[16,7]{1,0:T(8,128)} %copy.70.chosen, bf16[512,768]{1,0:T(8,128)(2,1)} %tok.9, bf16[768,2304]{1,0:T(8,128)(2,1)} %w_value.1, bf16[768,2304]{1,0:T(8,128)(2,1)} %w_value.1, bf16[1,768]{1,0:T(2,128)(2,1)} %broadcast_in_dim.59.b_value, s32[512,12]{1,0:T(8,128)} %bitcast.39), custom_call_target="tpu_custom_call" | custom-call | tf_op jit(solution)/shard_map/kv_kernel/pallas_call | solution.py:639
  13.4 7.8 %all-to-all-start = ((bf16[16,7,128,128]{3,2,1,0:T(8,128)(2,1)}), bf16[16,7,128,128]{3,2,1,0:T(8,128)(2,1)}, u32[]{:S(2)}, u32[]{:S(2)}) async-start(bf16[16,7,128,128]{3,2,1,0:T(8,128)(2,1)} %bitcast.36), calls=%async_computation | async-start | bytes 7340032 | tf_op jit(solution)/shard_map/all_to_all | solution.py:649
  25.6 5.8 %q_kernel.1.queries = bf16[12,512,128]{2,1,0:T(8,128)(2,1)} custom-call(bf16[512,768]{1,0:T(8,128)(2,1)} %tok.9, bf16[768,2304]{1,0:T(8,128)(2,1)} %w_value.1, bf16[1,768]{1,0:T(2,128)(2,1)} %broadcast_in_dim.36.b_query, s32[512,12]{1,0:T(8,128)} %bitcast.40), custom_call_target="tpu_custom_call" | custom-call | tf_op jit(solution)/shard_map/q_kernel/pallas_call | solution.py:658
  32.9 56.9 %all-to-all-done = bf16[16,7,128,128]{3,2,1,0:T(8,128)(2,1)} async-done(((bf16[16,7,128,128]{3,2,1,0:T(8,128)(2,1)}), bf16[16,7,128,128]{3,2,1,0:T(8,128)(2,1)}, u32[]{:S(2)}, u32[]{:S(2)}) %all-to-all-start) | async-done | bytes 3670048 | tf_op jit(solution)/shard_map/all_to_all | solution.py:649
  89.7 51.2 %mid_kernel.1 = (bf16[112,128,128]{2,1,0:T(8,128)(2,1)}, bf16[12,512,128]{2,1,0:T(8,128)(2,1)}, bf16[512,768]{1,0:T(8,128)(2,1)}, bf16[512,768]{1,0:T(8,128)(2,1...) custom-call(s32[96]{0:T(128)} %multiply_add_fusion.fetch, ...), custom_call_target="tpu_custom_call" | custom-call | tf_op jit(solution)/shard_map/mid_kernel/pallas_call | solution.py:689
  140.9 17.8 %all-to-all-start.1 = ((bf16[16,7,128,128]{3,2,1,0:T(8,128)(2,1)}), bf16[16,7,128,128]{3,2,1,0:T(8,128)(2,1)}, u32[]{:S(2)}, u32[]{:S(2)}) async-start(bf16[16,7,128,128]{3,2,1,0:T(8,128)(2,1)} %bitcast.38), calls=%async_computation.1 | async-start | bytes 7340032 | tf_op jit(solution)/shard_map/all_to_all | solution.py:731
  159.5 7.1 %up_kernel.1 = (bf16[768,1536]{1,0:T(8,128)(2,1)}, bf16[768,1536]{1,0:T(8,128)(2,1)}) custom-call(s32[81]{0:T(128)} %concatenate.56.info, bf16[512,768]{1,0:T(8,128)(2,1)} %get-tuple-element.63.z_low, bf16[512,3072]{1,0:T(8,128)(2,1)} %get-tuple-element.64.grad), custom_call_target="tpu_custom_call" | custom-call | flops 1 | bytes 1 | tf_op jit(solution)/shard_map/up_kernel/pallas_call | solution.py:742
  167.2 6.2 %down_kernel.1 = (bf16[768,1536]{1,0:T(8,128)(2,1)}, bf16[768,1536]{1,0:T(8,128)(2,1)}) custom-call(s32[81]{0:T(128)} %concatenate.56.info, bf16[512,3072]{1,0:T(8,128)(2,1)} %get-tuple-element.68.active, bf16[512,768]{1,0:T(8,128)(2,1)} %get-tuple-element.69.grad), custom_call_target="tpu_custom_call" | custom-call | flops 1 | bytes 1 | tf_op jit(solution)/shard_map/down_kernel/pallas_call | solution.py:742
  173.4 7.6 %out_q_kernel.1 = (bf16[768,896]{1,0:T(8,128)(2,1)}, bf16[768,896]{1,0:T(8,128)(2,1)}, bf16[512,768]{1,0:T(8,128)(2,1)}) custom-call(s32[81]{0:T(128)} %concatenate.56.info, bf16[512,768]{1,0:T(8,128)(2,1)} %get-tuple-element.72.attn, bf16[512,768]{1,0:T(8,128)(2,1)} %get-tuple-element.73.db, bf16[512,768]{1,0:T(8,128)(2,1)} %tok.9, ...), custom_call_target="tpu_custom_call" | custom-call | flops 1 | bytes 1 | tf_op jit(solution)/shard_map/out_q_kernel/pallas_call | solution.py:742
  189.1 23.1 %collective-permute-done.1 = bf16[384,1536]{1,0:T(8,128)(2,1)S(1)} collective-permute-done((bf16[384,1536]{1,0:T(8,128)(2,1)S(1)}, bf16[384,1536]{1,0:T(8,128)(2,1)S(1)}, u32[]{:S(2)}, u32[]{:S(2)}) %collective-permute-start.1) | collective-permute-done | bytes 1179680 | tf_op jit(solution)/shard_map/ppermute | solution.py:492
  215.9 20.6 %collective-permute-done.4 = bf16[384,1536]{1,0:T(8,128)(2,1)S(1)} collective-permute-done((bf16[384,1536]{1,0:T(8,128)(2,1)S(1)}, bf16[384,1536]{1,0:T(8,128)(2,1)S(1)}, u32[]{:S(2)}, u32[]{:S(2)}) %collective-permute-start.4) | collective-permute-done | bytes 1179680 | tf_op jit(solution)/shard_map/ppermute | solution.py:492
  244.4 7.2 %collective-permute-done.8 = bf16[192,896]{1,0:T(8,128)(2,1)} collective-permute-done((bf16[192,896]{1,0:T(8,128)(2,1)}, bf16[192,896]{1,0:T(8,128)(2,1)}, u32[]{:S(2)}, u32[]{:S(2)}) %collective-permute-start.8) | collective-permute-done | bytes 344096 | tf_op jit(solution)/shard_map/ppermute | solution.py:492
  254.4 9.6 %key_value_kernel.1 = (bf16[768,384]{1,0:T(8,128)(2,1)}, bf16[768,384]{1,0:T(8,128)(2,1)}, bf16[768,384]{1,0:T(8,128)(2,1)}, bf16[768,384]{1,0:T(8,128)(2,1)}, bf16[512,1536]{1,0:T(8,128)(2,1)}) custom-call(s32[81]{0:T(128)} %concatenate.56.info, s32[112]{0:T(128)} %select_n.216.segment, bf16[112,128,128]{2,1,0:T(8,128)(2,1)} %bitcast.10.returned, ...), custom_call_target="tpu_custom_call" | custom-call | tf_op jit(solution)/shard_map/key_value_kernel/pallas_call | solution.py:775
  270.5 5.1 %add_convert_fusion.2 = bf16[512,768]{1,0:T(8,128)(2,1)} fusion(f32[512,768]{1,0:T(8,128)} %get-tuple-element.86, bf16[768,2304]{1,0:T(8,128)(2,1)S(1)} %copy-done, bf16[512,1536]{1,0:T(8,128)(2,1)} %get-tuple-element.88, bf16[512,768]{1,0:T(8,128)(2,1)} %get-tuple-element.87), kind=kOutput, calls=%fused_computation.8 | convolution fusion | flops 1817444352 | bytes 8257536 | tf_op jit(solution)/shard_map/dot_general | solution.py:26
  282.9 4.8 %collective-permute-done.9 = bf16[96,3968]{1,0:T(8,128)(2,1)S(1)} collective-permute-done((bf16[96,3968]{1,0:T(8,128)(2,1)S(1)}, bf16[96,3968]{1,0:T(8,128)(2,1)S(1)}, u32[]{:S(2)}, u32[]{:S(2)}) %collective-permute-start.9) | collective-permute-done | bytes 761888 | tf_op jit(solution)/shard_map/ppermute | solution.py:492
  299.1 10.0 %collective-permute-done.17 = bf16[96,768]{1,0:T(8,128)(2,1)S(1)} collective-permute-done((bf16[96,768]{1,0:T(8,128)(2,1)S(1)}, bf16[96,768]{1,0:T(8,128)(2,1)S(1)}, u32[]{:S(2)}, u32[]{:S(2)}) %collective-permute-start.17) | collective-permute-done | bytes 147488 | tf_op jit(solution)/shard_map/ppermute | solution.py:492
  310.6 9.7 %collective-permute-done.18 = bf16[48,768]{1,0:T(8,128)(2,1)S(1)} collective-permute-done((bf16[48,768]{1,0:T(8,128)(2,1)S(1)}, bf16[48,768]{1,0:T(8,128)(2,1)S(1)}, u32[]{:S(2)}, u32[]{:S(2)}) %collective-permute-start.18) | collective-permute-done | bytes 73760 | tf_op jit(solution)/shard_map/ppermute | solution.py:492
  334.9 5.1 %collective-permute-done.22 = bf16[96,1536]{1,0:T(8,128)(2,1)S(1)} collective-permute-done((bf16[96,1536]{1,0:T(8,128)(2,1)S(1)}, bf16[96,1536]{1,0:T(8,128)(2,1)S(1)}, u32[]{:S(2)}, u32[]{:S(2)}) %collective-permute-start.22) | collective-permute-done | bytes 294944 | tf_op jit(solution)/shard_map/ppermute | solution.py:492
  347.2 7.3 %collective-permute-done.25 = bf16[192,1536]{1,0:T(8,128)(2,1)S(1)} collective-permute-done((bf16[192,1536]{1,0:T(8,128)(2,1)S(1)}, bf16[192,1536]{1,0:T(8,128)(2,1)S(1)}, u32[]{:S(2)}, u32[]{:S(2)}) %collective-permute-start.25) | collective-permute-done | bytes 589856 | tf_op jit(solution)/shard_map/ppermute | solution.py:492
  355.2 6.9 %collective-permute-done.27 = bf16[192,1664]{1,0:T(8,128)(2,1)S(1)} collective-permute-done((bf16[192,1664]{1,0:T(8,128)(2,1)S(1)}, bf16[192,1664]{1,0:T(8,128)(2,1)S(1)}, u32[]{:S(2)}, u32[]{:S(2)}) %collective-permute-start.27) | collective-permute-done | bytes 639008 | tf_op jit(solution)/shard_map/ppermute | solution.py:492
  365.1 17.8 %collective-permute-done.28.refs_0_ = bf16[384,1536]{1,0:T(8,128)(2,1)} collective-permute-done((bf16[384,1536]{1,0:T(8,128)(2,1)S(1)}, bf16[384,1536]{1,0:T(8,128)(2,1)}, u32[]{:S(2)}, u32[]{:S(2)}) %collective-permute-start.28) | collective-permute-done | bytes 1179680 | tf_op jit(solution)/shard_map/ppermute | solution.py:492
  383.3 8.0 %collective-permute-done.30.refs_2_ = bf16[384,1536]{1,0:T(8,128)(2,1)} collective-permute-done((bf16[384,1536]{1,0:T(8,128)(2,1)S(1)}, bf16[384,1536]{1,0:T(8,128)(2,1)}, u32[]{:S(2)}, u32[]{:S(2)}) %collective-permute-start.30) | collective-permute-done | bytes 1179680 | tf_op jit(solution)/shard_map/ppermute | solution.py:492
  399.0 5.8 %collective-permute-done.32.refs_4_ = bf16[384,1664]{1,0:T(8,128)(2,1)S(1)} collective-permute-done((bf16[384,1664]{1,0:T(8,128)(2,1)S(1)}, bf16[384,1664]{1,0:T(8,128)(2,1)S(1)}, u32[]{:S(2)}, u32[]{:S(2)}) %collective-permute-start.32) | collective-permute-done | bytes 1277984 | tf_op jit(solution)/shard_map/ppermute | solution.py:492
  410.3 7.4 %spread_last.1 = (f32[768,3072]{1,0:T(8,128)}, f32[4,768,768]{2,1,0:T(8,128)}, f32[768,768]{1,0:T(8,128)}, f32[768,2304]{1,0:T(8,128)}, f32[16,8,128]{2,1,0:T(8,128)}) custom-call(s32[81]{0:T(128)} %concatenate.56.info, ...), custom_call_target="tpu_custom_call", output_to_operand_aliasing={{0}: (7, {}), {1}: (8, {}), {2}: (9, {}), {3}: (10, {}), {4... | custom-call | tf_op jit(solution)/shard_map/spread_last/pallas_call | solution.py:833
  (196 shorter events, 102.6 us)
Async XLA Ops:
  13.4 76.3 %all-to-all-start = ((bf16[16,7,128,128]{3,2,1,0:T(8,128)(2,1)}), bf16[16,7,128,128]{3,2,1,0:T(8,128)(2,1)}, u32[]{:S(2)}, u32[]{:S(2)}) async-start(bf16[16,7,128,128]{3,2,1,0:T(8,128)(2,1)} %bitcast.36), calls=%async_computation | async-start | bytes 7340032 | tf_op jit(solution)/shard_map/all_to_all | solution.py:649
  140.9 113.5 %all-to-all-start.1 = ((bf16[16,7,128,128]{3,2,1,0:T(8,128)(2,1)}), bf16[16,7,128,128]{3,2,1,0:T(8,128)(2,1)}, u32[]{:S(2)}, u32[]{:S(2)}) async-start(bf16[16,7,128,128]{3,2,1,0:T(8,128)(2,1)} %bitcast.38), calls=%async_computation.1 | async-start | bytes 7340032 | tf_op jit(solution)/shard_map/all_to_all | solution.py:731
  166.6 15.0 %collective-permute-start = (bf16[768,1536]{1,0:T(8,128)(2,1)}, bf16[768,1536]{1,0:T(8,128)(2,1)}, u32[]{:S(2)}, u32[]{:S(2)}) collective-permute-start(bf16[768,1536]{1,0:T(8,128)(2,1)} %get-tuple-element.66), channel_id=1, source_target_pairs={{0,1},{1,0},{2,3},{3,2},{4,5},{5,4},{6,7},{7,6},{8,9},{9,8},{10,11... | collective-permute-start | bytes 7077896 | tf_op jit(solution)/shard_map/ppermute | solution.py:492
  183.3 28.9 %collective-permute-start.1 = (bf16[384,1536]{1,0:T(8,128)(2,1)S(1)}, bf16[384,1536]{1,0:T(8,128)(2,1)S(1)}, u32[]{:S(2)}, u32[]{:S(2)}) collective-permute-start(bf16[384,1536]{1,0:T(8,128)(2,1)S(1)} %add_convert_fusion.1), channel_id=1, source_target_pairs={{0,16},{16,0},{1,17},{17,1},{2,18},{18,2},{3,19},{19,3},{4,20},{20... | collective-permute-start | bytes 3538952 | tf_op jit(solution)/shard_map/ppermute | solution.py:492
  186.5 50.0 %collective-permute-start.4 = (bf16[384,1536]{1,0:T(8,128)(2,1)S(1)}, bf16[384,1536]{1,0:T(8,128)(2,1)S(1)}, u32[]{:S(2)}, u32[]{:S(2)}) collective-permute-start(bf16[384,1536]{1,0:T(8,128)(2,1)S(1)} %add_convert_fusion), channel_id=1, source_target_pairs={{0,16},{16,0},{1,17},{17,1},{2,18},{18,2},{3,19},{19,3},{4,20},{20... | collective-permute-start | bytes 3538952 | tf_op jit(solution)/shard_map/ppermute | solution.py:492
  187.3 53.7 %collective-permute-start.7 = (bf16[384,896]{1,0:T(8,128)(2,1)S(1)}, bf16[384,896]{1,0:T(8,128)(2,1)S(1)}, u32[]{:S(2)}, u32[]{:S(2)}) collective-permute-start(bf16[384,896]{1,0:T(8,128)(2,1)S(1)} %add_convert_fusion.3), channel_id=1, source_target_pairs={{0,2},{1,3},{2,0},{3,1},{4,6},{5,7},{6,4},{7,5},{8,10},{9,11},{10,... | collective-permute-start | bytes 2064392 | tf_op jit(solution)/shard_map/ppermute | solution.py:492
  214.3 37.3 %collective-permute-start.2 = (bf16[192,1536]{1,0:T(8,128)(2,1)}, bf16[192,1536]{1,0:T(8,128)(2,1)}, u32[]{:S(2)}, u32[]{:S(2)}) collective-permute-start(bf16[192,1536]{1,0:T(8,128)(2,1)} %add_convert_fusion.5), channel_id=1, source_target_pairs={{0,2},{1,3},{2,0},{3,1},{4,6},{5,7},{6,4},{7,5},{8,10},{9,11},{10,... | collective-permute-start | bytes 1769480 | tf_op jit(solution)/shard_map/ppermute | solution.py:492
  239.1 15.3 %collective-permute-start.5 = (bf16[192,1536]{1,0:T(8,128)(2,1)}, bf16[192,1536]{1,0:T(8,128)(2,1)}, u32[]{:S(2)}, u32[]{:S(2)}) collective-permute-start(bf16[192,1536]{1,0:T(8,128)(2,1)} %add_convert_fusion.4), channel_id=1, source_target_pairs={{0,2},{1,3},{2,0},{3,1},{4,6},{5,7},{6,4},{7,5},{8,10},{9,11},{10,... | collective-permute-start | bytes 1769480 | tf_op jit(solution)/shard_map/ppermute | solution.py:492
  264.0 15.5 %collective-permute-start.11 = (bf16[768,384]{1,0:T(8,128)(2,1)}, bf16[768,384]{1,0:T(8,128)(2,1)S(1)}, u32[]{:S(2)}, u32[]{:S(2)}) collective-permute-start(bf16[768,384]{1,0:T(8,128)(2,1)} %get-tuple-element.83), channel_id=1, source_target_pairs={{0,1},{1,0},{2,3},{3,2},{4,5},{5,4},{6,7},{7,6},{8,9},{9,8},{10,11... | collective-permute-start | bytes 1769480 | tf_op jit(solution)/shard_map/ppermute | solution.py:492
  264.1 17.1 %collective-permute-start.14 = (bf16[768,384]{1,0:T(8,128)(2,1)}, bf16[768,384]{1,0:T(8,128)(2,1)S(1)}, u32[]{:S(2)}, u32[]{:S(2)}) collective-permute-start(bf16[768,384]{1,0:T(8,128)(2,1)} %get-tuple-element.85), channel_id=1, source_target_pairs={{0,1},{1,0},{2,3},{3,2},{4,5},{5,4},{6,7},{7,6},{8,9},{9,8},{10,11... | collective-permute-start | bytes 1769480 | tf_op jit(solution)/shard_map/ppermute | solution.py:492
  268.6 19.1 %collective-permute-start.9 = (bf16[96,3968]{1,0:T(8,128)(2,1)S(1)}, bf16[96,3968]{1,0:T(8,128)(2,1)S(1)}, u32[]{:S(2)}, u32[]{:S(2)}) collective-permute-start(bf16[96,3968]{1,0:T(8,128)(2,1)S(1)} %pad_maximum_fusion.3), channel_id=1, source_target_pairs={{0,4},{1,5},{2,6},{3,7},{4,0},{5,1},{6,2},{7,3},{8,12},{9,13},{10,... | collective-permute-start | bytes 2285576 | tf_op jit(solution)/shard_map/ppermute | solution.py:492
  287.8 22.7 %collective-permute-start.10 = (bf16[48,3968]{1,0:T(8,128)(2,1)S(1)}, bf16[48,3968]{1,0:T(8,128)(2,1)S(1)}, u32[]{:S(2)}, u32[]{:S(2)}) collective-permute-start(bf16[48,3968]{1,0:T(8,128)(2,1)S(1)} %fusion.8), channel_id=1, source_target_pairs={{0,8},{1,9},{2,10},{3,11},{4,12},{5,13},{6,14},{7,15},{8,0},{9,1},... | collective-permute-start | bytes 1142792 | tf_op jit(solution)/shard_map/ppermute | solution.py:492
  297.5 11.6 %collective-permute-start.17 = (bf16[96,768]{1,0:T(8,128)(2,1)S(1)}, bf16[96,768]{1,0:T(8,128)(2,1)S(1)}, u32[]{:S(2)}, u32[]{:S(2)}) collective-permute-start(bf16[96,768]{1,0:T(8,128)(2,1)S(1)} %pad_maximum_fusion.11), channel_id=1, source_target_pairs={{0,4},{1,5},{2,6},{3,7},{4,0},{5,1},{6,2},{7,3},{8,12},{9,13},{10,... | collective-permute-start | bytes 442376 | tf_op jit(solution)/shard_map/ppermute | solution.py:492
  342.7 11.8 %collective-permute-start.25 = (bf16[192,1536]{1,0:T(8,128)(2,1)S(1)}, bf16[192,1536]{1,0:T(8,128)(2,1)S(1)}, u32[]{:S(2)}, u32[]{:S(2)}) collective-permute-start(bf16[192,1536]{1,0:T(8,128)(2,1)S(1)} %pad_maximum_fusion.5), channel_id=1, source_target_pairs={{0,2},{1,3},{2,0},{3,1},{4,6},{5,7},{6,4},{7,5},{8,10},{9,11},{10,... | collective-permute-start | bytes 1769480 | tf_op jit(solution)/shard_map/ppermute | solution.py:492
  342.8 12.2 %collective-permute-start.26 = (bf16[192,1536]{1,0:T(8,128)(2,1)S(1)}, bf16[192,1536]{1,0:T(8,128)(2,1)S(1)}, u32[]{:S(2)}, u32[]{:S(2)}) collective-permute-start(bf16[192,1536]{1,0:T(8,128)(2,1)S(1)} %pad_maximum_fusion.6), channel_id=1, source_target_pairs={{0,4},{1,5},{2,6},{3,7},{4,0},{5,1},{6,2},{7,3},{8,12},{9,13},{10,... | collective-permute-start | bytes 1769480 | tf_op jit(solution)/shard_map/ppermute | solution.py:492
  347.2 14.9 %collective-permute-start.27 = (bf16[192,1664]{1,0:T(8,128)(2,1)S(1)}, bf16[192,1664]{1,0:T(8,128)(2,1)S(1)}, u32[]{:S(2)}, u32[]{:S(2)}) collective-permute-start(bf16[192,1664]{1,0:T(8,128)(2,1)S(1)} %pad_maximum_fusion.4), channel_id=1, source_target_pairs={{0,16},{16,0},{1,17},{17,1},{2,18},{18,2},{3,19},{19,3},{4,20},{20... | collective-permute-start | bytes 1916936 | tf_op jit(solution)/shard_map/ppermute | solution.py:492
  362.2 20.8 %collective-permute-start.28 = (bf16[384,1536]{1,0:T(8,128)(2,1)S(1)}, bf16[384,1536]{1,0:T(8,128)(2,1)}, u32[]{:S(2)}, u32[]{:S(2)}) collective-permute-start(bf16[384,1536]{1,0:T(8,128)(2,1)S(1)} %pad_maximum_fusion.1.mine), channel_id=1, source_target_pairs={{0,16},{16,0},{1,17},{17,1},{2,18},{18,2},{3,19},{19,3},{4,20},{20... | collective-permute-start | bytes 3538952 | tf_op jit(solution)/shard_map/ppermute | solution.py:492
  362.3 21.0 %collective-permute-start.35 = (bf16[384,1536]{1,0:T(8,128)(2,1)S(1)}, bf16[384,1536]{1,0:T(8,128)(2,1)S(1)}, u32[]{:S(2)}, u32[]{:S(2)}) collective-permute-start(bf16[384,1536]{1,0:T(8,128)(2,1)S(1)} %pad_maximum_fusion.2.mine), channel_id=1, source_target_pairs={{0,1},{1,0},{2,3},{3,2},{4,5},{5,4},{6,7},{7,6},{8,9},{9,8},{10,11... | collective-permute-start | bytes 3538952 | tf_op jit(solution)/shard_map/ppermute | solution.py:492
  362.3 28.9 %collective-permute-start.30 = (bf16[384,1536]{1,0:T(8,128)(2,1)S(1)}, bf16[384,1536]{1,0:T(8,128)(2,1)}, u32[]{:S(2)}, u32[]{:S(2)}) collective-permute-start(bf16[384,1536]{1,0:T(8,128)(2,1)S(1)} %pad_maximum_fusion.2.mine), channel_id=1, source_target_pairs={{0,2},{1,3},{2,0},{3,1},{4,6},{5,7},{6,4},{7,5},{8,10},{9,11},{10,... | collective-permute-start | bytes 3538952 | tf_op jit(solution)/shard_map/ppermute | solution.py:492
  364.6 30.5 %collective-permute-start.34 = (bf16[384,1536]{1,0:T(8,128)(2,1)S(1)}, bf16[384,1536]{1,0:T(8,128)(2,1)}, u32[]{:S(2)}, u32[]{:S(2)}) collective-permute-start(bf16[384,1536]{1,0:T(8,128)(2,1)S(1)} %pad_maximum_fusion.1.mine), channel_id=1, source_target_pairs={{0,1},{1,0},{2,3},{3,2},{4,5},{5,4},{6,7},{7,6},{8,9},{9,8},{10,11... | collective-permute-start | bytes 3538952 | tf_op jit(solution)/shard_map/ppermute | solution.py:492
  364.8 40.0 %collective-permute-start.36 = (bf16[384,1664]{1,0:T(8,128)(2,1)S(1)}, bf16[384,1664]{1,0:T(8,128)(2,1)}, u32[]{:S(2)}, u32[]{:S(2)}) collective-permute-start(bf16[384,1664]{1,0:T(8,128)(2,1)S(1)} %pad_maximum_fusion.mine), channel_id=1, source_target_pairs={{0,1},{1,0},{2,3},{3,2},{4,5},{5,4},{6,7},{7,6},{8,9},{9,8},{10,11... | collective-permute-start | bytes 3833864 | tf_op jit(solution)/shard_map/ppermute | solution.py:492
  383.0 21.8 %collective-permute-start.32 = (bf16[384,1664]{1,0:T(8,128)(2,1)S(1)}, bf16[384,1664]{1,0:T(8,128)(2,1)S(1)}, u32[]{:S(2)}, u32[]{:S(2)}) collective-permute-start(bf16[384,1664]{1,0:T(8,128)(2,1)S(1)} %pad_maximum_fusion.mine), channel_id=1, source_target_pairs={{0,4},{1,5},{2,6},{3,7},{4,0},{5,1},{6,2},{7,3},{8,12},{9,13},{10,... | collective-permute-start | bytes 3833864 | tf_op jit(solution)/shard_map/ppermute | solution.py:492
  383.3 25.9 %collective-permute-start.29 = (bf16[384,1536]{1,0:T(8,128)(2,1)}, bf16[384,1536]{1,0:T(8,128)(2,1)}, u32[]{:S(2)}, u32[]{:S(2)}) collective-permute-start(bf16[384,1536]{1,0:T(8,128)(2,1)} %collective-permute-done.28.refs_0_), channel_id=1, source_target_pairs={{0,1},{1,0},{2,3},{3,2},{4,5},{5,4},{6,7},{7,6},{8,9},{9,8},{10,11... | collective-permute-start | bytes 3538952 | tf_op jit(solution)/shard_map/ppermute | solution.py:492
  391.3 17.9 %collective-permute-start.31 = (bf16[384,1536]{1,0:T(8,128)(2,1)}, bf16[384,1536]{1,0:T(8,128)(2,1)}, u32[]{:S(2)}, u32[]{:S(2)}) collective-permute-start(bf16[384,1536]{1,0:T(8,128)(2,1)} %collective-permute-done.30.refs_2_), channel_id=1, source_target_pairs={{0,1},{1,0},{2,3},{3,2},{4,5},{5,4},{6,7},{7,6},{8,9},{9,8},{10,11... | collective-permute-start | bytes 3538952 | tf_op jit(solution)/shard_map/ppermute | solution.py:492
  (40 other events, 373.5 us)

commit v3 on v2

--- a/solution.py
+++ b/solution.py
@@ -30,6 +30,10 @@
     return lax.dot_general(left, right, (((0,), (0,)), ((), ())), preferred_element_type=F32)
 
 
+def as_row(vector):
+    return vector[...].astype(F32).reshape(1, vector.shape[0])
+
+
 def left_half(shape):
     return lax.broadcasted_iota(jnp.int32, shape, 1) < HEAD_DIM
 
@@ -42,26 +46,36 @@
     return pltpu.CompilerParams(vmem_limit_bytes=megabytes << 20)
 
 
-def kv_kernel(chosen, tok, w_key, w_value, b_value, order, out, blocks, sem):
+def columns_of(perm, rows):
+    local = lax.rem(perm, rows)
+    return jnp.concatenate([local, local[: 16 - HEADS]]).T
+
+
+def kv_kernel(tok, w_key, w_value, b_value, perm, chosen_in, out, blocks, chosen, chosen_sem, sem):
+    fetch = pltpu.make_async_copy(chosen_in, chosen, chosen_sem)
+    fetch.start()
     rows = tok.shape[0]
+    order = columns_of(perm[0], rows)
     per_dev = rows // CLUS
     place = lax.broadcasted_iota(jnp.int32, (rows, rows), 1)
     left = left_half((rows, 2 * HEAD_DIM))
     inputs = tok[...]
+    keys = nn(inputs, w_key[...])
+    values = nn(inputs, w_value[...]) + as_row(b_value)
+    joined = []
+    for pair in range(HEADS // 2):
+        two = slice(pair * 2 * HEAD_DIM, (pair + 1) * 2 * HEAD_DIM)
+        key_two = keys[:, two]
+        value_two = pltpu.roll(values[:, two], HEAD_DIM, 1)
+        joined.append(jnp.where(left, key_two, value_two).astype(LOW))
+        joined.append(jnp.where(left, value_two, key_two).astype(LOW))
     for quad in range(HEADS // 4):
-        four = slice(quad * 4 * HEAD_DIM, (quad + 1) * 4 * HEAD_DIM)
-        keys = nn(inputs, w_key[:, four])
-        values = nn(inputs, w_value[:, four]) + b_value[:, four].astype(F32)
-        for pair in range(2):
-            two = slice(pair * 2 * HEAD_DIM, (pair + 1) * 2 * HEAD_DIM)
-            key_two = keys[:, two]
-            value_two = pltpu.roll(values[:, two], HEAD_DIM, 1)
-            for odd in range(2):
-                head = quad * 4 + pair * 2 + odd
-                joined = jnp.where(left, value_two, key_two) if odd else jnp.where(left, key_two, value_two)
-                hot = pick(order[:, head : head + 1] == place)
-                ranked = nn(hot, joined.astype(LOW)).astype(LOW)
-                blocks[head * per_dev : (head + 1) * per_dev] = ranked.reshape(per_dev, CLUS, 2 * HEAD_DIM)
+        heads = range(quad * 4, quad * 4 + 4)
+        hot = [pick(order[:, head : head + 1] == place) for head in heads]
+        ranked = [nn(one, joined[head]).astype(LOW) for one, head in zip(hot, heads)]
+        for head, value in zip(heads, ranked):
+            blocks[head * per_dev : (head + 1) * per_dev] = value.reshape(per_dev, CLUS, 2 * HEAD_DIM)
+    fetch.wait()
     devices, capacity = chosen.shape
 
     @pl.loop(0, devices)
@@ -74,14 +88,15 @@
     pltpu.make_async_copy(out, out, sem).wait()
 
 
-def q_kernel(tok, w_query, b_query, order, out):
+def q_kernel(tok, w_query, b_query, perm, out):
     rows = tok.shape[0]
+    order = columns_of(perm[0], rows)
     place = lax.broadcasted_iota(jnp.int32, (rows, rows), 1)
     left = left_half((rows, 2 * HEAD_DIM))
     inputs = tok[...]
     for quad in range(HEADS // 4):
         four = slice(quad * 4 * HEAD_DIM, (quad + 1) * 4 * HEAD_DIM)
-        queries = nn(inputs, w_query[:, four]) + b_query[:, four].astype(F32)
+        queries = nn(inputs, w_query[:, four]) + as_row(b_query)[:, four]
         queries = (queries.astype(LOW).astype(F32) * HEAD_DIM ** (-0.5)).astype(LOW)
         for pair in range(2):
             two = queries[:, pair * 2 * HEAD_DIM : (pair + 1) * 2 * HEAD_DIM]
@@ -93,12 +108,15 @@
                 out[head] = kept.astype(LOW)
 
 
-ROW_TILE = 128
+ROW_TILE = 512
 WIDE = 768
+WIDE_FORTH = 1024
+WIDE_BACK = 1536
 
 
 def mid_kernel(
-    fetch, queries, arrived, order, inverse, tok, cot, vecs, b_up, w_out_hbm, w_up_hbm, w_down_hbm,
+    fetch, queries, arrived, order, inverse, tok, cot,
+    b_out, gain_one, shift_one, b_up, b_down, gain_two, shift_two, w_out_hbm, w_up_hbm, w_down_hbm,
     back, dq_out, attn_out, z_out, active_out, du_out, df_out, db_out, dh1_out, layer_out, sums,
     kv, probs, attn, mixed, w_out, w_up, w_down, hidden, z_full, n_one, r_one, z_low, active, slope,
     dh2, df, db, d_out, dh1, final, dq, kv_sem, w_sem, out_sem, back_sem,
@@ -139,20 +157,24 @@
     def _(group):
         span = kv.at[pl.ds(group * each, each)]
         pltpu.make_async_copy(span, span, kv_sem.at[group]).wait()
-        for odd in range(2):
-            head = 2 * group + odd
-            for cluster in range(per_dev):
-                unit = head * per_dev + cluster
-                query = queries[head, cluster * CLUS : (cluster + 1) * CLUS, :]
-                pair = kv[pl.ds(unit * PAIRS, PAIRS)].reshape(PAIRS * CLUS, pair_width)
-                scores = nt(query, pair)
-                exponent = jnp.exp(scores - jnp.max(scores, -1, keepdims=True))
-                low = (exponent / jnp.sum(exponent, -1, keepdims=True)).astype(LOW)
-                probs[unit] = low
-                mixed[odd, cluster * CLUS : (cluster + 1) * CLUS, :] = nn(low, pair).astype(LOW)
-        even = nn(pick(down == order[2 * group]), mixed[0])
-        other = nn(pick(down == order[2 * group + 1]), mixed[1])
-        both = pltpu.roll(jnp.where(left_rows, other, even), HEAD_DIM, 1)
+        units = [(odd, cluster) for odd in range(2) for cluster in range(per_dev)]
+        clusters = [slice(cluster * CLUS, (cluster + 1) * CLUS) for cluster in range(per_dev)]
+        index = [(2 * group + odd) * per_dev + cluster for odd, cluster in units]
+        pair = [kv[pl.ds(unit * PAIRS, PAIRS)].reshape(PAIRS * CLUS, pair_width) for unit in index]
+        scores = [
+            nt(queries[2 * group + odd, clusters[cluster], :], both)
+            for (odd, cluster), both in zip(units, pair)
+        ]
+        exponent = [jnp.exp(value - jnp.max(value, -1, keepdims=True)) for value in scores]
+        low = [(value / jnp.sum(value, -1, keepdims=True)).astype(LOW) for value in exponent]
+        for (odd, cluster), unit, value, both in zip(units, index, low, pair):
+            probs[unit] = value
+            value = nn(value, both)
+            mixed[odd, clusters[cluster], :] = (
+                jnp.where(left, value, 0.0) if odd else jnp.where(left, 0.0, value)
+            ).astype(LOW)
+        hot = jnp.concatenate([pick(down == order[2 * group + odd]) for odd in range(2)], axis=1)
+        both = pltpu.roll(nn(hot, mixed[...].reshape(2 * rows, pair_width)), HEAD_DIM, 1)
         attn[:, pl.ds(pl.multiple_of(group * pair_width, pair_width), pair_width)] = both.astype(LOW)
 
     store(attn, attn_out)
@@ -162,25 +184,25 @@
     @pl.loop(0, tiles)
     def _(tile):
         at = pl.ds(pl.multiple_of(tile * ROW_TILE, ROW_TILE), ROW_TILE)
-        value = hidden[at, :] + (vecs[0:1, :] + tok[at, :].astype(F32))
+        value = hidden[at, :] + (as_row(b_out) + tok[at, :].astype(F32))
         centred = value - jnp.mean(value, -1, keepdims=True)
         scale = lax.rsqrt(jnp.mean(centred * centred, -1, keepdims=True) + 1e-06)
         unit = centred * scale
-        z = unit * vecs[1:2, :] + vecs[2:3, :]
+        z = unit * as_row(gain_one) + as_row(shift_one)
         n_one[at, :] = unit
         r_one[at, :] = scale
         z_low[at, :] = z.astype(LOW)
         z_full[at, :] = z
-        hidden[at, :] = z + vecs[3:4, :]
+        hidden[at, :] = z + as_row(b_down)
 
     store(z_low, z_out)
     loads[1].wait()
     loads[2].wait()
 
-    @pl.loop(0, width // WIDE)
+    @pl.loop(0, width // WIDE_FORTH)
     def _(step):
-        at = pl.ds(pl.multiple_of(step * WIDE, WIDE), WIDE)
-        inner = nn(z_low[...], w_up[:, at]) + b_up[:, at]
+        at = pl.ds(pl.multiple_of(step * WIDE_FORTH, WIDE_FORTH), WIDE_FORTH)
+        inner = nn(z_low[...], w_up[:, at]) + b_up[at].astype(F32).reshape(1, WIDE_FORTH)
         normal = 0.5 * (1.0 + lax.erf(inner * 0.7071067811865476))
         density = jnp.exp(inner * inner * -0.5) * 0.3989422804014327
         active[:, at] = (inner * normal).astype(LOW)
@@ -197,9 +219,9 @@
         centred = value - jnp.mean(value, -1, keepdims=True)
         scale = lax.rsqrt(jnp.mean(centred * centred, -1, keepdims=True) + 1e-06)
         unit = centred * scale
-        final[at, :] = (unit * vecs[4:5, :] + vecs[5:6, :]).astype(LOW)
+        final[at, :] = (unit * as_row(gain_two) + as_row(shift_two)).astype(LOW)
         grad = cot[at, :].astype(F32)
-        lifted = grad * vecs[4:5, :]
+        lifted = grad * as_row(gain_two)
         back_grad = scale * (
             lifted - jnp.mean(lifted, -1, keepdims=True) - unit * jnp.mean(lifted * unit, -1, keepdims=True)
         )
@@ -214,13 +236,16 @@
     store(df, df_out)
     ones = jnp.ones((8, rows), LOW)
 
-    @pl.loop(0, width // WIDE)
+    @pl.loop(0, width // WIDE_BACK)
     def _(step):
-        at = pl.ds(pl.multiple_of(step * WIDE, WIDE), WIDE)
+        at = pl.ds(pl.multiple_of(step * WIDE_BACK, WIDE_BACK), WIDE_BACK)
         grad = (nt(df[...], w_down[at, :]) * slope[:, at].astype(F32)).astype(LOW)
         slope[:, at] = grad
-        sums[pl.ds(8 + step, 1), :] = nn(ones, grad)[0:1]
-        dh2[...] += nt(grad, w_up[:, at])
+        total = nn(ones, grad)
+        for part in range(WIDE_BACK // D):
+            row = 8 + step * (WIDE_BACK // D) + part
+            sums[pl.ds(row, 1), :] = total[0:1, part * D : (part + 1) * D]
+        dh2[...] += nt(slope[:, at], w_up[:, at])
 
     store(slope, du_out)
 
@@ -229,7 +254,7 @@
         at = pl.ds(pl.multiple_of(tile * ROW_TILE, ROW_TILE), ROW_TILE)
         grad = dh2[at, :]
         unit = n_one[at, :]
-        lifted = grad * vecs[1:2, :]
+        lifted = grad * as_row(gain_one)
         back_grad = r_one[at, :] * (
             lifted - jnp.mean(lifted, -1, keepdims=True) - unit * jnp.mean(lifted * unit, -1, keepdims=True)
         )
@@ -248,33 +273,36 @@
     def _(group):
         lanes = pl.ds(pl.multiple_of(group * pair_width, pair_width), pair_width)
         tile = d_out[:, lanes]
-        bias = []
+        grads = []
+        for odd in range(2):
+            turned = pltpu.roll(nn(pick(down == inverse[2 * group + odd]), tile), HEAD_DIM, 1)
+            grads.append((jnp.where(left_rows, turned, 0.0) if odd else jnp.where(left_rows, 0.0, turned)).astype(LOW))
+        units = [(odd, cluster) for odd in range(2) for cluster in range(per_dev)]
+        clusters = [slice(cluster * CLUS, (cluster + 1) * CLUS) for cluster in range(per_dev)]
+        index = [(2 * group + odd) * per_dev + cluster for odd, cluster in units]
+        grad = [grads[odd][clusters[cluster]] for odd, cluster in units]
+        query = [queries[2 * group + odd, clusters[cluster], :] for odd, cluster in units]
+        pair = [kv[pl.ds(unit * PAIRS, PAIRS)].reshape(PAIRS * CLUS, pair_width) for unit in index]
+        low = [probs[unit] for unit in index]
+        d_probs = [nt(left_, right) for left_, right in zip(grad, pair)]
+        wide = [value.astype(F32) for value in low]
+        d_scores = [
+            (value * (grad_ - jnp.sum(grad_ * value, -1, keepdims=True))).astype(LOW)
+            for value, grad_ in zip(wide, d_probs)
+        ]
+        d_query = [nn(left_, right) * HEAD_DIM ** (-0.5) for left_, right in zip(d_scores, pair)]
+        d_pair = [tn(a, b) + tn(c, d) for a, b, c, d in zip(d_scores, query, low, grad)]
+        bias = [jnp.zeros((1, pair_width), F32)] * 2
         q_total = jnp.zeros((1, pair_width), F32)
-        for odd in range(2):
-            head = 2 * group + odd
-            turned = pltpu.roll(nn(pick(down == inverse[head]), tile), HEAD_DIM, 1)
-            grads = (jnp.where(left_rows, turned, 0.0) if odd else jnp.where(left_rows, 0.0, turned)).astype(LOW)
-            total = jnp.zeros((1, pair_width), F32)
-            for cluster in range(per_dev):
-                unit = head * per_dev + cluster
-                query = queries[head, cluster * CLUS : (cluster + 1) * CLUS, :]
-                grad = grads[cluster * CLUS : (cluster + 1) * CLUS]
-                pair = kv[pl.ds(unit * PAIRS, PAIRS)].reshape(PAIRS * CLUS, pair_width)
-                low = probs[unit]
-                wide = low.astype(F32)
-                d_probs = nt(grad, pair)
-                d_scores = (wide * (d_probs - jnp.sum(d_probs * wide, -1, keepdims=True))).astype(LOW)
-                d_query = nn(d_scores, pair) * HEAD_DIM ** (-0.5)
-                d_query = (jnp.where(left, 0.0, d_query) if odd else jnp.where(left, d_query, 0.0)).astype(LOW)
-                dq[head, cluster * CLUS : (cluster + 1) * CLUS, :] = d_query
-                q_total += jnp.sum(d_query.astype(F32), axis=0, keepdims=True)
-                d_pair = tn(d_scores, query) + tn(low, grad)
-                total += jnp.sum(d_pair, axis=0, keepdims=True)
-                kv[pl.ds(unit * PAIRS, PAIRS)] = d_pair.astype(LOW).reshape(PAIRS, CLUS, pair_width)
-                for part in range(PAIRS):
-                    entry = unit * PAIRS + part
-                    pltpu.make_async_copy(kv.at[entry], back.at[fetch[entry]], back_sem).start()
-            bias.append(total)
+        for (odd, cluster), unit, value, both in zip(units, index, d_query, d_pair):
+            value = (jnp.where(left, 0.0, value) if odd else jnp.where(left, value, 0.0)).astype(LOW)
+            dq[2 * group + odd, clusters[cluster], :] = value
+            q_total += jnp.sum(value.astype(F32), axis=0, keepdims=True)
+            bias[odd] += jnp.sum(both, axis=0, keepdims=True)
+            kv[pl.ds(unit * PAIRS, PAIRS)] = both.astype(LOW).reshape(PAIRS, CLUS, pair_width)
+        for step in range(each):
+            entry = group * each + step
+            pltpu.make_async_copy(kv.at[entry], back.at[fetch[entry]], back_sem).start()
         both = jnp.where(left_half((1, pair_width)), bias[1], bias[0])
         sums[7:8, lanes] = q_total
         sums[6:7, lanes] = pltpu.roll(jnp.broadcast_to(both, (8, pair_width)), HEAD_DIM, 1)[0:1]
@@ -315,14 +343,8 @@
     half = keep.shape[1]
     turned[...] = z_low[...].T
     for side, out in ((0, give), (1, keep)):
-        base = core_of(info, side) * half
-
-        @pl.loop(0, half // WIDE)
-        def _(step):
-            at = pl.ds(pl.multiple_of(base + step * WIDE, WIDE), WIDE)
-            to = pl.ds(pl.multiple_of(step * WIDE, WIDE), WIDE)
-            buf[side, :, to] = nn(turned[...], grad[:, at]).astype(LOW)
-
+        at = pl.ds(pl.multiple_of(core_of(info, side) * half, half), half)
+        buf[side] = nn(turned[...], grad[:, at]).astype(LOW)
         place_chunks(buf.at[side], out, info, sem.at[side])
     for side, out in ((0, give), (1, keep)):
         wait_chunks(buf.at[side], out, sem.at[side])
@@ -378,20 +400,24 @@
     left = left_half((rows, pair_width))
     total[...] = jnp.zeros_like(total)
 
-    @pl.loop(0, segment.shape[0])
+    @pl.loop(0, segment.shape[0], unroll=4)
     def _(slot):
         block = segment[slot]
         total[block] += returned[slot].astype(F32)
 
-    for pair in range(HEADS // 2):
-        placed = []
-        for head in (2 * pair, 2 * pair + 1):
-            summed = total[head * per_dev : (head + 1) * per_dev].reshape(rows, pair_width)
-            placed.append(nn(pick(down == order[head]), summed.astype(LOW)))
-        even, odd = placed
-        grad_kv[:, pair * pair_width : (pair + 1) * pair_width] = jnp.where(left, even, odd).astype(LOW)
-        values = pltpu.roll(jnp.where(left, odd, even), HEAD_DIM, 1)
-        grad_kv[:, D + pair * pair_width : D + (pair + 1) * pair_width] = values.astype(LOW)
+    for quad in range(HEADS // 4):
+        pairs = range(2 * quad, 2 * quad + 2)
+        heads = range(4 * quad, 4 * quad + 4)
+        hots = [pick(down == order[head]) for head in heads]
+        summed = [
+            total[head * per_dev : (head + 1) * per_dev].reshape(rows, pair_width).astype(LOW) for head in heads
+        ]
+        placed = [nn(hot, value) for hot, value in zip(hots, summed)]
+        for at, pair in enumerate(pairs):
+            even, odd = placed[2 * at], placed[2 * at + 1]
+            grad_kv[:, pair * pair_width : (pair + 1) * pair_width] = jnp.where(left, even, odd).astype(LOW)
+            values = pltpu.roll(jnp.where(left, odd, even), HEAD_DIM, 1)
+            grad_kv[:, D + pair * pair_width : D + (pair + 1) * pair_width] = values.astype(LOW)
     tok_t[...] = tok[...].T
     outs = ((key_give, key_keep), (value_give, value_keep))
     for side in range(2):
@@ -537,32 +563,21 @@
     return total
 
 
-def scatter_start(terms, bits):
-    rows = terms[-1].shape[0]
+def to_send(terms):
+    rows = min(term.shape[0] for term in terms)
+    return sum_rows(terms, rows // 2, rows).astype(LOW)
+
+
+def scatter_steps(terms, bits):
     for bit in bits:
-        if len(terms) > 2:
-            rows = terms[-1].shape[0]
-        terms = terms + [swap(sum_rows(terms, rows // 2, rows).astype(LOW), bit)]
-        rows //= 2
+        terms = terms + [swap(to_send(terms), bit)]
     return terms
 
 
-def scatter_end(sets, bits, further):
-    rows = sets[0][-1].shape[0]
-    more = []
-
-    def total(low, high):
-        value = jnp.concatenate([sum_rows(terms, low, high) for terms in sets], axis=1)
-        for term in more:
-            value = value + term[low:high].astype(F32)
-        return value.astype(LOW)
-
-    for bit in bits:
-        more.append(swap(total(rows // 2, rows), bit))
-        rows //= 2
-    value = total(0, rows)
+def finish(terms, further):
+    value = sum_rows(terms, 0, terms[-1].shape[0]).astype(LOW)
     for bit in further:
-        value = sum_rows([value, swap(value, bit)], 0, rows).astype(LOW)
+        value = sum_rows([value, swap(value, bit)], 0, value.shape[0]).astype(LOW)
     return value
 
 
@@ -570,12 +585,8 @@
     return lax.optimization_barrier(tuple(values))
 
 
-def gather_rows(values, orders):
-    for step in range(len(orders[0]) - 1):
-        values = tie(
-            jnp.concatenate([value, swap(value, order[step])]) for value, order in zip(values, orders)
-        )
-    return values
+def gather_step(value, bit):
+    return jnp.concatenate([value, swap(value, bit)])
 
 
 def per_device(
@@ -608,7 +619,6 @@
     pair_width = 2 * HEAD_DIM
     ff = w_up.shape[1]
     local_order = cluster_perm[0] - my_index * rows
-    order_cols = local_order.T
     order_rows = local_order[:, None, :]
 
     wanted = (
@@ -640,12 +650,17 @@
         kv_kernel,
         grid=(1,),
         out_shape=jax.ShapeDtypeStruct((slots, CLUS, pair_width), LOW),
-        in_specs=[smem, vmem, column_block(1), column_block(2), vmem, vmem],
+        in_specs=[vmem, column_block(1), column_block(2), vmem, vmem, vmem],
         out_specs=hbm,
-        scratch_shapes=[pltpu.VMEM((blocks, CLUS, pair_width), LOW), pltpu.SemaphoreType.DMA],
+        scratch_shapes=[
+            pltpu.VMEM((blocks, CLUS, pair_width), LOW),
+            pltpu.SMEM(chosen.shape, jnp.int32),
+            pltpu.SemaphoreType.DMA,
+            pltpu.SemaphoreType.DMA,
+        ],
         compiler_params=params(),
         name="kv_kernel",
-    )(chosen, tokens, w_qkv, w_qkv, b_value[None], order_cols)
+    )(tokens, w_qkv, w_qkv, b_value, cluster_perm, chosen)
     arrived = lax.all_to_all(
         outgoing.reshape(count_blk, capacity, CLUS, pair_width),
         "blk",
@@ -663,7 +678,7 @@
         out_specs=vmem,
         compiler_params=params(),
         name="q_kernel",
-    )(tokens, w_qkv, b_query[None], order_cols)
+    )(tokens, w_qkv, b_query, cluster_perm)
     filled = jnp.any(matches, axis=1)
     segment = jnp.where(filled, chosen, blocks).reshape(-1)
     my_source = lax.dynamic_index_in_dim(wanted, my_index, 0, keepdims=False) // per_dev
@@ -673,10 +688,6 @@
     inverse = jnp.sum(
         jnp.where(local_order[:, :, None] == places, places[None, :, None], 0), axis=1
     )[:, None, :]
-    vecs = jnp.stack(
-        [b_out, gain_one, shift_one, b_down, gain_two, shift_two, b_down, b_down]
-    ).astype(F32)
-
     def low(*shape):
         return jax.ShapeDtypeStruct(shape, LOW)
 
@@ -693,7 +704,7 @@
             low(rows, ff), low(rows, ff), low(rows, D), low(rows, D), full(rows, D), low(rows, D),
             full(16, D),
         ),
-        in_specs=[smem, vmem, hbm, vmem, vmem, vmem, vmem, vmem, vmem, hbm, hbm, hbm],
+        in_specs=[smem, vmem, hbm] + [vmem] * 11 + [hbm] * 3,
         out_specs=(hbm,) * 10 + (vmem,),
         scratch_shapes=[
             pltpu.VMEM((requests, CLUS, pair_width), LOW),
@@ -725,8 +736,8 @@
         compiler_params=params(),
         name="mid_kernel",
     )(
-        fetch, queries, arrived, order_rows, inverse, tokens, cotangent, vecs,
-        b_up[None].astype(F32), w_out, w_up, w_down,
+        fetch, queries, arrived, order_rows, inverse, tokens, cotangent,
+        b_out, gain_one, shift_one, b_up, b_down, gain_two, shift_two, w_out, w_up, w_down,
     )
     returned = lax.all_to_all(
         back.reshape(count_blk, capacity, CLUS, pair_width),
@@ -767,11 +778,16 @@
         (low(rows, D),),
         name="out_q_kernel",
     )
-    up = scatter_start([up_keep, swap(up_give, CORE)], (X, Y))
-    down = scatter_start([down_keep, swap(down_give, CORE)], (X, Y))
-    out_q = scatter_start([oq_keep, swap(oq_give, CORE)], (Y, X))
-
-    returned, up[-1], down[-1], out_q[-1] = tie((returned, up[-1], down[-1], out_q[-1]))
+    up = scatter_steps([up_keep, swap(up_give, CORE)], (X, Y))
+    down = scatter_steps([down_keep, swap(down_give, CORE)], (X,))
+    out_q = scatter_steps([oq_keep, swap(oq_give, CORE)], (Y, X))
+    up_step = to_send(up)
+    up_step, down[-1] = tie((up_step, down[-1]))
+    down_step = to_send(down)
+
+    returned, up_step, down_step, out_q[-1] = tie((returned, up_step, down_step, out_q[-1]))
+    up = up + [swap(up_step, Z0)]
+    down = down + [swap(down_step, Y)]
     key_give, key_keep, value_give, value_keep, grad_kv = pl.pallas_call(
         key_value_kernel,
         out_shape=(low(D, half),) * 4 + (low(rows, 2 * D),),
@@ -786,17 +802,26 @@
         compiler_params=params(),
         name="key_value_kernel",
     )(info, segment, returned, order_rows, tokens)
-    key = scatter_start([key_keep, swap(key_give, CORE)], (X, Y))
-    value = scatter_start([value_keep, swap(value_give, CORE)], (Y, X))
-    early = scatter_end([up, down, out_q], (Z0, Z1), further)
-    late = scatter_end([key, value], (Z0, Z1), further)
-    grad_proj = jnp.concatenate([grad_q, grad_kv], axis=1)
-    grad_tokens = (grad_resid + nt(grad_proj, w_qkv)).astype(LOW)
-    early, late, grad_tokens = tie((early, late, grad_tokens))
-    wide = ff // 2
-    up = early[:, :wide]
-    down = early[:, wide : 2 * wide]
-    rest = jnp.concatenate([early[:, 2 * wide :], late], axis=1)
+    down[-1], key_give, value_give = tie((down[-1], key_give, value_give))
+    key = scatter_steps([key_keep, swap(key_give, CORE)], (X, Y))
+    value = scatter_steps([value_keep, swap(value_give, CORE)], (Y, X))
+    up = finish(scatter_steps(up, (Z1,)), further)
+    down = finish(scatter_steps(down, (Z0, Z1)), further)
+    out_q = finish(scatter_steps(out_q, (Z0, Z1)), further)
+    late_given = swap(jnp.concatenate([to_send(key), to_send(value)], axis=1), Z0)
+    key = key + [late_given[:, :half]]
+    value = value + [late_given[:, half:]]
+    late_given = swap(jnp.concatenate([to_send(key), to_send(value)], axis=1), Z1)
+    key = finish(key + [late_given[:, :half]], further)
+    value = finish(value + [late_given[:, half:]], further)
+    thirds = [
+        gather_step(third, Z1)
+        for third in (
+            up,
+            down,
+            jnp.concatenate([out_q, key, value], axis=1),
+        )
+    ]
 
     def spread_call(start, route, mine, other, outs):
         count = len(outs)
@@ -815,9 +840,13 @@
         )(info, mine, other)
 
     orders = (ORDER_X, ORDER_Y, ORDER_Z)
-    mine = gather_rows((up, down, rest), orders)
-    last = [swap(value, order[-1]) for value, order in zip(mine, orders)]
-    other = [swap(value, CORE) for value in mine]
+    for step in (1, 2):
+        thirds = tie(gather_step(value, order[step]) for value, order in zip(thirds, orders))
+    grad_kv, *thirds = tie((grad_kv, *thirds))
+    grad_proj = jnp.concatenate([grad_q, grad_kv], axis=1)
+    grad_tokens = (grad_resid + nt(grad_proj, w_qkv)).astype(LOW)
+    last = [swap(value, order[-1]) for value, order in zip(thirds, orders)]
+    other = [swap(value, CORE) for value in thirds]
     outs = []
     for at, (start, route, shapes) in enumerate(
         (
@@ -826,7 +855,9 @@
             (49, attention_targets, (full(D, D), full(D, 3 * D), full(CHUNKS, 8, LANES))),
         )
     ):
-        outs += spread_call(start, route, mine[at], other[at], shapes)
+        outs += spread_call(start, route, thirds[at], other[at], shapes)
+    tied = tie((*last, *outs))
+    last, outs = tied[: len(last)], tied[len(last) :]
     last_pieces = []
     for value in last:
         last_pieces += [value, swap(value, CORE)]

time: 428 us -> 385 us (0.90)
  waiting for transfers between devices: 202 us -> 174 us
  Pallas kernels: 114 us -> 98.2 us
  other arithmetic: 24.2 us -> 31.9 us
    ppermute x37 -> x41, waiting for transfers between devices: 146 us -> 115 us  [swap(): return lax.ppermute(value, axis, [(i, i ^ distance) for i in range(size)])]
    pallas_call x1, Pallas kernels: 51.2 us -> 37.3 us  [per_device(): pl.pallas_call(mid_kernel, out_shape=(low(slots, CLUS, pair_width), low(H...]
    convert_element_type x16 -> x23, other arithmetic: 10.8 us -> 23.5 us  [the longest x19 19.9 us: to_send(): return sum_rows(terms, rows // 2, rows).astype(LOW)]
    ppermute x37 -> x41, starting transfers between devices: 36.9 us -> 34.7 us  [swap(): return lax.ppermute(value, axis, [(i, i ^ distance) for i in range(size)])]
  transfers between devices with their start and end apart: 39 -> 43, of which waited for: 21 -> 24; matrix products, arithmetic and copies ran while one was open for 7% -> 9% of each run, Pallas kernels for 9% -> 12%
where the time goes in v3:
time: 385 us; the launch traced here: 381 us
  waiting for transfers between devices  174 us (45%)
  Pallas kernels  98.2 us (26%)
  starting transfers between devices  59.9 us (16%)
  other arithmetic  31.9 us (8%)
  local copies, waits for them, and re-layouts  10.1 us (3%)
  matrix products  5.03 us (1%)
    ppermute x41, waiting for transfers between devices, swap(): return lax.ppermute(value, axis, [(i, i ^ distance) for i in range(size)])  115 us
    all_to_all x1, waiting for transfers between devices, per_device(): lax.all_to_all(outgoing.reshape(count_blk, capacity, CLUS, pair_width), '...  58.8 us
    pallas_call x1, Pallas kernels, per_device(): pl.pallas_call(mid_kernel, out_shape=(low(slots, CLUS, pair_width), low(H...  37.3 us
    ppermute x41, starting transfers between devices, swap(): return lax.ppermute(value, axis, [(i, i ^ distance) for i in range(size)])  34.7 us
    convert_element_type x19, other arithmetic, to_send(): return sum_rows(terms, rows // 2, rows).astype(LOW)  19.9 us
    pallas_call x3, Pallas kernels, halves(): pl.pallas_call(kernel, out_shape=(low(D, columns), low(D, columns)) + mor...  19.8 us
    all_to_all x1, starting transfers between devices, per_device(): lax.all_to_all(back.reshape(count_blk, capacity, CLUS, pair_width), 'blk'...  17.6 us
    pallas_call x3, Pallas kernels, spread_call(): pl.pallas_call(partial(spread_kernel, start, route, count), out_shape=out...  11.7 us
  transfers between devices with their start and end apart: 43, of which 24 were waited for; matrix products, arithmetic and copies ran while one was open for 9% of the time, Pallas kernels for 12%

profile of v3, /device:TPU:0, one launch (start us, length us, event | category | flops | bytes accessed | tf_op | source)
XLA Modules:
  0.0 380.9 jit_solution(13683153819265242775)
XLA Ops:
  4.3 6.9 %kv_kernel.1 = bf16[112,128,128]{2,1,0:T(8,128)(2,1)} custom-call(bf16[512,768]{1,0:T(8,128)(2,1)} %tok.9, bf16[768,2304]{1,0:T(8,128)(2,1)} %w_value.1, bf16[768,2304]{1,0:T(8,128)(2,1)} %w_value.1, bf16[768]{0:T(1024)(128)(2,1)} %b_value.1, s32[1,12,512]{2,1,0:T(8,128)} %copy.65.perm, s32[16,7]{1,0:T(8,128)} %copy.71.chosen_in), custom_call_target="tpu_custom_call" | custom-call | tf_op jit(solution)/shard_map/kv_kernel/pallas_call | solution.py:649
  11.2 7.6 %all-to-all-start = ((bf16[16,7,128,128]{3,2,1,0:T(8,128)(2,1)}), bf16[16,7,128,128]{3,2,1,0:T(8,128)(2,1)}, u32[]{:S(2)}, u32[]{:S(2)}) async-start(bf16[16,7,128,128]{3,2,1,0:T(8,128)(2,1)} %bitcast.32), calls=%async_computation | async-start | bytes 7340032 | tf_op jit(solution)/shard_map/all_to_all | solution.py:664
  21.4 5.7 %q_kernel.1.queries = bf16[12,512,128]{2,1,0:T(8,128)(2,1)} custom-call(bf16[512,768]{1,0:T(8,128)(2,1)} %tok.9, bf16[768,2304]{1,0:T(8,128)(2,1)} %w_value.1, bf16[768]{0:T(1024)(128)(2,1)} %b_query.1, s32[1,12,512]{2,1,0:T(8,128)} %copy.65.perm), custom_call_target="tpu_custom_call" | custom-call | tf_op jit(solution)/shard_map/q_kernel/pallas_call | solution.py:673
  28.6 58.8 %all-to-all-done = bf16[16,7,128,128]{3,2,1,0:T(8,128)(2,1)} async-done(((bf16[16,7,128,128]{3,2,1,0:T(8,128)(2,1)}), bf16[16,7,128,128]{3,2,1,0:T(8,128)(2,1)}, u32[]{:S(2)}, u32[]{:S(2)}) %all-to-all-start) | async-done | bytes 3670048 | tf_op jit(solution)/shard_map/all_to_all | solution.py:664
  87.4 37.3 %mid_kernel.1 = (bf16[112,128,128]{2,1,0:T(8,128)(2,1)}, bf16[12,512,128]{2,1,0:T(8,128)(2,1)}, bf16[512,768]{1,0:T(8,128)(2,1)}, bf16[512,768]{1,0:T(8,128)(2,1...) custom-call(s32[96]{0:T(128)} %multiply_add_fusion.fetch, ...), custom_call_target="tpu_custom_call" | custom-call | tf_op jit(solution)/shard_map/mid_kernel/pallas_call | solution.py:700
  124.8 17.6 %all-to-all-start.1 = ((bf16[16,7,128,128]{3,2,1,0:T(8,128)(2,1)}), bf16[16,7,128,128]{3,2,1,0:T(8,128)(2,1)}, u32[]{:S(2)}, u32[]{:S(2)}) async-start(bf16[16,7,128,128]{3,2,1,0:T(8,128)(2,1)} %bitcast.34), calls=%async_computation.1 | async-start | bytes 7340032 | tf_op jit(solution)/shard_map/all_to_all | solution.py:742
  143.1 6.2 %up_kernel.1 = (bf16[768,1536]{1,0:T(8,128)(2,1)}, bf16[768,1536]{1,0:T(8,128)(2,1)}) custom-call(s32[81]{0:T(128)} %concatenate.45.info, bf16[512,768]{1,0:T(8,128)(2,1)} %get-tuple-element.81.z_low, bf16[512,3072]{1,0:T(8,128)(2,1)} %get-tuple-element.82.grad), custom_call_target="tpu_custom_call" | custom-call | flops 1 | bytes 1 | tf_op jit(solution)/shard_map/up_kernel/pallas_call | solution.py:753
  149.6 6.2 %down_kernel.1 = (bf16[768,1536]{1,0:T(8,128)(2,1)}, bf16[768,1536]{1,0:T(8,128)(2,1)}) custom-call(s32[81]{0:T(128)} %concatenate.45.info, bf16[512,3072]{1,0:T(8,128)(2,1)} %get-tuple-element.85.active, bf16[512,768]{1,0:T(8,128)(2,1)} %get-tuple-element.86.grad), custom_call_target="tpu_custom_call" | custom-call | flops 1 | bytes 1 | tf_op jit(solution)/shard_map/down_kernel/pallas_call | solution.py:753
  156.1 7.5 %out_q_kernel.1 = (bf16[768,896]{1,0:T(8,128)(2,1)}, bf16[768,896]{1,0:T(8,128)(2,1)}, bf16[512,768]{1,0:T(8,128)(2,1)}) custom-call(s32[81]{0:T(128)} %concatenate.45.info, bf16[512,768]{1,0:T(8,128)(2,1)} %get-tuple-element.75.attn, bf16[512,768]{1,0:T(8,128)(2,1)} %get-tuple-element.76.db, bf16[512,768]{1,0:T(8,128)(2,1)} %tok.9, ...), custom_call_target="tpu_custom_call" | custom-call | flops 1 | bytes 1 | tf_op jit(solution)/shard_map/out_q_kernel/pallas_call | solution.py:753
  174.6 21.6 %collective-permute-done.1 = bf16[384,1536]{1,0:T(8,128)(2,1)S(1)} collective-permute-done((bf16[384,1536]{1,0:T(8,128)(2,1)S(1)}, bf16[384,1536]{1,0:T(8,128)(2,1)S(1)}, u32[]{:S(2)}, u32[]{:S(2)}) %collective-permute-start.1) | collective-permute-done | bytes 1179680 | tf_op jit(solution)/shard_map/ppermute | solution.py:518
  203.5 18.6 %collective-permute-done.2 = bf16[192,1536]{1,0:T(8,128)(2,1)S(1)} collective-permute-done((bf16[192,1536]{1,0:T(8,128)(2,1)S(1)}, bf16[192,1536]{1,0:T(8,128)(2,1)S(1)}, u32[]{:S(2)}, u32[]{:S(2)}) %collective-permute-start.2) | collective-permute-done | bytes 589856 | tf_op jit(solution)/shard_map/ppermute | solution.py:518
  234.8 9.3 %key_value_kernel.1 = (bf16[768,384]{1,0:T(8,128)(2,1)}, bf16[768,384]{1,0:T(8,128)(2,1)}, bf16[768,384]{1,0:T(8,128)(2,1)}, bf16[768,384]{1,0:T(8,128)(2,1)}, bf16[512,1536]{1,0:T(8,128)(2,1)}) custom-call(s32[81]{0:T(128)} %concatenate.45.info, s32[112]{0:T(128)} %select_n.216.segment, bf16[112,128,128]{2,1,0:T(8,128)(2,1)} %bitcast.8.returned, ...), custom_call_target="tpu_custom_call" | custom-call | tf_op jit(solution)/shard_map/key_value_kernel/pallas_call | solution.py:791
  252.0 6.0 %collective-permute-done.9 = bf16[48,1536]{1,0:T(8,128)(2,1)S(1)} collective-permute-done((bf16[48,1536]{1,0:T(8,128)(2,1)S(1)}, bf16[48,1536]{1,0:T(8,128)(2,1)S(1)}, u32[]{:S(2)}, u32[]{:S(2)}) %collective-permute-start.9) | collective-permute-done | bytes 147488 | tf_op jit(solution)/shard_map/ppermute | solution.py:518
  269.0 4.3 %collective-permute-done.20 = bf16[384,384]{1,0:T(8,128)(2,1)S(1)} collective-permute-done((bf16[384,384]{1,0:T(8,128)(2,1)S(1)}, bf16[384,384]{1,0:T(8,128)(2,1)S(1)}, u32[]{:S(2)}, u32[]{:S(2)}) %collective-permute-start.20) | collective-permute-done | bytes 294944 | tf_op jit(solution)/shard_map/ppermute | solution.py:518
  286.5 9.0 %collective-permute-done.14 = bf16[48,1536]{1,0:T(8,128)(2,1)S(1)} collective-permute-done((bf16[48,1536]{1,0:T(8,128)(2,1)S(1)}, bf16[48,1536]{1,0:T(8,128)(2,1)S(1)}, u32[]{:S(2)}, u32[]{:S(2)}) %collective-permute-start.14) | collective-permute-done | bytes 147488 | tf_op jit(solution)/shard_map/ppermute | solution.py:518
  299.8 4.5 %collective-permute-done.15 = bf16[48,1536]{1,0:T(8,128)(2,1)S(1)} collective-permute-done((bf16[48,1536]{1,0:T(8,128)(2,1)S(1)}, bf16[48,1536]{1,0:T(8,128)(2,1)S(1)}, u32[]{:S(2)}, u32[]{:S(2)}) %collective-permute-start.15) | collective-permute-done | bytes 147488 | tf_op jit(solution)/shard_map/ppermute | solution.py:518
  306.9 4.1 %collective-permute-done.16 = bf16[96,1536]{1,0:T(8,128)(2,1)S(1)} collective-permute-done((bf16[96,1536]{1,0:T(8,128)(2,1)S(1)}, bf16[96,1536]{1,0:T(8,128)(2,1)S(1)}, u32[]{:S(2)}, u32[]{:S(2)}) %collective-permute-start.16) | collective-permute-done | bytes 294944 | tf_op jit(solution)/shard_map/ppermute | solution.py:518
  316.8 9.6 %collective-permute-done.29 = bf16[192,1536]{1,0:T(8,128)(2,1)S(1)} collective-permute-done((bf16[192,1536]{1,0:T(8,128)(2,1)S(1)}, bf16[192,1536]{1,0:T(8,128)(2,1)S(1)}, u32[]{:S(2)}, u32[]{:S(2)}) %collective-permute-start.29) | collective-permute-done | bytes 589856 | tf_op jit(solution)/shard_map/ppermute | solution.py:518
  334.4 3.8 %down_targets.1.refs_7_ = f32[4,768,768]{2,1,0:T(8,128)} custom-call(s32[81]{0:T(128)} %concatenate.45.info, bf16[384,1536]{1,0:T(8,128)(2,1)} %pad_maximum_fusion.2.mine, bf16[384,1536]{1,0:T(8,128)(2,1)} %copy-done.12), custom_call_target="tpu_custom_call" | custom-call | flops 20000000000 | bytes 20000000 | tf_op jit(solution)/shard_map/down_targets/pallas_call | solution.py:828
  339.3 3.8 %up_targets.1.refs_6_ = f32[768,3072]{1,0:T(8,128)} custom-call(s32[81]{0:T(128)} %concatenate.45.info, bf16[384,1536]{1,0:T(8,128)(2,1)} %pad_maximum_fusion.1.mine, bf16[384,1536]{1,0:T(8,128)(2,1)} %copy-done.11), custom_call_target="tpu_custom_call" | custom-call | flops 20000000000 | bytes 20000000 | tf_op jit(solution)/shard_map/up_targets/pallas_call | solution.py:828
  343.1 4.1 %attention_targets.1 = (f32[768,768]{1,0:T(8,128)}, f32[768,2304]{1,0:T(8,128)}, f32[16,8,128]{2,1,0:T(8,128)}) custom-call(s32[81]{0:T(128)} %concatenate.45.info, bf16[384,1664]{1,0:T(8,128)(2,1)} %pad_maximum_fusion.mine, bf16[384,1664]{1,0:T(8,128)(2,1)} %collective-permute-done.37.other), custom_call_target="tpu_custom_call" | custom-call | flops 20000000000 | bytes 20000000 | tf_op jit(solution)/shard_map/attention_targets/pallas_call | solution.py:828
  347.2 11.4 %collective-permute-done.32.refs_0_ = bf16[384,1536]{1,0:T(8,128)(2,1)} collective-permute-done((bf16[384,1536]{1,0:T(8,128)(2,1)}, bf16[384,1536]{1,0:T(8,128)(2,1)}, u32[]{:S(2)}, u32[]{:S(2)}) %collective-permute-start.32) | collective-permute-done | bytes 1179680 | tf_op jit(solution)/shard_map/ppermute | solution.py:518
  364.2 5.0 %add_convert_fusion.2 = bf16[512,768]{1,0:T(8,128)(2,1)} fusion(f32[512,768]{1,0:T(8,128)} %get-tuple-element.74, bf16[768,2304]{1,0:T(8,128)(2,1)S(1)} %copy-done, bf16[512,1536]{1,0:T(8,128)(2,1)} %get-tuple-element.111, bf16[512,768]{1,0:T(8,128)(2,1)} %get-tuple-element.79), kind=kOutput, calls=%fused_computation.8 | convolution fusion | flops 1817444352 | bytes 8257536 | tf_op jit(solution)/shard_map/dot_general | solution.py:26
  370.4 7.4 %spread_last.1 = (f32[768,3072]{1,0:T(8,128)}, f32[4,768,768]{2,1,0:T(8,128)}, f32[768,768]{1,0:T(8,128)}, f32[768,2304]{1,0:T(8,128)}, f32[16,8,128]{2,1,0:T(8,128)}) custom-call(s32[81]{0:T(128)} %concatenate.45.info, ...), custom_call_target="tpu_custom_call", output_to_operand_aliasing={{0}: (7, {}), {1}: (8, {}), {2}: (9, {}), {3}: (10, {}), {4... | custom-call | tf_op jit(solution)/shard_map/spread_last/pallas_call | solution.py:864
  (170 shorter events, 102.7 us)
Async XLA Ops:
  11.2 76.2 %all-to-all-start = ((bf16[16,7,128,128]{3,2,1,0:T(8,128)(2,1)}), bf16[16,7,128,128]{3,2,1,0:T(8,128)(2,1)}, u32[]{:S(2)}, u32[]{:S(2)}) async-start(bf16[16,7,128,128]{3,2,1,0:T(8,128)(2,1)} %bitcast.32), calls=%async_computation | async-start | bytes 7340032 | tf_op jit(solution)/shard_map/all_to_all | solution.py:664
  124.8 103.5 %all-to-all-start.1 = ((bf16[16,7,128,128]{3,2,1,0:T(8,128)(2,1)}), bf16[16,7,128,128]{3,2,1,0:T(8,128)(2,1)}, u32[]{:S(2)}, u32[]{:S(2)}) async-start(bf16[16,7,128,128]{3,2,1,0:T(8,128)(2,1)} %bitcast.34), calls=%async_computation.1 | async-start | bytes 7340032 | tf_op jit(solution)/shard_map/all_to_all | solution.py:742
  149.3 14.6 %collective-permute-start = (bf16[768,1536]{1,0:T(8,128)(2,1)}, bf16[768,1536]{1,0:T(8,128)(2,1)S(1)}, u32[]{:S(2)}, u32[]{:S(2)}) collective-permute-start(bf16[768,1536]{1,0:T(8,128)(2,1)} %get-tuple-element.84), channel_id=1, source_target_pairs={{0,1},{1,0},{2,3},{3,2},{4,5},{5,4},{6,7},{7,6},{8,9},{9,8},{10,11... | collective-permute-start | bytes 7077896 | tf_op jit(solution)/shard_map/ppermute | solution.py:518
  155.8 16.7 %collective-permute-start.3 = (bf16[768,1536]{1,0:T(8,128)(2,1)}, bf16[768,1536]{1,0:T(8,128)(2,1)}, u32[]{:S(2)}, u32[]{:S(2)}) collective-permute-start(bf16[768,1536]{1,0:T(8,128)(2,1)} %get-tuple-element.88), channel_id=1, source_target_pairs={{0,1},{1,0},{2,3},{3,2},{4,5},{5,4},{6,7},{7,6},{8,9},{9,8},{10,11... | collective-permute-start | bytes 7077896 | tf_op jit(solution)/shard_map/ppermute | solution.py:518
  167.4 28.9 %collective-permute-start.1 = (bf16[384,1536]{1,0:T(8,128)(2,1)S(1)}, bf16[384,1536]{1,0:T(8,128)(2,1)S(1)}, u32[]{:S(2)}, u32[]{:S(2)}) collective-permute-start(bf16[384,1536]{1,0:T(8,128)(2,1)S(1)} %add_convert_fusion.1), channel_id=1, source_target_pairs={{0,16},{16,0},{1,17},{17,1},{2,18},{18,2},{3,19},{19,3},{4,20},{20... | collective-permute-start | bytes 3538952 | tf_op jit(solution)/shard_map/ppermute | solution.py:518
  170.7 29.9 %collective-permute-start.6 = (bf16[384,896]{1,0:T(8,128)(2,1)S(1)}, bf16[384,896]{1,0:T(8,128)(2,1)S(1)}, u32[]{:S(2)}, u32[]{:S(2)}) collective-permute-start(bf16[384,896]{1,0:T(8,128)(2,1)S(1)} %add_convert_fusion.3), channel_id=1, source_target_pairs={{0,2},{1,3},{2,0},{3,1},{4,6},{5,7},{6,4},{7,5},{8,10},{9,11},{10,... | collective-permute-start | bytes 2064392 | tf_op jit(solution)/shard_map/ppermute | solution.py:518
  174.0 50.3 %collective-permute-start.4 = (bf16[384,1536]{1,0:T(8,128)(2,1)S(1)}, bf16[384,1536]{1,0:T(8,128)(2,1)S(1)}, u32[]{:S(2)}, u32[]{:S(2)}) collective-permute-start(bf16[384,1536]{1,0:T(8,128)(2,1)S(1)} %add_convert_fusion), channel_id=1, source_target_pairs={{0,16},{16,0},{1,17},{17,1},{2,18},{18,2},{3,19},{19,3},{4,20},{20... | collective-permute-start | bytes 3538952 | tf_op jit(solution)/shard_map/ppermute | solution.py:518
  198.1 24.0 %collective-permute-start.2 = (bf16[192,1536]{1,0:T(8,128)(2,1)S(1)}, bf16[192,1536]{1,0:T(8,128)(2,1)S(1)}, u32[]{:S(2)}, u32[]{:S(2)}) collective-permute-start(bf16[192,1536]{1,0:T(8,128)(2,1)S(1)} %add_convert_fusion.5), channel_id=1, source_target_pairs={{0,2},{1,3},{2,0},{3,1},{4,6},{5,7},{6,4},{7,5},{8,10},{9,11},{10,... | collective-permute-start | bytes 1769480 | tf_op jit(solution)/shard_map/ppermute | solution.py:518
  202.0 26.3 %collective-permute-start.7 = (bf16[192,896]{1,0:T(8,128)(2,1)S(1)}, bf16[192,896]{1,0:T(8,128)(2,1)}, u32[]{:S(2)}, u32[]{:S(2)}) collective-permute-start(bf16[192,896]{1,0:T(8,128)(2,1)S(1)} %add_convert_fusion.6), channel_id=1, source_target_pairs={{0,16},{16,0},{1,17},{17,1},{2,18},{18,2},{3,19},{19,3},{4,20},{20... | collective-permute-start | bytes 1032200 | tf_op jit(solution)/shard_map/ppermute | solution.py:518
  230.2 13.8 %collective-permute-start.17 = (bf16[96,896]{1,0:T(8,128)(2,1)}, bf16[96,896]{1,0:T(8,128)(2,1)}, u32[]{:S(2)}, u32[]{:S(2)}) collective-permute-start(bf16[96,896]{1,0:T(8,128)(2,1)} %add_convert_fusion.11), channel_id=1, source_target_pairs={{0,4},{1,5},{2,6},{3,7},{4,0},{5,1},{6,2},{7,3},{8,12},{9,13},{10,... | collective-permute-start | bytes 516104 | tf_op jit(solution)/shard_map/ppermute | solution.py:518
  232.0 15.7 %collective-permute-start.8 = (bf16[96,1536]{1,0:T(8,128)(2,1)}, bf16[96,1536]{1,0:T(8,128)(2,1)}, u32[]{:S(2)}, u32[]{:S(2)}) collective-permute-start(bf16[96,1536]{1,0:T(8,128)(2,1)} %add_convert_fusion.10), channel_id=1, source_target_pairs={{0,4},{1,5},{2,6},{3,7},{4,0},{5,1},{6,2},{7,3},{8,12},{9,13},{10,... | collective-permute-start | bytes 884744 | tf_op jit(solution)/shard_map/ppermute | solution.py:518
  233.0 18.9 %collective-permute-start.12 = (bf16[192,1536]{1,0:T(8,128)(2,1)}, bf16[192,1536]{1,0:T(8,128)(2,1)}, u32[]{:S(2)}, u32[]{:S(2)}) collective-permute-start(bf16[192,1536]{1,0:T(8,128)(2,1)} %add_convert_fusion.4), channel_id=1, source_target_pairs={{0,2},{1,3},{2,0},{3,1},{4,6},{5,7},{6,4},{7,5},{8,10},{9,11},{10,... | collective-permute-start | bytes 1769480 | tf_op jit(solution)/shard_map/ppermute | solution.py:518
  251.9 12.1 %collective-permute-start.19 = (bf16[768,384]{1,0:T(8,128)(2,1)S(1)}, bf16[768,384]{1,0:T(8,128)(2,1)S(1)}, u32[]{:S(2)}, u32[]{:S(2)}) collective-permute-start(bf16[768,384]{1,0:T(8,128)(2,1)S(1)} %copy-done.14), channel_id=1, source_target_pairs={{0,1},{1,0},{2,3},{3,2},{4,5},{5,4},{6,7},{7,6},{8,9},{9,8},{10,11... | collective-permute-start | bytes 1769480 | tf_op jit(solution)/shard_map/ppermute | solution.py:518
  260.6 19.8 %collective-permute-start.13 = (bf16[96,1536]{1,0:T(8,128)(2,1)S(1)}, bf16[96,1536]{1,0:T(8,128)(2,1)S(1)}, u32[]{:S(2)}, u32[]{:S(2)}) collective-permute-start(bf16[96,1536]{1,0:T(8,128)(2,1)S(1)} %add_convert_fusion.9), channel_id=1, source_target_pairs={{0,4},{1,5},{2,6},{3,7},{4,0},{5,1},{6,2},{7,3},{8,12},{9,13},{10,... | collective-permute-start | bytes 884744 | tf_op jit(solution)/shard_map/ppermute | solution.py:518
  268.9 37.9 %collective-permute-start.11 = (bf16[96,1536]{1,0:T(8,128)(2,1)S(1)}, bf16[96,1536]{1,0:T(8,128)(2,1)S(1)}, u32[]{:S(2)}, u32[]{:S(2)}) collective-permute-start(bf16[96,1536]{1,0:T(8,128)(2,1)S(1)} %pad_maximum_fusion.7), channel_id=1, source_target_pairs={{0,4},{1,5},{2,6},{3,7},{4,0},{5,1},{6,2},{7,3},{8,12},{9,13},{10,... | collective-permute-start | bytes 884744 | tf_op jit(solution)/shard_map/ppermute | solution.py:518
  281.5 14.0 %collective-permute-start.14 = (bf16[48,1536]{1,0:T(8,128)(2,1)S(1)}, bf16[48,1536]{1,0:T(8,128)(2,1)S(1)}, u32[]{:S(2)}, u32[]{:S(2)}) collective-permute-start(bf16[48,1536]{1,0:T(8,128)(2,1)S(1)} %add_convert_fusion.15), channel_id=1, source_target_pairs={{0,8},{1,9},{2,10},{3,11},{4,12},{5,13},{6,14},{7,15},{8,0},{9,1},... | collective-permute-start | bytes 442376 | tf_op jit(solution)/shard_map/ppermute | solution.py:518
  286.4 12.3 %collective-permute-start.26 = (bf16[48,768]{1,0:T(8,128)(2,1)S(1)}, bf16[48,768]{1,0:T(8,128)(2,1)S(1)}, u32[]{:S(2)}, u32[]{:S(2)}) collective-permute-start(bf16[48,768]{1,0:T(8,128)(2,1)S(1)} %pad_maximum_fusion.11), channel_id=1, source_target_pairs={{0,8},{1,9},{2,10},{3,11},{4,12},{5,13},{6,14},{7,15},{8,0},{9,1},... | collective-permute-start | bytes 221192 | tf_op jit(solution)/shard_map/ppermute | solution.py:518
  313.8 12.6 %collective-permute-start.29 = (bf16[192,1536]{1,0:T(8,128)(2,1)S(1)}, bf16[192,1536]{1,0:T(8,128)(2,1)S(1)}, u32[]{:S(2)}, u32[]{:S(2)}) collective-permute-start(bf16[192,1536]{1,0:T(8,128)(2,1)S(1)} %pad_maximum_fusion.4), channel_id=1, source_target_pairs={{0,2},{1,3},{2,0},{3,1},{4,6},{5,7},{6,4},{7,5},{8,10},{9,11},{10,... | collective-permute-start | bytes 1769480 | tf_op jit(solution)/shard_map/ppermute | solution.py:518
  314.8 12.8 %collective-permute-start.30 = (bf16[192,1536]{1,0:T(8,128)(2,1)S(1)}, bf16[192,1536]{1,0:T(8,128)(2,1)S(1)}, u32[]{:S(2)}, u32[]{:S(2)}) collective-permute-start(bf16[192,1536]{1,0:T(8,128)(2,1)S(1)} %pad_maximum_fusion.5), channel_id=1, source_target_pairs={{0,4},{1,5},{2,6},{3,7},{4,0},{5,1},{6,2},{7,3},{8,12},{9,13},{10,... | collective-permute-start | bytes 1769480 | tf_op jit(solution)/shard_map/ppermute | solution.py:518
  315.7 13.0 %collective-permute-start.31 = (bf16[192,1664]{1,0:T(8,128)(2,1)S(1)}, bf16[192,1664]{1,0:T(8,128)(2,1)S(1)}, u32[]{:S(2)}, u32[]{:S(2)}) collective-permute-start(bf16[192,1664]{1,0:T(8,128)(2,1)S(1)} %pad_maximum_fusion.3), channel_id=1, source_target_pairs={{0,16},{16,0},{1,17},{17,1},{2,18},{18,2},{3,19},{19,3},{4,20},{20... | collective-permute-start | bytes 1916936 | tf_op jit(solution)/shard_map/ppermute | solution.py:518
  330.5 28.2 %collective-permute-start.32 = (bf16[384,1536]{1,0:T(8,128)(2,1)}, bf16[384,1536]{1,0:T(8,128)(2,1)}, u32[]{:S(2)}, u32[]{:S(2)}) collective-permute-start(bf16[384,1536]{1,0:T(8,128)(2,1)} %pad_maximum_fusion.1.mine), channel_id=1, source_target_pairs={{0,16},{16,0},{1,17},{17,1},{2,18},{18,2},{3,19},{19,3},{4,20},{20... | collective-permute-start | bytes 3538952 | tf_op jit(solution)/shard_map/ppermute | solution.py:518
  332.1 27.9 %collective-permute-start.33 = (bf16[384,1536]{1,0:T(8,128)(2,1)}, bf16[384,1536]{1,0:T(8,128)(2,1)}, u32[]{:S(2)}, u32[]{:S(2)}) collective-permute-start(bf16[384,1536]{1,0:T(8,128)(2,1)} %pad_maximum_fusion.2.mine), channel_id=1, source_target_pairs={{0,2},{1,3},{2,0},{3,1},{4,6},{5,7},{6,4},{7,5},{8,10},{9,11},{10,... | collective-permute-start | bytes 3538952 | tf_op jit(solution)/shard_map/ppermute | solution.py:518
  332.9 10.2 %collective-permute-start.37 = (bf16[384,1664]{1,0:T(8,128)(2,1)}, bf16[384,1664]{1,0:T(8,128)(2,1)}, u32[]{:S(2)}, u32[]{:S(2)}) collective-permute-start(bf16[384,1664]{1,0:T(8,128)(2,1)} %pad_maximum_fusion.mine), channel_id=1, source_target_pairs={{0,1},{1,0},{2,3},{3,2},{4,5},{5,4},{6,7},{7,6},{8,9},{9,8},{10,11... | collective-permute-start | bytes 3833864 | tf_op jit(solution)/shard_map/ppermute | solution.py:518
  333.0 30.7 %collective-permute-start.34 = (bf16[384,1664]{1,0:T(8,128)(2,1)}, bf16[384,1664]{1,0:T(8,128)(2,1)}, u32[]{:S(2)}, u32[]{:S(2)}) collective-permute-start(bf16[384,1664]{1,0:T(8,128)(2,1)} %pad_maximum_fusion.mine), channel_id=1, source_target_pairs={{0,4},{1,5},{2,6},{3,7},{4,0},{5,1},{6,2},{7,3},{8,12},{9,13},{10,... | collective-permute-start | bytes 3833864 | tf_op jit(solution)/shard_map/ppermute | solution.py:518
  (34 other events, 303.6 us)

commit v4 on v3

--- a/solution.py
+++ b/solution.py
@@ -115,13 +115,13 @@
 
 
 def mid_kernel(
-    fetch, queries, arrived, order, inverse, tok, cot,
+    fetch, queries, arrived, order, inverse, tok_hbm, cot_hbm,
     b_out, gain_one, shift_one, b_up, b_down, gain_two, shift_two, w_out_hbm, w_up_hbm, w_down_hbm,
     back, dq_out, attn_out, z_out, active_out, du_out, df_out, db_out, dh1_out, layer_out, sums,
     kv, probs, attn, mixed, w_out, w_up, w_down, hidden, z_full, n_one, r_one, z_low, active, slope,
-    dh2, df, db, d_out, dh1, final, dq, kv_sem, w_sem, out_sem, back_sem,
+    dh2, df, db, d_out, dh1, final, dq, tok, cot, kv_sem, w_sem, out_sem, back_sem,
 ):
-    rows = tok.shape[0]
+    rows = tok_hbm.shape[0]
     per_dev = rows // CLUS
     pair_width = 2 * HEAD_DIM
     requests = fetch.shape[0]
@@ -141,7 +141,7 @@
     loads = [
         pltpu.make_async_copy(source, target, w_sem.at[at])
         for at, (source, target) in enumerate(
-            ((w_out_hbm, w_out), (w_up_hbm, w_up), (w_down_hbm, w_down))
+            ((w_out_hbm, w_out), (tok_hbm, tok), (w_up_hbm, w_up), (w_down_hbm, w_down), (cot_hbm, cot))
         )
     ]
     for load in loads:
@@ -179,6 +179,7 @@
 
     store(attn, attn_out)
     loads[0].wait()
+    loads[1].wait()
     hidden[...] = nn(attn[...], w_out[...])
 
     @pl.loop(0, tiles)
@@ -196,8 +197,8 @@
         hidden[at, :] = z + as_row(b_down)
 
     store(z_low, z_out)
-    loads[1].wait()
     loads[2].wait()
+    loads[3].wait()
 
     @pl.loop(0, width // WIDE_FORTH)
     def _(step):
@@ -210,6 +211,7 @@
         hidden[...] += nn(active[:, at], w_down[at, :])
 
     store(active, active_out)
+    loads[4].wait()
     sums[...] = jnp.zeros_like(sums)
 
     @pl.loop(0, tiles)
@@ -384,26 +386,42 @@
         at = pl.ds(pl.multiple_of(core_of(info, side) * half, half), half)
         buf[side, :, :half] = nn(attn_t[...], db[:, at]).astype(LOW)
         buf[side, :, half:D] = nn(tok_t[...], grad_q[:, at]).astype(LOW)
-        place_chunks(buf.at[side], out, info, sem.at[side], 65)
+        place_chunks(buf.at[side], out, info, sem.at[side])
     for side, out in ((0, give), (1, keep)):
         wait_chunks(buf.at[side], out, sem.at[side])
 
 
 def key_value_kernel(
-    info, segment, returned, order, tok, key_give, key_keep, value_give, value_keep, grad_kv, total, tok_t, buf, sem
+    info, segment, returned_hbm, order, tok, key_give, key_keep, value_give, value_keep, grad_kv_hbm,
+    returned, total, tok_t, grad_kv, buf, load_sem, kv_sem, sem,
 ):
     rows = tok.shape[0]
     half = D // 2
     per_dev = rows // CLUS
     pair_width = 2 * HEAD_DIM
+    devices = load_sem.shape[0]
+    capacity = segment.shape[0] // devices
+
+    def load(device):
+        span = pl.ds(device * capacity, capacity)
+        return pltpu.make_async_copy(returned_hbm.at[span], returned.at[span], load_sem.at[device])
+
+    @pl.loop(0, devices)
+    def _(device):
+        load(device).start()
+
     down = lax.broadcasted_iota(jnp.int32, (rows, rows), 0)
     left = left_half((rows, pair_width))
     total[...] = jnp.zeros_like(total)
-
-    @pl.loop(0, segment.shape[0], unroll=4)
-    def _(slot):
-        block = segment[slot]
-        total[block] += returned[slot].astype(F32)
+    tok_t[...] = tok[...].T
+
+    @pl.loop(0, devices)
+    def _(device):
+        load(device).wait()
+        for step in range(capacity):
+            slot = device * capacity + step
+            block = segment[slot]
+            total[block] += returned[slot].astype(F32)
 
     for quad in range(HEADS // 4):
         pairs = range(2 * quad, 2 * quad + 2)
@@ -418,17 +436,20 @@
             grad_kv[:, pair * pair_width : (pair + 1) * pair_width] = jnp.where(left, even, odd).astype(LOW)
             values = pltpu.roll(jnp.where(left, odd, even), HEAD_DIM, 1)
             grad_kv[:, D + pair * pair_width : D + (pair + 1) * pair_width] = values.astype(LOW)
-    tok_t[...] = tok[...].T
+    stored = pltpu.make_async_copy(grad_kv, grad_kv_hbm, kv_sem)
+    stored.start()
     outs = ((key_give, key_keep), (value_give, value_keep))
     for side in range(2):
         base = core_of(info, side) * half
+        parts = [grad_kv[:, pl.ds(pl.multiple_of(part * D + base, half), half)] for part in range(2)]
+        value = nn(tok_t[...], jnp.concatenate(parts, axis=1)).astype(LOW)
         for part in range(2):
-            at = pl.ds(pl.multiple_of(part * D + base, half), half)
-            buf[part, side] = nn(tok_t[...], grad_kv[:, at]).astype(LOW)
+            buf[part, side] = value[:, part * half : (part + 1) * half]
             place_chunks(buf.at[part, side], outs[part][side], info, sem.at[part, side], 65 if part else 1)
     for side in range(2):
         for part in range(2):
             wait_chunks(buf.at[part, side], outs[part][side], sem.at[part, side])
+    stored.wait()
 
 
 def spread_start(info, start, pieces, targets, buf, sem):
@@ -436,22 +457,16 @@
     copies = []
     for at, piece in enumerate(pieces):
         core = core_of(info, 1 - at)
-        for chunk in range(CHUNKS // 2):
+        for chunk in range(buf.shape[1]):
             buf[at, chunk] = piece[chunk * size : (chunk + 1) * size].astype(F32)
-            for lanes, target in targets(core, info[start + chunk], size, at == 0):
-                copies.append(pltpu.make_async_copy(buf.at[at, chunk, : target.shape[0], lanes], target, sem))
+            for lanes, target in targets(core, chunk_rows(info[start + chunk], size)):
+                copies.append(pltpu.make_async_copy(buf.at[at, chunk, :, lanes], target, sem))
                 copies[-1].start()
     return copies
 
 
-def spread(info, start, pieces, targets, buf, sem):
-    for copy in spread_start(info, start, pieces, targets, buf, sem):
-        copy.wait()
-
-
 def up_targets(out, half):
-    def targets(core, chunk, size, mine):
-        rows = chunk_rows(chunk, size)
+    def targets(core, rows):
         yield pl.ds(0, half), out.at[rows, pl.ds(pl.multiple_of(core * half, half), half)]
 
     return targets
@@ -460,50 +475,78 @@
 def down_targets(out, half):
     parts = half // D
 
-    def targets(core, chunk, size, mine):
-        rows = chunk_rows(chunk, size)
+    def targets(core, rows):
         for part in range(parts):
             yield pl.ds(part * D, D), out.at[core * parts + part, rows]
 
     return targets
 
 
-def attention_targets(w_out, w_qkv, vectors, wide):
+def attention_targets(w_out, w_qkv):
     half = D // 2
 
-    def targets(core, chunk, size, mine):
-        rows = chunk_rows(chunk, size)
+    def targets(core, rows):
         at = pl.ds(pl.multiple_of(core * half, half), half)
         yield pl.ds(0, half), w_out.at[rows, at]
         for part, lane in enumerate((half, D + LANES, D + LANES + half)):
             to = pl.ds(pl.multiple_of(part * D + core * half, half), half)
             yield pl.ds(lane, half), w_qkv.at[rows, to]
-        if mine:
-            yield pl.ds(D, LANES), vectors.at[chunk]
 
     return targets
 
 
-def spread_kernel(start, route, count, info, mine, other, *refs):
-    buf, sem = refs[-2:]
-    spread(info, start, (mine, other), route(*refs[:count], mine.shape[1]), buf, sem)
-
-
-def spread_last_kernel(info, *refs):
-    pieces, outs, staged, bufs = refs[:6], refs[11:16], refs[16:22], refs[22:25]
-    load_sem, sem = refs[25:]
-    w_up, w_down, w_out, w_qkv, vectors = outs
+def spread_groups(groups, info, pieces, outs, staged, bufs, load_sem, sem):
+    w_up, w_down, w_out, w_qkv = outs
     half = w_up.shape[1] // 2
+    routes = (up_targets(w_up, half), down_targets(w_down, half), attention_targets(w_out, w_qkv))
     loads = []
     for at, (source, target) in enumerate(zip(pieces, staged)):
         loads.append(pltpu.make_async_copy(source, target, load_sem.at[at]))
         loads[-1].start()
-    routes = (up_targets(w_up, half), down_targets(w_down, half), attention_targets(w_out, w_qkv, vectors, half))
     copies = []
-    for at, (start, targets) in enumerate(zip((25, 41, 57), routes)):
+    for at, (third, start) in enumerate(groups):
         for load in loads[2 * at : 2 * at + 2]:
             load.wait()
-        copies += spread_start(info, start, staged[2 * at : 2 * at + 2], targets, bufs[at], sem.at[at])
+        copies += spread_start(info, start, staged[2 * at : 2 * at + 2], routes[third], bufs[at], sem.at[at])
+    return copies
+
+
+def spread_kernel(groups, info, *refs):
+    pairs = len(groups)
+    pieces, scratch = refs[: 2 * pairs], refs[-3 * pairs - 2 :]
+    outs = refs[-3 * pairs - 6 : -3 * pairs - 2]
+    staged, bufs = scratch[: 2 * pairs], scratch[2 * pairs : 3 * pairs]
+    for copy in spread_groups(groups, info, pieces, outs, staged, bufs, *scratch[3 * pairs :]):
+        copy.wait()
+
+
+def spread_last_kernel(groups, start, info, *refs):
+    pairs = len(groups)
+    pieces, sources = refs[: 2 * pairs], refs[2 * pairs : 2 * pairs + 4]
+    rest = refs[2 * pairs + 8 :]
+    outs, vectors, rest = rest[:4], rest[4:13], rest[13:]
+    staged, bufs = rest[: 2 * pairs], rest[2 * pairs : 3 * pairs]
+    load_sem, sem, columns, table, column_sem = rest[3 * pairs :]
+    loads = [
+        pltpu.make_async_copy(source.at[:, D : D + LANES], columns.at[at], column_sem.at[at])
+        for at, source in enumerate(sources)
+    ]
+    for load in loads:
+        load.start()
+    copies = spread_groups(groups, info, pieces, outs, staged, bufs, load_sem, sem)
+    size = D // CHUNKS
+    each = CHUNKS // len(sources)
+    for at, load in enumerate(loads):
+        load.wait()
+        for chunk in range(each):
+            table[info[start + at * each + chunk]] = columns[at, chunk * size : chunk * size + 16].astype(F32)
+
+    def whole(vector):
+        return jnp.concatenate([table[vector, row : row + 1] for row in range(D // LANES)], axis=1)
+
+    for at, vector in enumerate(vectors):
+        count = vector.shape[0] // D
+        vector[...] = jnp.concatenate([whole(at + part) for part in range(count)], axis=1).reshape(count * D)
     for copy in copies:
         copy.wait()
 
@@ -704,7 +747,7 @@
             low(rows, ff), low(rows, ff), low(rows, D), low(rows, D), full(rows, D), low(rows, D),
             full(16, D),
         ),
-        in_specs=[smem, vmem, hbm] + [vmem] * 11 + [hbm] * 3,
+        in_specs=[smem, vmem, hbm, vmem, vmem, hbm, hbm] + [vmem] * 7 + [hbm] * 3,
         out_specs=(hbm,) * 10 + (vmem,),
         scratch_shapes=[
             pltpu.VMEM((requests, CLUS, pair_width), LOW),
@@ -728,8 +771,10 @@
             pltpu.VMEM((rows, D), F32),
             pltpu.VMEM((rows, D), LOW),
             pltpu.VMEM((HEADS, rows, pair_width), LOW),
+            pltpu.VMEM((rows, D), LOW),
+            pltpu.VMEM((rows, D), LOW),
             pltpu.SemaphoreType.DMA((HEADS // 2,)),
-            pltpu.SemaphoreType.DMA((3,)),
+            pltpu.SemaphoreType.DMA((5,)),
             pltpu.SemaphoreType.DMA((9,)),
             pltpu.SemaphoreType.DMA,
         ],
@@ -770,6 +815,8 @@
     down_give, down_keep = halves(
         down_kernel, (info, active, grad_second), ff // 2, [], name="down_kernel"
     )
+    up = [up_keep, swap(up_give, CORE)]
+    up_step, attn = tie((to_send(up), attn))
     oq_give, oq_keep, grad_q = halves(
         out_q_kernel,
         (info, attn, grad_branch, tokens, dq_sorted, order_rows, sums),
@@ -778,9 +825,9 @@
         (low(rows, D),),
         name="out_q_kernel",
     )
-    up = scatter_steps([up_keep, swap(up_give, CORE)], (X, Y))
+    up = scatter_steps(up + [swap(up_step, X)], (Y,))
     down = scatter_steps([down_keep, swap(down_give, CORE)], (X,))
-    out_q = scatter_steps([oq_keep, swap(oq_give, CORE)], (Y, X))
+    out_q = scatter_steps([oq_keep, swap(oq_give, CORE)], (X,))
     up_step = to_send(up)
     up_step, down[-1] = tie((up_step, down[-1]))
     down_step = to_send(down)
@@ -788,15 +835,20 @@
     returned, up_step, down_step, out_q[-1] = tie((returned, up_step, down_step, out_q[-1]))
     up = up + [swap(up_step, Z0)]
     down = down + [swap(down_step, Y)]
+    out_q = scatter_steps(out_q, (Y,))
     key_give, key_keep, value_give, value_keep, grad_kv = pl.pallas_call(
         key_value_kernel,
         out_shape=(low(D, half),) * 4 + (low(rows, 2 * D),),
-        in_specs=[smem, smem, vmem, vmem, vmem],
-        out_specs=(hbm,) * 4 + (vmem,),
+        in_specs=[smem, smem, hbm, vmem, vmem],
+        out_specs=(hbm,) * 5,
         scratch_shapes=[
+            pltpu.VMEM((slots, CLUS, pair_width), LOW),
             pltpu.VMEM((blocks + 1, CLUS, pair_width), F32),
             turned,
+            pltpu.VMEM((rows, 2 * D), LOW),
             pltpu.VMEM((2, 2, D, half), LOW),
+            pltpu.SemaphoreType.DMA((count_blk,)),
+            pltpu.SemaphoreType.DMA,
             pltpu.SemaphoreType.DMA((2, 2)),
         ],
         compiler_params=params(),
@@ -823,63 +875,74 @@
         )
     ]
 
-    def spread_call(start, route, mine, other, outs):
-        count = len(outs)
+    orders = (ORDER_X, ORDER_Y, ORDER_Z)
+    starts = (17, 33, 49)
+    weights = (full(D, ff), full(ff // D, D, D), full(D, D), full(D, 3 * D))
+
+    def swap_all(values, step):
+        return [swap(value, order[step]) for value, order in zip(values, orders)]
+
+    def spread_scratch(pieces):
+        rows_each = D // CHUNKS
+        return (
+            [pltpu.VMEM(piece.shape, LOW) for piece in pieces]
+            + [
+                pltpu.VMEM((2, piece.shape[0] // rows_each, rows_each, piece.shape[1]), F32)
+                for piece in pieces[::2]
+            ]
+            + [
+                pltpu.SemaphoreType.DMA((len(pieces),)),
+                pltpu.SemaphoreType.DMA((len(pieces) // 2,)),
+            ]
+        )
+
+    def with_other(sets):
+        return [array for value in sets for array in (value, swap(value, CORE))]
+
+    def spread(sets, offsets, outs=()):
+        pieces = with_other(sets)
+        groups = tuple((third, starts[third] + offset) for offset in offsets for third in range(3))
         return pl.pallas_call(
-            partial(spread_kernel, start, route, count),
-            out_shape=outs,
-            in_specs=[smem, vmem, vmem],
-            out_specs=(hbm,) * count,
-            scratch_shapes=[
-                pltpu.VMEM((2, CHUNKS // 2, D // CHUNKS, mine.shape[1]), F32),
-                pltpu.SemaphoreType.DMA,
-            ],
+            partial(spread_kernel, groups),
+            out_shape=weights,
+            in_specs=[smem] + [hbm] * (len(pieces) + len(outs)),
+            out_specs=(hbm,) * 4,
+            scratch_shapes=spread_scratch(pieces),
+            input_output_aliases={1 + len(pieces) + at: at for at in range(len(outs))},
             compiler_params=params(),
-            cost_estimate=pl.CostEstimate(flops=20_000_000_000, bytes_accessed=20_000_000, transcendentals=0),
-            name=route.__name__,
-        )(info, mine, other)
-
-    orders = (ORDER_X, ORDER_Y, ORDER_Z)
-    for step in (1, 2):
-        thirds = tie(gather_step(value, order[step]) for value, order in zip(thirds, orders))
-    grad_kv, *thirds = tie((grad_kv, *thirds))
+            name="spread",
+        )(info, *pieces, *outs)
+
+    thirds = list(tie(gather_step(value, order[1]) for value, order in zip(thirds, orders)))
+    third_step = swap_all(thirds, 2)
+    fourth_step = swap_all(thirds, 3)
+    outs = spread(thirds, (0,))
+    tied = tie((*third_step, grad_kv))
+    third_step, grad_kv = list(tied[:3]), tied[3]
+    last_step = swap_all(third_step, 3)
     grad_proj = jnp.concatenate([grad_q, grad_kv], axis=1)
     grad_tokens = (grad_resid + nt(grad_proj, w_qkv)).astype(LOW)
-    last = [swap(value, order[-1]) for value, order in zip(thirds, orders)]
-    other = [swap(value, CORE) for value in thirds]
-    outs = []
-    for at, (start, route, shapes) in enumerate(
-        (
-            (17, up_targets, (full(D, ff),)),
-            (33, down_targets, (full(ff // D, D, D),)),
-            (49, attention_targets, (full(D, D), full(D, 3 * D), full(CHUNKS, 8, LANES))),
-        )
-    ):
-        outs += spread_call(start, route, thirds[at], other[at], shapes)
-    tied = tie((*last, *outs))
-    last, outs = tied[: len(last)], tied[len(last) :]
-    last_pieces = []
-    for value in last:
-        last_pieces += [value, swap(value, CORE)]
-    sum_up, sum_down, sum_out, sum_qkv, vectors = pl.pallas_call(
-        spread_last_kernel,
-        out_shape=tuple(full(*out.shape) for out in outs),
-        in_specs=[smem] + [hbm] * 11,
-        out_specs=(hbm,) * 5,
-        scratch_shapes=[pltpu.VMEM(piece.shape, LOW) for piece in last_pieces]
+    tied = tie((*fourth_step, *outs, grad_tokens))
+    fourth_step, outs, grad_tokens = list(tied[:3]), tied[3:7], tied[7]
+    outs = spread(third_step + fourth_step, (4, 8), outs)
+    tied = tie((*last_step, *outs))
+    last_step, outs = list(tied[:3]), tied[3:]
+    pieces = with_other(last_step)
+    sum_up, sum_down, sum_out, sum_qkv, *vectors = pl.pallas_call(
+        partial(spread_last_kernel, tuple((third, starts[third] + 12) for third in range(3)), starts[2]),
+        out_shape=weights + (full(D),) * 8 + (full(ff),),
+        in_specs=[smem] + [hbm] * (len(pieces) + 8),
+        out_specs=(hbm,) * 4 + (vmem,) * 9,
+        scratch_shapes=spread_scratch(pieces)
         + [
-            pltpu.VMEM((2, CHUNKS // 2, D // CHUNKS, piece.shape[1]), F32)
-            for piece in last_pieces[::2]
-        ]
-        + [
-            pltpu.SemaphoreType.DMA((6,)),
-            pltpu.SemaphoreType.DMA((3,)),
+            pltpu.VMEM((4, D // 4, LANES), LOW),
+            pltpu.VMEM((CHUNKS, 16, LANES), F32),
+            pltpu.SemaphoreType.DMA((4,)),
         ],
-        input_output_aliases={7 + at: at for at in range(5)},
+        input_output_aliases={1 + len(pieces) + 4 + at: at for at in range(4)},
         compiler_params=params(),
         name="spread_last",
-    )(info, *last_pieces, *outs)
-    vectors = vectors[:, : D // LANES].reshape(CHUNKS, D)
+    )(info, *pieces, thirds[2], third_step[2], fourth_step[2], last_step[2], *outs)
     return (
         layer_out,
         grad_tokens,
@@ -891,7 +954,7 @@
         vectors[3],
         vectors[4],
         sum_up,
-        vectors[8 : 8 + ff // D].reshape(ff),
+        vectors[8],
         sum_down.reshape(ff, D),
         vectors[2],
         vectors[0],

time: 385 us -> 379 us (0.984)
  starting transfers between devices: 59.9 us -> 67 us
  other arithmetic: 31.9 us -> 26.1 us
  waiting for transfers between devices: 174 us -> 169 us
    ppermute x41 -> x50, starting transfers between devices: 34.7 us -> 41.8 us  [swap(): return lax.ppermute(value, axis, [(i, i ^ distance) for i in range(size)])]
    ppermute x41 -> x50, waiting for transfers between devices: 115 us -> 110 us  [swap(): return lax.ppermute(value, axis, [(i, i ^ distance) for i in range(size)])]
    pallas_call x4 -> x3, Pallas kernels: 19.1 us -> 18.3 us  [the longest x2 12.8 us: spread(): pl.pallas_call(partial(spread_kernel, groups), out_shape=weights, in_spec...]
  transfers between devices with their start and end apart: 43 -> 52, of which waited for: 24 -> 27; matrix products, arithmetic and copies ran while one was open for 9% -> 8% of each run, Pallas kernels for 12% -> 13%
where the time goes in v4:
time: 379 us; the launch traced here: 375 us
  waiting for transfers between devices  169 us (45%)
  Pallas kernels  96.4 us (25%)
  starting transfers between devices  67 us (18%)
  other arithmetic  26.1 us (7%)
  local copies, waits for them, and re-layouts  9.65 us (3%)
  matrix products  5.03 us (1%)
    ppermute x50, waiting for transfers between devices, swap(): return lax.ppermute(value, axis, [(i, i ^ distance) for i in range(size)])  110 us
    all_to_all x1, waiting for transfers between devices, per_device(): lax.all_to_all(outgoing.reshape(count_blk, capacity, CLUS, pair_width), '...  58.8 us
    ppermute x50, starting transfers between devices, swap(): return lax.ppermute(value, axis, [(i, i ^ distance) for i in range(size)])  41.8 us
    pallas_call x1, Pallas kernels, per_device(): pl.pallas_call(mid_kernel, out_shape=(low(slots, CLUS, pair_width), low(H...  36.9 us
    pallas_call x3, Pallas kernels, halves(): pl.pallas_call(kernel, out_shape=(low(D, columns), low(D, columns)) + mor...  20.1 us
    all_to_all x1, starting transfers between devices, per_device(): lax.all_to_all(back.reshape(count_blk, capacity, CLUS, pair_width), 'blk'...  17.6 us
    convert_element_type x19, other arithmetic, to_send(): return sum_rows(terms, rows // 2, rows).astype(LOW)  16.7 us
    pallas_call x2, Pallas kernels, spread(): pl.pallas_call(partial(spread_kernel, groups), out_shape=weights, in_spec...  12.8 us
  transfers between devices with their start and end apart: 52, of which 27 were waited for; matrix products, arithmetic and copies ran while one was open for 8% of the time, Pallas kernels for 13%

profile of v4, /device:TPU:0, one launch (start us, length us, event | category | flops | bytes accessed | tf_op | source)
XLA Modules:
  0.0 374.5 jit_solution(9025280017299881516)
XLA Ops:
  4.3 6.9 %kv_kernel.1 = bf16[112,128,128]{2,1,0:T(8,128)(2,1)} custom-call(bf16[512,768]{1,0:T(8,128)(2,1)} %tok.7, bf16[768,2304]{1,0:T(8,128)(2,1)} %w_value.1, bf16[768,2304]{1,0:T(8,128)(2,1)} %w_value.1, bf16[768]{0:T(1024)(128)(2,1)} %b_value.1, s32[1,12,512]{2,1,0:T(8,128)} %copy.68.perm, s32[16,7]{1,0:T(8,128)} %copy.74.chosen_in), custom_call_target="tpu_custom_call" | custom-call | tf_op jit(solution)/shard_map/kv_kernel/pallas_call | solution.py:692
  11.2 7.6 %all-to-all-start = ((bf16[16,7,128,128]{3,2,1,0:T(8,128)(2,1)}), bf16[16,7,128,128]{3,2,1,0:T(8,128)(2,1)}, u32[]{:S(2)}, u32[]{:S(2)}) async-start(bf16[16,7,128,128]{3,2,1,0:T(8,128)(2,1)} %bitcast.17), calls=%async_computation | async-start | bytes 7340032 | tf_op jit(solution)/shard_map/all_to_all | solution.py:707
  21.4 5.7 %q_kernel.1.queries = bf16[12,512,128]{2,1,0:T(8,128)(2,1)} custom-call(bf16[512,768]{1,0:T(8,128)(2,1)} %tok.7, bf16[768,2304]{1,0:T(8,128)(2,1)} %w_value.1, bf16[768]{0:T(1024)(128)(2,1)} %b_query.1, s32[1,12,512]{2,1,0:T(8,128)} %copy.68.perm), custom_call_target="tpu_custom_call" | custom-call | tf_op jit(solution)/shard_map/q_kernel/pallas_call | solution.py:716
  28.6 58.8 %all-to-all-done = bf16[16,7,128,128]{3,2,1,0:T(8,128)(2,1)} async-done(((bf16[16,7,128,128]{3,2,1,0:T(8,128)(2,1)}), bf16[16,7,128,128]{3,2,1,0:T(8,128)(2,1)}, u32[]{:S(2)}, u32[]{:S(2)}) %all-to-all-start) | async-done | bytes 3670048 | tf_op jit(solution)/shard_map/all_to_all | solution.py:707
  87.4 36.9 %mid_kernel.1 = (bf16[112,128,128]{2,1,0:T(8,128)(2,1)}, bf16[12,512,128]{2,1,0:T(8,128)(2,1)}, bf16[512,768]{1,0:T(8,128)(2,1)}, bf16[512,768]{1,0:T(8,128)(2,1...) custom-call(s32[96]{0:T(128)} %multiply_add_fusion.fetch, ...), custom_call_target="tpu_custom_call" | custom-call | tf_op jit(solution)/shard_map/mid_kernel/pallas_call | solution.py:743
  124.3 17.6 %all-to-all-start.1 = ((bf16[16,7,128,128]{3,2,1,0:T(8,128)(2,1)}), bf16[16,7,128,128]{3,2,1,0:T(8,128)(2,1)}, u32[]{:S(2)}, u32[]{:S(2)}) async-start(bf16[16,7,128,128]{3,2,1,0:T(8,128)(2,1)} %bitcast.18), calls=%async_computation.1 | async-start | bytes 7340032 | tf_op jit(solution)/shard_map/all_to_all | solution.py:787
  142.7 6.2 %up_kernel.1 = (bf16[768,1536]{1,0:T(8,128)(2,1)}, bf16[768,1536]{1,0:T(8,128)(2,1)}) custom-call(s32[81]{0:T(128)} %concatenate.36.info, bf16[512,768]{1,0:T(8,128)(2,1)} %get-tuple-element.93.z_low, bf16[512,3072]{1,0:T(8,128)(2,1)} %get-tuple-element.94.grad), custom_call_target="tpu_custom_call" | custom-call | flops 1 | bytes 1 | tf_op jit(solution)/shard_map/up_kernel/pallas_call | solution.py:798
  149.2 6.3 %down_kernel.1 = (bf16[768,1536]{1,0:T(8,128)(2,1)}, bf16[768,1536]{1,0:T(8,128)(2,1)}) custom-call(s32[81]{0:T(128)} %concatenate.36.info, bf16[512,3072]{1,0:T(8,128)(2,1)} %get-tuple-element.100.active, bf16[512,768]{1,0:T(8,128)(2,1)} %get-tuple-element.101.grad), custom_call_target="tpu_custom_call" | custom-call | flops 1 | bytes 1 | tf_op jit(solution)/shard_map/down_kernel/pallas_call | solution.py:798
  158.9 7.6 %out_q_kernel.1 = (bf16[768,896]{1,0:T(8,128)(2,1)}, bf16[768,896]{1,0:T(8,128)(2,1)}, bf16[512,768]{1,0:T(8,128)(2,1)}) custom-call(s32[81]{0:T(128)} %concatenate.36.info, bf16[512,768]{1,0:T(8,128)(2,1)} %get-tuple-element.106.attn, bf16[512,768]{1,0:T(8,128)(2,1)} %get-tuple-element.107.db, bf16[512,768]{1,0:T(8,128)(2,1)} %tok.7, ...), custom_call_target="tpu_custom_call" | custom-call | flops 1 | bytes 1 | tf_op jit(solution)/shard_map/out_q_kernel/pallas_call | solution.py:798
  168.8 17.5 %collective-permute-done.1 = bf16[384,1536]{1,0:T(8,128)(2,1)} collective-permute-done((bf16[384,1536]{1,0:T(8,128)(2,1)S(1)}, bf16[384,1536]{1,0:T(8,128)(2,1)}, u32[]{:S(2)}, u32[]{:S(2)}) %collective-permute-start.1) | collective-permute-done | bytes 1179680 | tf_op jit(solution)/shard_map/ppermute | solution.py:561
  191.8 20.1 %collective-permute-done.2 = bf16[192,1536]{1,0:T(8,128)(2,1)S(1)} collective-permute-done((bf16[192,1536]{1,0:T(8,128)(2,1)S(1)}, bf16[192,1536]{1,0:T(8,128)(2,1)S(1)}, u32[]{:S(2)}, u32[]{:S(2)}) %collective-permute-start.2) | collective-permute-done | bytes 589856 | tf_op jit(solution)/shard_map/ppermute | solution.py:561
  217.3 8.3 %collective-permute-done.6 = bf16[384,896]{1,0:T(8,128)(2,1)S(1)} collective-permute-done((bf16[384,896]{1,0:T(8,128)(2,1)S(1)}, bf16[384,896]{1,0:T(8,128)(2,1)S(1)}, u32[]{:S(2)}, u32[]{:S(2)}) %collective-permute-start.6) | collective-permute-done | bytes 688160 | tf_op jit(solution)/shard_map/ppermute | solution.py:561
  231.2 8.3 %key_value_kernel.1 = (bf16[768,384]{1,0:T(8,128)(2,1)}, bf16[768,384]{1,0:T(8,128)(2,1)}, bf16[768,384]{1,0:T(8,128)(2,1)}, bf16[768,384]{1,0:T(8,128)(2,1)}, bf16[512,1536]{1,0:T(8,128)(2,1)}) custom-call(s32[81]{0:T(128)} %concatenate.36.info, s32[112]{0:T(128)} %select_n.216.segment, bf16[112,128,128]{2,1,0:T(8,128)(2,1)} %bitcast.8.returned_hbm, ...), custom_call_target="tpu_custom_call" | custom-call | tf_op jit(solution)/shard_map/key_value_kernel/pallas_call | solution.py:839
  245.3 4.2 %collective-permute-done.8 = bf16[48,1536]{1,0:T(8,128)(2,1)S(1)} collective-permute-done((bf16[48,1536]{1,0:T(8,128)(2,1)S(1)}, bf16[48,1536]{1,0:T(8,128)(2,1)S(1)}, u32[]{:S(2)}, u32[]{:S(2)}) %collective-permute-start.8) | collective-permute-done | bytes 147488 | tf_op jit(solution)/shard_map/ppermute | solution.py:561
  256.8 4.2 %collective-permute-done.9 = bf16[48,1536]{1,0:T(8,128)(2,1)S(1)} collective-permute-done((bf16[48,1536]{1,0:T(8,128)(2,1)S(1)}, bf16[48,1536]{1,0:T(8,128)(2,1)S(1)}, u32[]{:S(2)}, u32[]{:S(2)}) %collective-permute-start.9) | collective-permute-done | bytes 147488 | tf_op jit(solution)/shard_map/ppermute | solution.py:561
  284.8 7.8 %collective-permute-done.13 = bf16[48,1536]{1,0:T(8,128)(2,1)S(1)} collective-permute-done((bf16[48,1536]{1,0:T(8,128)(2,1)S(1)}, bf16[48,1536]{1,0:T(8,128)(2,1)S(1)}, u32[]{:S(2)}, u32[]{:S(2)}) %collective-permute-start.13) | collective-permute-done | bytes 147488 | tf_op jit(solution)/shard_map/ppermute | solution.py:561
  296.9 4.7 %collective-permute-done.14 = bf16[48,1536]{1,0:T(8,128)(2,1)S(1)} collective-permute-done((bf16[48,1536]{1,0:T(8,128)(2,1)S(1)}, bf16[48,1536]{1,0:T(8,128)(2,1)S(1)}, u32[]{:S(2)}, u32[]{:S(2)}) %collective-permute-start.14) | collective-permute-done | bytes 147488 | tf_op jit(solution)/shard_map/ppermute | solution.py:561
  304.8 6.2 %collective-permute-done.15 = bf16[96,1536]{1,0:T(8,128)(2,1)S(1)} collective-permute-done((bf16[96,1536]{1,0:T(8,128)(2,1)S(1)}, bf16[96,1536]{1,0:T(8,128)(2,1)S(1)}, u32[]{:S(2)}, u32[]{:S(2)}) %collective-permute-start.15) | collective-permute-done | bytes 294944 | tf_op jit(solution)/shard_map/ppermute | solution.py:561
  317.9 6.8 %collective-permute-done.35.refs_0_ = bf16[192,1536]{1,0:T(8,128)(2,1)} collective-permute-done((bf16[192,1536]{1,0:T(8,128)(2,1)S(1)}, bf16[192,1536]{1,0:T(8,128)(2,1)}, u32[]{:S(2)}, u32[]{:S(2)}) %collective-permute-start.35) | collective-permute-done | bytes 589856 | tf_op jit(solution)/shard_map/ppermute | solution.py:561
  329.1 5.2 %spread.2 = (f32[768,3072]{1,0:T(8,128)}, f32[4,768,768]{2,1,0:T(8,128)}, f32[768,768]{1,0:T(8,128)}, f32[768,2304]{1,0:T(8,128)}) custom-call(s32[81]{0:T(128)} %concatenate.36.info, bf16[192,1536]{1,0:T(8,128)(2,1)} %copy-done.4, bf16[192,1536]{1,0:T(8,128)(2,1)} %copy-done.15, bf16[192,1536]{1,0:T(8,128)(2,1)} %pad_maximum_fusion.2.refs_2_, ...), custom_call_target="tpu_custom_call" | custom-call | tf_op jit(solution)/shard_map/spread/pallas_call | solution.py:905
  334.3 5.0 %add_convert_fusion.2 = bf16[512,768]{1,0:T(8,128)(2,1)} fusion(f32[512,768]{1,0:T(8,128)} %get-tuple-element.130, bf16[768,2304]{1,0:T(8,128)(2,1)S(1)} %copy-done, bf16[512,1536]{1,0:T(8,128)(2,1)} %get-tuple-element.133, bf16[512,768]{1,0:T(8,128)(2,1)} %get-tuple-element.131), kind=kOutput, calls=%fused_computation.8 | convolution fusion | flops 1817444352 | bytes 8257536 | tf_op jit(solution)/shard_map/dot_general | solution.py:26
  350.5 7.5 %spread.3 = (f32[768,3072]{1,0:T(8,128)}, f32[4,768,768]{2,1,0:T(8,128)}, f32[768,768]{1,0:T(8,128)}, f32[768,2304]{1,0:T(8,128)}) custom-call(s32[81]{0:T(128)} %concatenate.36.info, bf16[192,1536]{1,0:T(8,128)(2,1)} %collective-permute-done.35.refs_0_, ...), custom_call_target="tpu_custom_call", output_to_operand_aliasing={{0}: (13, {}), {1}: (14, {}), {2}: (15, {}), {3}: (16, {})} | custom-call | tf_op jit(solution)/shard_map/spread/pallas_call | solution.py:905
  358.1 4.2 %collective-permute-done.38.refs_0_ = bf16[192,1536]{1,0:T(8,128)(2,1)S(1)} collective-permute-done((bf16[192,1536]{1,0:T(8,128)(2,1)}, bf16[192,1536]{1,0:T(8,128)(2,1)S(1)}, u32[]{:S(2)}, u32[]{:S(2)}) %collective-permute-start.38) | collective-permute-done | bytes 589856 | tf_op jit(solution)/shard_map/ppermute | solution.py:561
  368.5 5.5 %spread_last.1 = (f32[768,3072]{1,0:T(8,128)}, f32[4,768,768]{2,1,0:T(8,128)}, f32[768,768]{1,0:T(8,128)}, f32[768,2304]{1,0:T(8,128)}, f32[768]{0:T(1024)}, /*i...) custom-call(s32[81]{0:T(128)} %concatenate.36.info, ...), custom_call_target="tpu_custom_call", output_to_operand_aliasing={{0}: (11, {}), {1}: (12, {}), {2}: (13, {}), {3}: (14, {})} | custom-call | tf_op jit(solution)/shard_map/spread_last/pallas_call | solution.py:931
  (205 shorter events, 103.2 us)
Async XLA Ops:
  11.2 76.2 %all-to-all-start = ((bf16[16,7,128,128]{3,2,1,0:T(8,128)(2,1)}), bf16[16,7,128,128]{3,2,1,0:T(8,128)(2,1)}, u32[]{:S(2)}, u32[]{:S(2)}) async-start(bf16[16,7,128,128]{3,2,1,0:T(8,128)(2,1)} %bitcast.17), calls=%async_computation | async-start | bytes 7340032 | tf_op jit(solution)/shard_map/all_to_all | solution.py:707
  124.3 101.3 %all-to-all-start.1 = ((bf16[16,7,128,128]{3,2,1,0:T(8,128)(2,1)}), bf16[16,7,128,128]{3,2,1,0:T(8,128)(2,1)}, u32[]{:S(2)}, u32[]{:S(2)}) async-start(bf16[16,7,128,128]{3,2,1,0:T(8,128)(2,1)} %bitcast.18), calls=%async_computation.1 | async-start | bytes 7340032 | tf_op jit(solution)/shard_map/all_to_all | solution.py:787
  155.5 11.2 %collective-permute-start.3 = (bf16[768,1536]{1,0:T(8,128)(2,1)}, bf16[768,1536]{1,0:T(8,128)(2,1)}, u32[]{:S(2)}, u32[]{:S(2)}) collective-permute-start(bf16[768,1536]{1,0:T(8,128)(2,1)} %get-tuple-element.103), channel_id=1, source_target_pairs={{0,1},{1,0},{2,3},{3,2},{4,5},{5,4},{6,7},{7,6},{8,9},{9,8},{10,11... | collective-permute-start | bytes 7077896 | tf_op jit(solution)/shard_map/ppermute | solution.py:561
  157.4 29.0 %collective-permute-start.1 = (bf16[384,1536]{1,0:T(8,128)(2,1)S(1)}, bf16[384,1536]{1,0:T(8,128)(2,1)}, u32[]{:S(2)}, u32[]{:S(2)}) collective-permute-start(bf16[384,1536]{1,0:T(8,128)(2,1)S(1)} %add_convert_fusion.1), channel_id=1, source_target_pairs={{0,16},{16,0},{1,17},{17,1},{2,18},{18,2},{3,19},{19,3},{4,20},{20... | collective-permute-start | bytes 3538952 | tf_op jit(solution)/shard_map/ppermute | solution.py:561
  166.6 23.5 %collective-permute-start.5 = (bf16[768,896]{1,0:T(8,128)(2,1)}, bf16[768,896]{1,0:T(8,128)(2,1)S(1)}, u32[]{:S(2)}, u32[]{:S(2)}) collective-permute-start(bf16[768,896]{1,0:T(8,128)(2,1)} %get-tuple-element.111), channel_id=1, source_target_pairs={{0,1},{1,0},{2,3},{3,2},{4,5},{5,4},{6,7},{7,6},{8,9},{9,8},{10,11... | collective-permute-start | bytes 4128776 | tf_op jit(solution)/shard_map/ppermute | solution.py:561
  168.2 45.9 %collective-permute-start.4 = (bf16[384,1536]{1,0:T(8,128)(2,1)S(1)}, bf16[384,1536]{1,0:T(8,128)(2,1)S(1)}, u32[]{:S(2)}, u32[]{:S(2)}) collective-permute-start(bf16[384,1536]{1,0:T(8,128)(2,1)S(1)} %add_convert_fusion), channel_id=1, source_target_pairs={{0,16},{16,0},{1,17},{17,1},{2,18},{18,2},{3,19},{19,3},{4,20},{20... | collective-permute-start | bytes 3538952 | tf_op jit(solution)/shard_map/ppermute | solution.py:561
  188.0 23.9 %collective-permute-start.2 = (bf16[192,1536]{1,0:T(8,128)(2,1)S(1)}, bf16[192,1536]{1,0:T(8,128)(2,1)S(1)}, u32[]{:S(2)}, u32[]{:S(2)}) collective-permute-start(bf16[192,1536]{1,0:T(8,128)(2,1)S(1)} %add_convert_fusion.5), channel_id=1, source_target_pairs={{0,2},{1,3},{2,0},{3,1},{4,6},{5,7},{6,4},{7,5},{8,10},{9,11},{10,... | collective-permute-start | bytes 1769480 | tf_op jit(solution)/shard_map/ppermute | solution.py:561
  190.3 35.3 %collective-permute-start.6 = (bf16[384,896]{1,0:T(8,128)(2,1)S(1)}, bf16[384,896]{1,0:T(8,128)(2,1)S(1)}, u32[]{:S(2)}, u32[]{:S(2)}) collective-permute-start(bf16[384,896]{1,0:T(8,128)(2,1)S(1)} %add_convert_fusion.3), channel_id=1, source_target_pairs={{0,16},{16,0},{1,17},{17,1},{2,18},{18,2},{3,19},{19,3},{4,20},{20... | collective-permute-start | bytes 2064392 | tf_op jit(solution)/shard_map/ppermute | solution.py:561
  225.6 14.0 %collective-permute-start.7 = (bf16[96,1536]{1,0:T(8,128)(2,1)}, bf16[96,1536]{1,0:T(8,128)(2,1)}, u32[]{:S(2)}, u32[]{:S(2)}) collective-permute-start(bf16[96,1536]{1,0:T(8,128)(2,1)} %add_convert_fusion.10), channel_id=1, source_target_pairs={{0,4},{1,5},{2,6},{3,7},{4,0},{5,1},{6,2},{7,3},{8,12},{9,13},{10,... | collective-permute-start | bytes 884744 | tf_op jit(solution)/shard_map/ppermute | solution.py:561
  229.2 14.4 %collective-permute-start.16 = (bf16[192,896]{1,0:T(8,128)(2,1)S(1)}, bf16[192,896]{1,0:T(8,128)(2,1)S(1)}, u32[]{:S(2)}, u32[]{:S(2)}) collective-permute-start(bf16[192,896]{1,0:T(8,128)(2,1)S(1)} %add_convert_fusion.6), channel_id=1, source_target_pairs={{0,2},{1,3},{2,0},{3,1},{4,6},{5,7},{6,4},{7,5},{8,10},{9,11},{10,... | collective-permute-start | bytes 1032200 | tf_op jit(solution)/shard_map/ppermute | solution.py:561
  230.7 24.1 %collective-permute-start.11 = (bf16[192,1536]{1,0:T(8,128)(2,1)}, bf16[192,1536]{1,0:T(8,128)(2,1)}, u32[]{:S(2)}, u32[]{:S(2)}) collective-permute-start(bf16[192,1536]{1,0:T(8,128)(2,1)} %add_convert_fusion.4), channel_id=1, source_target_pairs={{0,2},{1,3},{2,0},{3,1},{4,6},{5,7},{6,4},{7,5},{8,10},{9,11},{10,... | collective-permute-start | bytes 1769480 | tf_op jit(solution)/shard_map/ppermute | solution.py:561
  253.1 11.2 %collective-permute-start.18 = (bf16[48,896]{1,0:T(8,128)(2,1)S(1)}, bf16[48,896]{1,0:T(8,128)(2,1)S(1)}, u32[]{:S(2)}, u32[]{:S(2)}) collective-permute-start(bf16[48,896]{1,0:T(8,128)(2,1)S(1)} %add_convert_fusion.19), channel_id=1, source_target_pairs={{0,8},{1,9},{2,10},{3,11},{4,12},{5,13},{6,14},{7,15},{8,0},{9,1},... | collective-permute-start | bytes 258056 | tf_op jit(solution)/shard_map/ppermute | solution.py:561
  256.6 21.7 %collective-permute-start.12 = (bf16[96,1536]{1,0:T(8,128)(2,1)S(1)}, bf16[96,1536]{1,0:T(8,128)(2,1)S(1)}, u32[]{:S(2)}, u32[]{:S(2)}) collective-permute-start(bf16[96,1536]{1,0:T(8,128)(2,1)S(1)} %add_convert_fusion.9), channel_id=1, source_target_pairs={{0,4},{1,5},{2,6},{3,7},{4,0},{5,1},{6,2},{7,3},{8,12},{9,13},{10,... | collective-permute-start | bytes 884744 | tf_op jit(solution)/shard_map/ppermute | solution.py:561
  261.0 43.7 %collective-permute-start.10 = (bf16[96,1536]{1,0:T(8,128)(2,1)S(1)}, bf16[96,1536]{1,0:T(8,128)(2,1)S(1)}, u32[]{:S(2)}, u32[]{:S(2)}) collective-permute-start(bf16[96,1536]{1,0:T(8,128)(2,1)S(1)} %pad_maximum_fusion.4), channel_id=1, source_target_pairs={{0,4},{1,5},{2,6},{3,7},{4,0},{5,1},{6,2},{7,3},{8,12},{9,13},{10,... | collective-permute-start | bytes 884744 | tf_op jit(solution)/shard_map/ppermute | solution.py:561
  279.3 13.3 %collective-permute-start.13 = (bf16[48,1536]{1,0:T(8,128)(2,1)S(1)}, bf16[48,1536]{1,0:T(8,128)(2,1)S(1)}, u32[]{:S(2)}, u32[]{:S(2)}) collective-permute-start(bf16[48,1536]{1,0:T(8,128)(2,1)S(1)} %add_convert_fusion.15), channel_id=1, source_target_pairs={{0,8},{1,9},{2,10},{3,11},{4,12},{5,13},{6,14},{7,15},{8,0},{9,1},... | collective-permute-start | bytes 442376 | tf_op jit(solution)/shard_map/ppermute | solution.py:561
  282.2 12.0 %collective-permute-start.26 = (bf16[48,768]{1,0:T(8,128)(2,1)S(1)}, bf16[48,768]{1,0:T(8,128)(2,1)S(1)}, u32[]{:S(2)}, u32[]{:S(2)}) collective-permute-start(bf16[48,768]{1,0:T(8,128)(2,1)S(1)} %pad_maximum_fusion.8), channel_id=1, source_target_pairs={{0,8},{1,9},{2,10},{3,11},{4,12},{5,13},{6,14},{7,15},{8,0},{9,1},... | collective-permute-start | bytes 221192 | tf_op jit(solution)/shard_map/ppermute | solution.py:561
  316.0 12.3 %collective-permute-start.37 = (bf16[192,1664]{1,0:T(8,128)(2,1)}, bf16[192,1664]{1,0:T(8,128)(2,1)}, u32[]{:S(2)}, u32[]{:S(2)}) collective-permute-start(bf16[192,1664]{1,0:T(8,128)(2,1)} %pad_maximum_fusion.refs_4_.refs_6_), channel_id=1, source_target_pairs={{0,16},{16,0},{1,17},{17,1},{2,18},{18,2},{3,19},{19,3},{4,20},{20... | collective-permute-start | bytes 1916936 | tf_op jit(solution)/shard_map/ppermute | solution.py:561
  317.4 11.7 %collective-permute-start.34 = (bf16[192,1664]{1,0:T(8,128)(2,1)}, bf16[192,1664]{1,0:T(8,128)(2,1)}, u32[]{:S(2)}, u32[]{:S(2)}) collective-permute-start(bf16[192,1664]{1,0:T(8,128)(2,1)} %pad_maximum_fusion.refs_4_.refs_6_), channel_id=1, source_target_pairs={{0,1},{1,0},{2,3},{3,2},{4,5},{5,4},{6,7},{7,6},{8,9},{9,8},{10,11... | collective-permute-start | bytes 1916936 | tf_op jit(solution)/shard_map/ppermute | solution.py:561
  327.6 14.6 %collective-permute-start.31 = (bf16[192,1664]{1,0:T(8,128)(2,1)}, bf16[192,1664]{1,0:T(8,128)(2,1)}, u32[]{:S(2)}, u32[]{:S(2)}) collective-permute-start(bf16[192,1664]{1,0:T(8,128)(2,1)} %pad_maximum_fusion.refs_4_.refs_6_), channel_id=1, source_target_pairs={{0,4},{1,5},{2,6},{3,7},{4,0},{5,1},{6,2},{7,3},{8,12},{9,13},{10,... | collective-permute-start | bytes 1916936 | tf_op jit(solution)/shard_map/ppermute | solution.py:561
  327.6 13.1 %collective-permute-start.29 = (bf16[192,1536]{1,0:T(8,128)(2,1)S(1)}, bf16[192,1536]{1,0:T(8,128)(2,1)}, u32[]{:S(2)}, u32[]{:S(2)}) collective-permute-start(bf16[192,1536]{1,0:T(8,128)(2,1)S(1)} %pad_maximum_fusion.1.refs_0_), channel_id=1, source_target_pairs={{0,16},{16,0},{1,17},{17,1},{2,18},{18,2},{3,19},{19,3},{4,20},{20... | collective-permute-start | bytes 1769480 | tf_op jit(solution)/shard_map/ppermute | solution.py:561
  328.4 13.8 %collective-permute-start.30 = (bf16[192,1536]{1,0:T(8,128)(2,1)}, bf16[192,1536]{1,0:T(8,128)(2,1)}, u32[]{:S(2)}, u32[]{:S(2)}) collective-permute-start(bf16[192,1536]{1,0:T(8,128)(2,1)} %pad_maximum_fusion.2.refs_2_), channel_id=1, source_target_pairs={{0,2},{1,3},{2,0},{3,1},{4,6},{5,7},{6,4},{7,5},{8,10},{9,11},{10,... | collective-permute-start | bytes 1769480 | tf_op jit(solution)/shard_map/ppermute | solution.py:561
  345.2 17.8 %collective-permute-start.40 = (bf16[192,1664]{1,0:T(8,128)(2,1)}, bf16[192,1664]{1,0:T(8,128)(2,1)S(1)}, u32[]{:S(2)}, u32[]{:S(2)}) collective-permute-start(bf16[192,1664]{1,0:T(8,128)(2,1)} %collective-permute-done.37.refs_4_.refs_7_), channel_id=1, source_target_pairs={{0,4},{1,5},{2,6},{3,7},{4,0},{5,1},{6,2},{7,3},{8,12},{9,13},{10,... | collective-permute-start | bytes 1916936 | tf_op jit(solution)/shard_map/ppermute | solution.py:561
  346.9 15.4 %collective-permute-start.38 = (bf16[192,1536]{1,0:T(8,128)(2,1)}, bf16[192,1536]{1,0:T(8,128)(2,1)S(1)}, u32[]{:S(2)}, u32[]{:S(2)}) collective-permute-start(bf16[192,1536]{1,0:T(8,128)(2,1)} %collective-permute-done.35.refs_0_), channel_id=1, source_target_pairs={{0,16},{16,0},{1,17},{17,1},{2,18},{18,2},{3,19},{19,3},{4,20},{20... | collective-permute-start | bytes 1769480 | tf_op jit(solution)/shard_map/ppermute | solution.py:561
  347.8 15.3 %collective-permute-start.39 = (bf16[192,1536]{1,0:T(8,128)(2,1)}, bf16[192,1536]{1,0:T(8,128)(2,1)S(1)}, u32[]{:S(2)}, u32[]{:S(2)}) collective-permute-start(bf16[192,1536]{1,0:T(8,128)(2,1)} %collective-permute-done.36.refs_2_), channel_id=1, source_target_pairs={{0,2},{1,3},{2,0},{3,1},{4,6},{5,7},{6,4},{7,5},{8,10},{9,11},{10,... | collective-permute-start | bytes 1769480 | tf_op jit(solution)/shard_map/ppermute | solution.py:561
  (55 other events, 386.6 us)

commit v5 on v4

--- a/solution.py
+++ b/solution.py
@@ -316,7 +316,8 @@
         copy.wait()
 
 
-CHUNKS = 16
+CHUNKS = 8
+VECTORS = 16
 
 
 def chunk_rows(at, size):
@@ -375,9 +376,9 @@
         grad_q[:, lanes] = total.astype(LOW)
     attn_t[...] = attn[...].T
     tok_t[...] = tok[...].T
-    size = D // CHUNKS
+    size = D // VECTORS
     filler = jnp.zeros((size - D // LANES, LANES), F32)
-    for vector in range(CHUNKS):
+    for vector in range(VECTORS):
         rows_of = [sums[vector : vector + 1, row * LANES : (row + 1) * LANES] for row in range(D // LANES)]
         value = jnp.concatenate(rows_of + [filler]).astype(LOW)
         for side in range(2):
@@ -445,7 +446,7 @@
         value = nn(tok_t[...], jnp.concatenate(parts, axis=1)).astype(LOW)
         for part in range(2):
             buf[part, side] = value[:, part * half : (part + 1) * half]
-            place_chunks(buf.at[part, side], outs[part][side], info, sem.at[part, side], 65 if part else 1)
+            place_chunks(buf.at[part, side], outs[part][side], info, sem.at[part, side], 33 if part else 1)
     for side in range(2):
         for part in range(2):
             wait_chunks(buf.at[part, side], outs[part][side], sem.at[part, side])
@@ -534,12 +535,14 @@
     for load in loads:
         load.start()
     copies = spread_groups(groups, info, pieces, outs, staged, bufs, load_sem, sem)
-    size = D // CHUNKS
+    size = D // VECTORS
     each = CHUNKS // len(sources)
+    inside = VECTORS // CHUNKS
     for at, load in enumerate(loads):
         load.wait()
-        for chunk in range(each):
-            table[info[start + at * each + chunk]] = columns[at, chunk * size : chunk * size + 16].astype(F32)
+        for row in range(each * inside):
+            vector = info[start + at * each + row // inside] * inside + row % inside
+            table[vector] = columns[at, row * size : row * size + 16].astype(F32)
 
     def whole(vector):
         return jnp.concatenate([table[vector, row : row + 1] for row in range(D // LANES)], axis=1)
@@ -551,8 +554,9 @@
         copy.wait()
 
 
-X, Y, Z0, Z1 = ("dp", 1), ("blk", 2), ("blk", 4), ("blk", 8)
+X, Y, Z = ("dp", 1), ("blk", 2), ("blk", 4)
 CORE = ("blk", 1)
+ORDERS = ((Z, Y, X), (X, Z, Y), (Y, X, Z))
 
 
 def swap(value, bit):
@@ -563,40 +567,29 @@
 
 def further_bits(count_blk):
     bits = []
-    distance = 16
+    distance = 8
     while distance < count_blk:
         bits.append(("blk", distance))
         distance *= 2
     return bits
 
 
-def chip_bits():
-    return [(lax.axis_index(axis) // distance) % 2 for axis, distance in (X, Y, Z0, Z1)]
-
-
 def chunk_places():
-    x, y, z0, z1 = chip_bits()
-    chip = x * 8 + y * 4 + z0 * 2 + z1
+    x, y, z = [(lax.axis_index(axis) // distance) % 2 for axis, distance in (X, Y, Z)]
+    chip = x * 4 + y * 2 + z
     core = lax.axis_index("blk") % 2
     every = jnp.arange(CHUNKS, dtype=jnp.int32)
-    value = {X: 8, Y: 4, Z0: 2, Z1: 1}
+    value = {X: 4, Y: 2, Z: 1}
 
     def from_order(order):
         at = sum(((every // 2**step) % 2) * value[bit] for step, bit in enumerate(order))
         return at ^ chip
 
     placed = every ^ chip
-    x_y_swapped = placed % 4 + (placed // 8) * 4 + (placed // 4 % 2) * 8
+    x_y_swapped = placed % 2 + (placed // 4) * 2 + (placed // 2 % 2) * 4
     return jnp.concatenate(
-        [core[None], placed]
-        + [from_order(order) for order in (ORDER_X, ORDER_Y, ORDER_Z)]
-        + [x_y_swapped]
+        [core[None], placed] + [from_order(order) for order in ORDERS] + [x_y_swapped]
     )
-
-
-ORDER_X = (Z1, Z0, Y, X)
-ORDER_Y = (Z1, X, Z0, Y)
-ORDER_Z = (Z1, Y, X, Z0)
 
 
 def sum_rows(terms, low, high):
@@ -833,7 +826,7 @@
     down_step = to_send(down)
 
     returned, up_step, down_step, out_q[-1] = tie((returned, up_step, down_step, out_q[-1]))
-    up = up + [swap(up_step, Z0)]
+    up = up + [swap(up_step, Z)]
     down = down + [swap(down_step, Y)]
     out_q = scatter_steps(out_q, (Y,))
     key_give, key_keep, value_give, value_keep, grad_kv = pl.pallas_call(
@@ -857,30 +850,21 @@
     down[-1], key_give, value_give = tie((down[-1], key_give, value_give))
     key = scatter_steps([key_keep, swap(key_give, CORE)], (X, Y))
     value = scatter_steps([value_keep, swap(value_give, CORE)], (Y, X))
-    up = finish(scatter_steps(up, (Z1,)), further)
-    down = finish(scatter_steps(down, (Z0, Z1)), further)
-    out_q = finish(scatter_steps(out_q, (Z0, Z1)), further)
-    late_given = swap(jnp.concatenate([to_send(key), to_send(value)], axis=1), Z0)
+    late_given = swap(jnp.concatenate([to_send(key), to_send(value)], axis=1), Z)
     key = key + [late_given[:, :half]]
     value = value + [late_given[:, half:]]
-    late_given = swap(jnp.concatenate([to_send(key), to_send(value)], axis=1), Z1)
-    key = finish(key + [late_given[:, :half]], further)
-    value = finish(value + [late_given[:, half:]], further)
-    thirds = [
-        gather_step(third, Z1)
-        for third in (
-            up,
-            down,
-            jnp.concatenate([out_q, key, value], axis=1),
-        )
-    ]
-
-    orders = (ORDER_X, ORDER_Y, ORDER_Z)
-    starts = (17, 33, 49)
+    up = finish(up, further)
+    down = finish(scatter_steps(down, (Z,)), further)
+    out_q = finish(scatter_steps(out_q, (Z,)), further)
+    both = jnp.concatenate([sum_rows(terms, 0, terms[-1].shape[0]) for terms in (key, value)], axis=1)
+    both = finish([both.astype(LOW)], further)
+    thirds = (up, down, jnp.concatenate([out_q, both], axis=1))
+
+    starts = (9, 17, 25)
     weights = (full(D, ff), full(ff // D, D, D), full(D, D), full(D, 3 * D))
 
     def swap_all(values, step):
-        return [swap(value, order[step]) for value, order in zip(values, orders)]
+        return [swap(value, order[step]) for value, order in zip(values, ORDERS)]
 
     def spread_scratch(pieces):
         rows_each = D // CHUNKS
@@ -913,30 +897,30 @@
             name="spread",
         )(info, *pieces, *outs)
 
-    thirds = list(tie(gather_step(value, order[1]) for value, order in zip(thirds, orders)))
-    third_step = swap_all(thirds, 2)
-    fourth_step = swap_all(thirds, 3)
+    thirds = list(tie(gather_step(value, order[0]) for value, order in zip(thirds, ORDERS)))
+    third_step = swap_all(thirds, 1)
+    fourth_step = swap_all(thirds, 2)
     outs = spread(thirds, (0,))
     tied = tie((*third_step, grad_kv))
     third_step, grad_kv = list(tied[:3]), tied[3]
-    last_step = swap_all(third_step, 3)
+    last_step = swap_all(third_step, 2)
     grad_proj = jnp.concatenate([grad_q, grad_kv], axis=1)
     grad_tokens = (grad_resid + nt(grad_proj, w_qkv)).astype(LOW)
     tied = tie((*fourth_step, *outs, grad_tokens))
     fourth_step, outs, grad_tokens = list(tied[:3]), tied[3:7], tied[7]
-    outs = spread(third_step + fourth_step, (4, 8), outs)
+    outs = spread(third_step + fourth_step, (2, 4), outs)
     tied = tie((*last_step, *outs))
     last_step, outs = list(tied[:3]), tied[3:]
     pieces = with_other(last_step)
     sum_up, sum_down, sum_out, sum_qkv, *vectors = pl.pallas_call(
-        partial(spread_last_kernel, tuple((third, starts[third] + 12) for third in range(3)), starts[2]),
+        partial(spread_last_kernel, tuple((third, starts[third] + 6) for third in range(3)), starts[2]),
         out_shape=weights + (full(D),) * 8 + (full(ff),),
         in_specs=[smem] + [hbm] * (len(pieces) + 8),
         out_specs=(hbm,) * 4 + (vmem,) * 9,
         scratch_shapes=spread_scratch(pieces)
         + [
             pltpu.VMEM((4, D // 4, LANES), LOW),
-            pltpu.VMEM((CHUNKS, 16, LANES), F32),
+            pltpu.VMEM((VECTORS, 16, LANES), F32),
             pltpu.SemaphoreType.DMA((4,)),
         ],
         input_output_aliases={1 + len(pieces) + 4 + at: at for at in range(4)},

time: 379 us -> 374 us (0.987)
    convert_element_type x19 -> x15, other arithmetic: 16.7 us -> 13.4 us  [to_send(): return sum_rows(terms, rows // 2, rows).astype(LOW)]
    ppermute x50 -> x47, waiting for transfers between devices: 110 us -> 107 us  [swap(): return lax.ppermute(value, axis, [(i, i ^ distance) for i in range(size)])]
    ppermute x50 -> x47, starting transfers between devices: 41.8 us -> 42.4 us  [swap(): return lax.ppermute(value, axis, [(i, i ^ distance) for i in range(size)])]
  transfers between devices with their start and end apart: 52 -> 49, of which waited for: 27 -> 25; matrix products, arithmetic and copies ran while one was open for 8% -> 8% of each run, Pallas kernels for 13% -> 13%
where the time goes in v5:
time: 374 us; the launch traced here: 370 us
  waiting for transfers between devices  166 us (44%)
  Pallas kernels  96 us (26%)
  starting transfers between devices  67.6 us (18%)
  other arithmetic  23.7 us (6%)
  local copies, waits for them, and re-layouts  9.92 us (3%)
  matrix products  5.03 us (1%)
    ppermute x47, waiting for transfers between devices, swap(): return lax.ppermute(value, axis, [(i, i ^ distance) for i in range(size)])  107 us
    all_to_all x1, waiting for transfers between devices, per_device(): lax.all_to_all(outgoing.reshape(count_blk, capacity, CLUS, pair_width), '...  58.8 us
    ppermute x47, starting transfers between devices, swap(): return lax.ppermute(value, axis, [(i, i ^ distance) for i in range(size)])  42.4 us
    pallas_call x1, Pallas kernels, per_device(): pl.pallas_call(mid_kernel, out_shape=(low(slots, CLUS, pair_width), low(H...  36.9 us
    pallas_call x3, Pallas kernels, halves(): pl.pallas_call(kernel, out_shape=(low(D, columns), low(D, columns)) + mor...  20 us
    all_to_all x1, starting transfers between devices, per_device(): lax.all_to_all(back.reshape(count_blk, capacity, CLUS, pair_width), 'blk'...  17.6 us
    convert_element_type x15, other arithmetic, to_send(): return sum_rows(terms, rows // 2, rows).astype(LOW)  13.4 us
    pallas_call x2, Pallas kernels, spread(): pl.pallas_call(partial(spread_kernel, groups), out_shape=weights, in_spec...  12.4 us
  transfers between devices with their start and end apart: 49, of which 25 were waited for; matrix products, arithmetic and copies ran while one was open for 8% of the time, Pallas kernels for 13%

profile of v5, /device:TPU:0, one launch (start us, length us, event | category | flops | bytes accessed | tf_op | source)
XLA Modules:
  0.0 369.9 jit_solution(3515123780242685846)
XLA Ops:
  4.3 6.9 %kv_kernel.1 = bf16[112,128,128]{2,1,0:T(8,128)(2,1)} custom-call(bf16[512,768]{1,0:T(8,128)(2,1)} %tok.7, bf16[768,2304]{1,0:T(8,128)(2,1)} %w_value.1, bf16[768,2304]{1,0:T(8,128)(2,1)} %w_value.1, bf16[768]{0:T(1024)(128)(2,1)} %b_value.1, s32[1,12,512]{2,1,0:T(8,128)} %copy.68.perm, s32[16,7]{1,0:T(8,128)} %copy.74.chosen_in), custom_call_target="tpu_custom_call" | custom-call | tf_op jit(solution)/shard_map/kv_kernel/pallas_call | solution.py:685
  11.2 7.6 %all-to-all-start = ((bf16[16,7,128,128]{3,2,1,0:T(8,128)(2,1)}), bf16[16,7,128,128]{3,2,1,0:T(8,128)(2,1)}, u32[]{:S(2)}, u32[]{:S(2)}) async-start(bf16[16,7,128,128]{3,2,1,0:T(8,128)(2,1)} %bitcast.17), calls=%async_computation | async-start | bytes 7340032 | tf_op jit(solution)/shard_map/all_to_all | solution.py:700
  21.4 5.7 %q_kernel.1.queries = bf16[12,512,128]{2,1,0:T(8,128)(2,1)} custom-call(bf16[512,768]{1,0:T(8,128)(2,1)} %tok.7, bf16[768,2304]{1,0:T(8,128)(2,1)} %w_value.1, bf16[768]{0:T(1024)(128)(2,1)} %b_query.1, s32[1,12,512]{2,1,0:T(8,128)} %copy.68.perm), custom_call_target="tpu_custom_call" | custom-call | tf_op jit(solution)/shard_map/q_kernel/pallas_call | solution.py:709
  28.6 58.8 %all-to-all-done = bf16[16,7,128,128]{3,2,1,0:T(8,128)(2,1)} async-done(((bf16[16,7,128,128]{3,2,1,0:T(8,128)(2,1)}), bf16[16,7,128,128]{3,2,1,0:T(8,128)(2,1)}, u32[]{:S(2)}, u32[]{:S(2)}) %all-to-all-start) | async-done | bytes 3670048 | tf_op jit(solution)/shard_map/all_to_all | solution.py:700
  87.4 36.9 %mid_kernel.1 = (bf16[112,128,128]{2,1,0:T(8,128)(2,1)}, bf16[12,512,128]{2,1,0:T(8,128)(2,1)}, bf16[512,768]{1,0:T(8,128)(2,1)}, bf16[512,768]{1,0:T(8,128)(2,1...) custom-call(s32[96]{0:T(128)} %multiply_add_fusion.fetch, ...), custom_call_target="tpu_custom_call" | custom-call | tf_op jit(solution)/shard_map/mid_kernel/pallas_call | solution.py:736
  124.3 17.6 %all-to-all-start.1 = ((bf16[16,7,128,128]{3,2,1,0:T(8,128)(2,1)}), bf16[16,7,128,128]{3,2,1,0:T(8,128)(2,1)}, u32[]{:S(2)}, u32[]{:S(2)}) async-start(bf16[16,7,128,128]{3,2,1,0:T(8,128)(2,1)} %bitcast.18), calls=%async_computation.1 | async-start | bytes 7340032 | tf_op jit(solution)/shard_map/all_to_all | solution.py:780
  142.7 6.2 %up_kernel.1 = (bf16[768,1536]{1,0:T(8,128)(2,1)}, bf16[768,1536]{1,0:T(8,128)(2,1)}) custom-call(s32[41]{0:T(128)} %concatenate.25.info, bf16[512,768]{1,0:T(8,128)(2,1)} %get-tuple-element.93.z_low, bf16[512,3072]{1,0:T(8,128)(2,1)} %get-tuple-element.94.grad), custom_call_target="tpu_custom_call" | custom-call | flops 1 | bytes 1 | tf_op jit(solution)/shard_map/up_kernel/pallas_call | solution.py:791
  149.3 6.4 %down_kernel.1 = (bf16[768,1536]{1,0:T(8,128)(2,1)}, bf16[768,1536]{1,0:T(8,128)(2,1)}) custom-call(s32[41]{0:T(128)} %concatenate.25.info, bf16[512,3072]{1,0:T(8,128)(2,1)} %get-tuple-element.100.active, bf16[512,768]{1,0:T(8,128)(2,1)} %get-tuple-element.101.grad), custom_call_target="tpu_custom_call" | custom-call | flops 1 | bytes 1 | tf_op jit(solution)/shard_map/down_kernel/pallas_call | solution.py:791
  159.0 7.5 %out_q_kernel.1 = (bf16[768,896]{1,0:T(8,128)(2,1)}, bf16[768,896]{1,0:T(8,128)(2,1)}, bf16[512,768]{1,0:T(8,128)(2,1)}) custom-call(s32[41]{0:T(128)} %concatenate.25.info, bf16[512,768]{1,0:T(8,128)(2,1)} %get-tuple-element.106.attn, bf16[512,768]{1,0:T(8,128)(2,1)} %get-tuple-element.107.db, bf16[512,768]{1,0:T(8,128)(2,1)} %tok.7, ...), custom_call_target="tpu_custom_call" | custom-call | flops 1 | bytes 1 | tf_op jit(solution)/shard_map/out_q_kernel/pallas_call | solution.py:791
  169.1 17.3 %collective-permute-done.1 = bf16[384,1536]{1,0:T(8,128)(2,1)} collective-permute-done((bf16[384,1536]{1,0:T(8,128)(2,1)S(1)}, bf16[384,1536]{1,0:T(8,128)(2,1)}, u32[]{:S(2)}, u32[]{:S(2)}) %collective-permute-start.1) | collective-permute-done | bytes 1179680 | tf_op jit(solution)/shard_map/ppermute | solution.py:565
  191.8 20.3 %collective-permute-done.2 = bf16[192,1536]{1,0:T(8,128)(2,1)S(1)} collective-permute-done((bf16[192,1536]{1,0:T(8,128)(2,1)S(1)}, bf16[192,1536]{1,0:T(8,128)(2,1)S(1)}, u32[]{:S(2)}, u32[]{:S(2)}) %collective-permute-start.2) | collective-permute-done | bytes 589856 | tf_op jit(solution)/shard_map/ppermute | solution.py:565
  217.5 8.3 %collective-permute-done.6 = bf16[384,896]{1,0:T(8,128)(2,1)S(1)} collective-permute-done((bf16[384,896]{1,0:T(8,128)(2,1)S(1)}, bf16[384,896]{1,0:T(8,128)(2,1)S(1)}, u32[]{:S(2)}, u32[]{:S(2)}) %collective-permute-start.6) | collective-permute-done | bytes 688160 | tf_op jit(solution)/shard_map/ppermute | solution.py:565
  231.6 8.4 %key_value_kernel.1 = (bf16[768,384]{1,0:T(8,128)(2,1)}, bf16[768,384]{1,0:T(8,128)(2,1)}, bf16[768,384]{1,0:T(8,128)(2,1)}, bf16[768,384]{1,0:T(8,128)(2,1)}, bf16[512,1536]{1,0:T(8,128)(2,1)}) custom-call(s32[41]{0:T(128)} %concatenate.25.info, s32[112]{0:T(128)} %select_n.184.segment, bf16[112,128,128]{2,1,0:T(8,128)(2,1)} %bitcast.8.returned_hbm, ...), custom_call_target="tpu_custom_call" | custom-call | tf_op jit(solution)/shard_map/key_value_kernel/pallas_call | solution.py:832
  254.1 9.1 %collective-permute-done.8 = bf16[96,1536]{1,0:T(8,128)(2,1)S(1)} collective-permute-done((bf16[96,1536]{1,0:T(8,128)(2,1)S(1)}, bf16[96,1536]{1,0:T(8,128)(2,1)S(1)}, u32[]{:S(2)}, u32[]{:S(2)}) %collective-permute-start.8) | collective-permute-done | bytes 294944 | tf_op jit(solution)/shard_map/ppermute | solution.py:565
  266.7 3.5 collective-permute-done.18
  275.6 3.0 collective-permute-done.22
  287.4 9.1 %collective-permute-done.12 = bf16[96,1536]{1,0:T(8,128)(2,1)S(1)} collective-permute-done((bf16[96,1536]{1,0:T(8,128)(2,1)S(1)}, bf16[96,1536]{1,0:T(8,128)(2,1)S(1)}, u32[]{:S(2)}, u32[]{:S(2)}) %collective-permute-start.12) | collective-permute-done | bytes 294944 | tf_op jit(solution)/shard_map/ppermute | solution.py:565
  299.6 3.8 %collective-permute-done.13 = bf16[96,1536]{1,0:T(8,128)(2,1)S(1)} collective-permute-done((bf16[96,1536]{1,0:T(8,128)(2,1)S(1)}, bf16[96,1536]{1,0:T(8,128)(2,1)S(1)}, u32[]{:S(2)}, u32[]{:S(2)}) %collective-permute-start.13) | collective-permute-done | bytes 294944 | tf_op jit(solution)/shard_map/ppermute | solution.py:565
  310.3 7.8 %collective-permute-done.32.refs_0_ = bf16[192,1536]{1,0:T(8,128)(2,1)} collective-permute-done((bf16[192,1536]{1,0:T(8,128)(2,1)S(1)}, bf16[192,1536]{1,0:T(8,128)(2,1)}, u32[]{:S(2)}, u32[]{:S(2)}) %collective-permute-start.32) | collective-permute-done | bytes 589856 | tf_op jit(solution)/shard_map/ppermute | solution.py:565
  325.2 4.9 %spread.2 = (f32[768,3072]{1,0:T(8,128)}, f32[4,768,768]{2,1,0:T(8,128)}, f32[768,768]{1,0:T(8,128)}, f32[768,2304]{1,0:T(8,128)}) custom-call(s32[41]{0:T(128)} %concatenate.25.info, bf16[192,1536]{1,0:T(8,128)(2,1)} %copy-done.4, bf16[192,1536]{1,0:T(8,128)(2,1)} %copy-done.15, bf16[192,1536]{1,0:T(8,128)(2,1)} %pad_maximum_fusion.2.refs_2_, ...), custom_call_target="tpu_custom_call" | custom-call | tf_op jit(solution)/shard_map/spread/pallas_call | solution.py:889
  330.1 5.0 %add_convert_fusion.2 = bf16[512,768]{1,0:T(8,128)(2,1)} fusion(f32[512,768]{1,0:T(8,128)} %get-tuple-element.130, bf16[768,2304]{1,0:T(8,128)(2,1)S(1)} %copy-done, bf16[512,1536]{1,0:T(8,128)(2,1)} %get-tuple-element.133, bf16[512,768]{1,0:T(8,128)(2,1)} %get-tuple-element.131), kind=kOutput, calls=%fused_computation.8 | convolution fusion | flops 1817444352 | bytes 8257536 | tf_op jit(solution)/shard_map/dot_general | solution.py:26
  345.7 7.5 %spread.3 = (f32[768,3072]{1,0:T(8,128)}, f32[4,768,768]{2,1,0:T(8,128)}, f32[768,768]{1,0:T(8,128)}, f32[768,2304]{1,0:T(8,128)}) custom-call(s32[41]{0:T(128)} %concatenate.25.info, bf16[192,1536]{1,0:T(8,128)(2,1)} %collective-permute-done.32.refs_0_, ...), custom_call_target="tpu_custom_call", output_to_operand_aliasing={{0}: (13, {}), {1}: (14, {}), {2}: (15, {}), {3}: (16, {})} | custom-call | tf_op jit(solution)/shard_map/spread/pallas_call | solution.py:889
  353.3 4.2 %collective-permute-done.35.refs_0_ = bf16[192,1536]{1,0:T(8,128)(2,1)S(1)} collective-permute-done((bf16[192,1536]{1,0:T(8,128)(2,1)}, bf16[192,1536]{1,0:T(8,128)(2,1)S(1)}, u32[]{:S(2)}, u32[]{:S(2)}) %collective-permute-start.35) | collective-permute-done | bytes 589856 | tf_op jit(solution)/shard_map/ppermute | solution.py:565
  363.9 5.6 %spread_last.1 = (f32[768,3072]{1,0:T(8,128)}, f32[4,768,768]{2,1,0:T(8,128)}, f32[768,768]{1,0:T(8,128)}, f32[768,2304]{1,0:T(8,128)}, f32[768]{0:T(1024)}, /*i...) custom-call(s32[41]{0:T(128)} %concatenate.25.info, ...), custom_call_target="tpu_custom_call", output_to_operand_aliasing={{0}: (11, {}), {1}: (12, {}), {2}: (13, {}), {3}: (14, {})} | custom-call | tf_op jit(solution)/shard_map/spread_last/pallas_call | solution.py:915
  (196 shorter events, 96.5 us)
Async XLA Ops:
  11.2 76.2 %all-to-all-start = ((bf16[16,7,128,128]{3,2,1,0:T(8,128)(2,1)}), bf16[16,7,128,128]{3,2,1,0:T(8,128)(2,1)}, u32[]{:S(2)}, u32[]{:S(2)}) async-start(bf16[16,7,128,128]{3,2,1,0:T(8,128)(2,1)} %bitcast.17), calls=%async_computation | async-start | bytes 7340032 | tf_op jit(solution)/shard_map/all_to_all | solution.py:700
  124.3 101.4 %all-to-all-start.1 = ((bf16[16,7,128,128]{3,2,1,0:T(8,128)(2,1)}), bf16[16,7,128,128]{3,2,1,0:T(8,128)(2,1)}, u32[]{:S(2)}, u32[]{:S(2)}) async-start(bf16[16,7,128,128]{3,2,1,0:T(8,128)(2,1)} %bitcast.18), calls=%async_computation.1 | async-start | bytes 7340032 | tf_op jit(solution)/shard_map/all_to_all | solution.py:780
  157.5 29.0 %collective-permute-start.1 = (bf16[384,1536]{1,0:T(8,128)(2,1)S(1)}, bf16[384,1536]{1,0:T(8,128)(2,1)}, u32[]{:S(2)}, u32[]{:S(2)}) collective-permute-start(bf16[384,1536]{1,0:T(8,128)(2,1)S(1)} %add_convert_fusion.1), channel_id=1, source_target_pairs={{0,16},{16,0},{1,17},{17,1},{2,18},{18,2},{3,19},{19,3},{4,20},{20... | collective-permute-start | bytes 3538952 | tf_op jit(solution)/shard_map/ppermute | solution.py:565
  166.5 23.5 %collective-permute-start.5 = (bf16[768,896]{1,0:T(8,128)(2,1)}, bf16[768,896]{1,0:T(8,128)(2,1)S(1)}, u32[]{:S(2)}, u32[]{:S(2)}) collective-permute-start(bf16[768,896]{1,0:T(8,128)(2,1)} %get-tuple-element.111), channel_id=1, source_target_pairs={{0,1},{1,0},{2,3},{3,2},{4,5},{5,4},{6,7},{7,6},{8,9},{9,8},{10,11... | collective-permute-start | bytes 4128776 | tf_op jit(solution)/shard_map/ppermute | solution.py:565
  168.3 46.0 %collective-permute-start.4 = (bf16[384,1536]{1,0:T(8,128)(2,1)S(1)}, bf16[384,1536]{1,0:T(8,128)(2,1)S(1)}, u32[]{:S(2)}, u32[]{:S(2)}) collective-permute-start(bf16[384,1536]{1,0:T(8,128)(2,1)S(1)} %add_convert_fusion), channel_id=1, source_target_pairs={{0,16},{16,0},{1,17},{17,1},{2,18},{18,2},{3,19},{19,3},{4,20},{20... | collective-permute-start | bytes 3538952 | tf_op jit(solution)/shard_map/ppermute | solution.py:565
  188.1 24.0 %collective-permute-start.2 = (bf16[192,1536]{1,0:T(8,128)(2,1)S(1)}, bf16[192,1536]{1,0:T(8,128)(2,1)S(1)}, u32[]{:S(2)}, u32[]{:S(2)}) collective-permute-start(bf16[192,1536]{1,0:T(8,128)(2,1)S(1)} %add_convert_fusion.5), channel_id=1, source_target_pairs={{0,2},{1,3},{2,0},{3,1},{4,6},{5,7},{6,4},{7,5},{8,10},{9,11},{10,... | collective-permute-start | bytes 1769480 | tf_op jit(solution)/shard_map/ppermute | solution.py:565
  190.2 35.6 %collective-permute-start.6 = (bf16[384,896]{1,0:T(8,128)(2,1)S(1)}, bf16[384,896]{1,0:T(8,128)(2,1)S(1)}, u32[]{:S(2)}, u32[]{:S(2)}) collective-permute-start(bf16[384,896]{1,0:T(8,128)(2,1)S(1)} %add_convert_fusion.3), channel_id=1, source_target_pairs={{0,16},{16,0},{1,17},{17,1},{2,18},{18,2},{3,19},{19,3},{4,20},{20... | collective-permute-start | bytes 2064392 | tf_op jit(solution)/shard_map/ppermute | solution.py:565
  227.0 13.1 %collective-permute-start.14 = (bf16[192,896]{1,0:T(8,128)(2,1)S(1)}, bf16[192,896]{1,0:T(8,128)(2,1)}, u32[]{:S(2)}, u32[]{:S(2)}) collective-permute-start(bf16[192,896]{1,0:T(8,128)(2,1)S(1)} %add_convert_fusion.6), channel_id=1, source_target_pairs={{0,2},{1,3},{2,0},{3,1},{4,6},{5,7},{6,4},{7,5},{8,10},{9,11},{10,... | collective-permute-start | bytes 1032200 | tf_op jit(solution)/shard_map/ppermute | solution.py:565
  228.8 13.0 %collective-permute-start.7 = (bf16[96,1536]{1,0:T(8,128)(2,1)}, bf16[96,1536]{1,0:T(8,128)(2,1)}, u32[]{:S(2)}, u32[]{:S(2)}) collective-permute-start(bf16[96,1536]{1,0:T(8,128)(2,1)} %add_convert_fusion.14), channel_id=1, source_target_pairs={{0,4},{1,5},{2,6},{3,7},{4,0},{5,1},{6,2},{7,3},{8,12},{9,13},{10,... | collective-permute-start | bytes 884744 | tf_op jit(solution)/shard_map/ppermute | solution.py:565
  231.1 21.2 %collective-permute-start.10 = (bf16[192,1536]{1,0:T(8,128)(2,1)}, bf16[192,1536]{1,0:T(8,128)(2,1)}, u32[]{:S(2)}, u32[]{:S(2)}) collective-permute-start(bf16[192,1536]{1,0:T(8,128)(2,1)} %add_convert_fusion.4), channel_id=1, source_target_pairs={{0,2},{1,3},{2,0},{3,1},{4,6},{5,7},{6,4},{7,5},{8,10},{9,11},{10,... | collective-permute-start | bytes 1769480 | tf_op jit(solution)/shard_map/ppermute | solution.py:565
  243.4 19.8 %collective-permute-start.8 = (bf16[96,1536]{1,0:T(8,128)(2,1)S(1)}, bf16[96,1536]{1,0:T(8,128)(2,1)S(1)}, u32[]{:S(2)}, u32[]{:S(2)}) collective-permute-start(bf16[96,1536]{1,0:T(8,128)(2,1)S(1)} %add_convert_fusion.13), channel_id=1, source_target_pairs={{0,8},{1,9},{2,10},{3,11},{4,12},{5,13},{6,14},{7,15},{8,0},{9,1},... | collective-permute-start | bytes 884744 | tf_op jit(solution)/shard_map/ppermute | solution.py:565
  249.6 17.0 %collective-permute-start.16 = (bf16[96,896]{1,0:T(8,128)(2,1)S(1)}, bf16[96,896]{1,0:T(8,128)(2,1)S(1)}, u32[]{:S(2)}, u32[]{:S(2)}) collective-permute-start(bf16[96,896]{1,0:T(8,128)(2,1)S(1)} %add_convert_fusion.16), channel_id=1, source_target_pairs={{0,8},{1,9},{2,10},{3,11},{4,12},{5,13},{6,14},{7,15},{8,0},{9,1},... | collective-permute-start | bytes 516104 | tf_op jit(solution)/shard_map/ppermute | solution.py:565
  254.0 26.7 %collective-permute-start.11 = (bf16[96,1536]{1,0:T(8,128)(2,1)S(1)}, bf16[96,1536]{1,0:T(8,128)(2,1)S(1)}, u32[]{:S(2)}, u32[]{:S(2)}) collective-permute-start(bf16[96,1536]{1,0:T(8,128)(2,1)S(1)} %add_convert_fusion.11), channel_id=1, source_target_pairs={{0,4},{1,5},{2,6},{3,7},{4,0},{5,1},{6,2},{7,3},{8,12},{9,13},{10,... | collective-permute-start | bytes 884744 | tf_op jit(solution)/shard_map/ppermute | solution.py:565
  263.2 36.3 %collective-permute-start.9 = (bf16[96,1536]{1,0:T(8,128)(2,1)S(1)}, bf16[96,1536]{1,0:T(8,128)(2,1)S(1)}, u32[]{:S(2)}, u32[]{:S(2)}) collective-permute-start(bf16[96,1536]{1,0:T(8,128)(2,1)S(1)} %add_convert_fusion.12), channel_id=1, source_target_pairs={{0,4},{1,5},{2,6},{3,7},{4,0},{5,1},{6,2},{7,3},{8,12},{9,13},{10,... | collective-permute-start | bytes 884744 | tf_op jit(solution)/shard_map/ppermute | solution.py:565
  282.0 14.5 %collective-permute-start.12 = (bf16[96,1536]{1,0:T(8,128)(2,1)S(1)}, bf16[96,1536]{1,0:T(8,128)(2,1)S(1)}, u32[]{:S(2)}, u32[]{:S(2)}) collective-permute-start(bf16[96,1536]{1,0:T(8,128)(2,1)S(1)} %add_convert_fusion.10), channel_id=1, source_target_pairs={{0,8},{1,9},{2,10},{3,11},{4,12},{5,13},{6,14},{7,15},{8,0},{9,1},... | collective-permute-start | bytes 884744 | tf_op jit(solution)/shard_map/ppermute | solution.py:565
  284.9 13.2 %collective-permute-start.24 = (bf16[96,768]{1,0:T(8,128)(2,1)S(1)}, bf16[96,768]{1,0:T(8,128)(2,1)S(1)}, u32[]{:S(2)}, u32[]{:S(2)}) collective-permute-start(bf16[96,768]{1,0:T(8,128)(2,1)S(1)} %pad_maximum_fusion.5), channel_id=1, source_target_pairs={{0,8},{1,9},{2,10},{3,11},{4,12},{5,13},{6,14},{7,15},{8,0},{9,1},... | collective-permute-start | bytes 442376 | tf_op jit(solution)/shard_map/ppermute | solution.py:565
  307.5 16.7 %collective-permute-start.34 = (bf16[192,1664]{1,0:T(8,128)(2,1)}, bf16[192,1664]{1,0:T(8,128)(2,1)}, u32[]{:S(2)}, u32[]{:S(2)}) collective-permute-start(bf16[192,1664]{1,0:T(8,128)(2,1)} %pad_maximum_fusion.refs_4_.refs_6_), channel_id=1, source_target_pairs={{0,16},{16,0},{1,17},{17,1},{2,18},{18,2},{3,19},{19,3},{4,20},{20... | collective-permute-start | bytes 1916936 | tf_op jit(solution)/shard_map/ppermute | solution.py:565
  309.8 15.4 %collective-permute-start.31 = (bf16[192,1664]{1,0:T(8,128)(2,1)}, bf16[192,1664]{1,0:T(8,128)(2,1)}, u32[]{:S(2)}, u32[]{:S(2)}) collective-permute-start(bf16[192,1664]{1,0:T(8,128)(2,1)} %pad_maximum_fusion.refs_4_.refs_6_), channel_id=1, source_target_pairs={{0,1},{1,0},{2,3},{3,2},{4,5},{5,4},{6,7},{7,6},{8,9},{9,8},{10,11... | collective-permute-start | bytes 1916936 | tf_op jit(solution)/shard_map/ppermute | solution.py:565
  320.7 17.2 %collective-permute-start.28 = (bf16[192,1664]{1,0:T(8,128)(2,1)}, bf16[192,1664]{1,0:T(8,128)(2,1)}, u32[]{:S(2)}, u32[]{:S(2)}) collective-permute-start(bf16[192,1664]{1,0:T(8,128)(2,1)} %pad_maximum_fusion.refs_4_.refs_6_), channel_id=1, source_target_pairs={{0,4},{1,5},{2,6},{3,7},{4,0},{5,1},{6,2},{7,3},{8,12},{9,13},{10,... | collective-permute-start | bytes 1916936 | tf_op jit(solution)/shard_map/ppermute | solution.py:565
  323.1 13.9 %collective-permute-start.26 = (bf16[192,1536]{1,0:T(8,128)(2,1)S(1)}, bf16[192,1536]{1,0:T(8,128)(2,1)}, u32[]{:S(2)}, u32[]{:S(2)}) collective-permute-start(bf16[192,1536]{1,0:T(8,128)(2,1)S(1)} %pad_maximum_fusion.1.refs_0_), channel_id=1, source_target_pairs={{0,16},{16,0},{1,17},{17,1},{2,18},{18,2},{3,19},{19,3},{4,20},{20... | collective-permute-start | bytes 1769480 | tf_op jit(solution)/shard_map/ppermute | solution.py:565
  324.2 13.8 %collective-permute-start.27 = (bf16[192,1536]{1,0:T(8,128)(2,1)}, bf16[192,1536]{1,0:T(8,128)(2,1)}, u32[]{:S(2)}, u32[]{:S(2)}) collective-permute-start(bf16[192,1536]{1,0:T(8,128)(2,1)} %pad_maximum_fusion.2.refs_2_), channel_id=1, source_target_pairs={{0,2},{1,3},{2,0},{3,1},{4,6},{5,7},{6,4},{7,5},{8,10},{9,11},{10,... | collective-permute-start | bytes 1769480 | tf_op jit(solution)/shard_map/ppermute | solution.py:565
  341.0 17.3 %collective-permute-start.37 = (bf16[192,1664]{1,0:T(8,128)(2,1)}, bf16[192,1664]{1,0:T(8,128)(2,1)S(1)}, u32[]{:S(2)}, u32[]{:S(2)}) collective-permute-start(bf16[192,1664]{1,0:T(8,128)(2,1)} %collective-permute-done.34.refs_4_.refs_7_), channel_id=1, source_target_pairs={{0,4},{1,5},{2,6},{3,7},{4,0},{5,1},{6,2},{7,3},{8,12},{9,13},{10,... | collective-permute-start | bytes 1916936 | tf_op jit(solution)/shard_map/ppermute | solution.py:565
  342.2 15.4 %collective-permute-start.35 = (bf16[192,1536]{1,0:T(8,128)(2,1)}, bf16[192,1536]{1,0:T(8,128)(2,1)S(1)}, u32[]{:S(2)}, u32[]{:S(2)}) collective-permute-start(bf16[192,1536]{1,0:T(8,128)(2,1)} %collective-permute-done.32.refs_0_), channel_id=1, source_target_pairs={{0,16},{16,0},{1,17},{17,1},{2,18},{18,2},{3,19},{19,3},{4,20},{20... | collective-permute-start | bytes 1769480 | tf_op jit(solution)/shard_map/ppermute | solution.py:565
  343.0 15.3 %collective-permute-start.36 = (bf16[192,1536]{1,0:T(8,128)(2,1)}, bf16[192,1536]{1,0:T(8,128)(2,1)S(1)}, u32[]{:S(2)}, u32[]{:S(2)}) collective-permute-start(bf16[192,1536]{1,0:T(8,128)(2,1)} %collective-permute-done.33.refs_2_), channel_id=1, source_target_pairs={{0,2},{1,3},{2,0},{3,1},{4,6},{5,7},{6,4},{7,5},{8,10},{9,11},{10,... | collective-permute-start | bytes 1769480 | tf_op jit(solution)/shard_map/ppermute | solution.py:565
  (52 other events, 408.4 us)

commit v6 on v5

--- a/solution.py
+++ b/solution.py
@@ -496,28 +496,21 @@
     return targets
 
 
-def spread_groups(groups, info, pieces, outs, staged, bufs, load_sem, sem):
+def spread_groups(groups, info, pieces, outs, bufs, sem):
     w_up, w_down, w_out, w_qkv = outs
     half = w_up.shape[1] // 2
     routes = (up_targets(w_up, half), down_targets(w_down, half), attention_targets(w_out, w_qkv))
-    loads = []
-    for at, (source, target) in enumerate(zip(pieces, staged)):
-        loads.append(pltpu.make_async_copy(source, target, load_sem.at[at]))
-        loads[-1].start()
     copies = []
     for at, (third, start) in enumerate(groups):
-        for load in loads[2 * at : 2 * at + 2]:
-            load.wait()
-        copies += spread_start(info, start, staged[2 * at : 2 * at + 2], routes[third], bufs[at], sem.at[at])
+        copies += spread_start(info, start, pieces[2 * at : 2 * at + 2], routes[third], bufs[at], sem.at[at])
     return copies
 
 
 def spread_kernel(groups, info, *refs):
     pairs = len(groups)
-    pieces, scratch = refs[: 2 * pairs], refs[-3 * pairs - 2 :]
-    outs = refs[-3 * pairs - 6 : -3 * pairs - 2]
-    staged, bufs = scratch[: 2 * pairs], scratch[2 * pairs : 3 * pairs]
-    for copy in spread_groups(groups, info, pieces, outs, staged, bufs, *scratch[3 * pairs :]):
+    pieces, bufs, sem = refs[: 2 * pairs], refs[-pairs - 1 : -1], refs[-1]
+    outs = refs[-pairs - 5 : -pairs - 1]
+    for copy in spread_groups(groups, info, pieces, outs, bufs, sem):
         copy.wait()
 
 
@@ -526,15 +519,15 @@
     pieces, sources = refs[: 2 * pairs], refs[2 * pairs : 2 * pairs + 4]
     rest = refs[2 * pairs + 8 :]
     outs, vectors, rest = rest[:4], rest[4:13], rest[13:]
-    staged, bufs = rest[: 2 * pairs], rest[2 * pairs : 3 * pairs]
-    load_sem, sem, columns, table, column_sem = rest[3 * pairs :]
+    bufs = rest[:pairs]
+    sem, columns, table, column_sem = rest[pairs:]
     loads = [
         pltpu.make_async_copy(source.at[:, D : D + LANES], columns.at[at], column_sem.at[at])
         for at, source in enumerate(sources)
     ]
     for load in loads:
         load.start()
-    copies = spread_groups(groups, info, pieces, outs, staged, bufs, load_sem, sem)
+    copies = spread_groups(groups, info, pieces, outs, bufs, sem)
     size = D // VECTORS
     each = CHUNKS // len(sources)
     inside = VECTORS // CHUNKS
@@ -869,15 +862,11 @@
     def spread_scratch(pieces):
         rows_each = D // CHUNKS
         return (
-            [pltpu.VMEM(piece.shape, LOW) for piece in pieces]
-            + [
+            [
                 pltpu.VMEM((2, piece.shape[0] // rows_each, rows_each, piece.shape[1]), F32)
                 for piece in pieces[::2]
             ]
-            + [
-                pltpu.SemaphoreType.DMA((len(pieces),)),
-                pltpu.SemaphoreType.DMA((len(pieces) // 2,)),
-            ]
+            + [pltpu.SemaphoreType.DMA((len(pieces) // 2,))]
         )
 
     def with_other(sets):
@@ -889,11 +878,11 @@
         return pl.pallas_call(
             partial(spread_kernel, groups),
             out_shape=weights,
-            in_specs=[smem] + [hbm] * (len(pieces) + len(outs)),
+            in_specs=[smem] + [vmem] * len(pieces) + [hbm] * len(outs),
             out_specs=(hbm,) * 4,
             scratch_shapes=spread_scratch(pieces),
             input_output_aliases={1 + len(pieces) + at: at for at in range(len(outs))},
-            compiler_params=params(),
+            compiler_params=params(32),
             name="spread",
         )(info, *pieces, *outs)
 
@@ -915,7 +904,7 @@
     sum_up, sum_down, sum_out, sum_qkv, *vectors = pl.pallas_call(
         partial(spread_last_kernel, tuple((third, starts[third] + 6) for third in range(3)), starts[2]),
         out_shape=weights + (full(D),) * 8 + (full(ff),),
-        in_specs=[smem] + [hbm] * (len(pieces) + 8),
+        in_specs=[smem] + [vmem] * len(pieces) + [hbm] * 8,
         out_specs=(hbm,) * 4 + (vmem,) * 9,
         scratch_shapes=spread_scratch(pieces)
         + [
@@ -924,7 +913,7 @@
             pltpu.SemaphoreType.DMA((4,)),
         ],
         input_output_aliases={1 + len(pieces) + 4 + at: at for at in range(4)},
-        compiler_params=params(),
+        compiler_params=params(24),
         name="spread_last",
     )(info, *pieces, thirds[2], third_step[2], fourth_step[2], last_step[2], *outs)
     return (

time: 374 us -> 368 us (0.984)
  waiting for transfers between devices: 166 us -> 174 us
  Pallas kernels: 96 us -> 91.3 us
  local copies, waits for them, and re-layouts: 9.92 us -> 6.03 us
    ppermute x47, waiting for transfers between devices: 107 us -> 115 us  [swap(): return lax.ppermute(value, axis, [(i, i ^ distance) for i in range(size)])]
    unnamed x57 -> x37, local copies, waits for them, and re-layouts: 7.07 us -> 3.25 us
  transfers between devices with their start and end apart: 49 -> 49, of which waited for: 25 -> 25; matrix products, arithmetic and copies ran while one was open for 8% -> 7% of each run, Pallas kernels for 13% -> 12%
where the time goes in v6:
time: 368 us; the launch traced here: 364 us
  waiting for transfers between devices  174 us (47%)
  Pallas kernels  91.3 us (25%)
  starting transfers between devices  66.2 us (18%)
  other arithmetic  21.9 us (6%)
  local copies, waits for them, and re-layouts  6.03 us (2%)
    ppermute x47, waiting for transfers between devices, swap(): return lax.ppermute(value, axis, [(i, i ^ distance) for i in range(size)])  115 us
    all_to_all x1, waiting for transfers between devices, per_device(): lax.all_to_all(outgoing.reshape(count_blk, capacity, CLUS, pair_width), '...  58.9 us
    ppermute x47, starting transfers between devices, swap(): return lax.ppermute(value, axis, [(i, i ^ distance) for i in range(size)])  41 us
    pallas_call x1, Pallas kernels, per_device(): pl.pallas_call(mid_kernel, out_shape=(low(slots, CLUS, pair_width), low(H...  36.9 us
    pallas_call x3, Pallas kernels, halves(): pl.pallas_call(kernel, out_shape=(low(D, columns), low(D, columns)) + mor...  20.1 us
    all_to_all x1, starting transfers between devices, per_device(): lax.all_to_all(back.reshape(count_blk, capacity, CLUS, pair_width), 'blk'...  17.6 us
    convert_element_type x15, other arithmetic, to_send(): return sum_rows(terms, rows // 2, rows).astype(LOW)  13.4 us
    pallas_call x2, Pallas kernels, spread(): pl.pallas_call(partial(spread_kernel, groups), out_shape=weights, in_spec...  9.1 us
  transfers between devices with their start and end apart: 49, of which 25 were waited for; matrix products, arithmetic and copies ran while one was open for 7% of the time, Pallas kernels for 12%

profile of v6, /device:TPU:0, one launch (start us, length us, event | category | flops | bytes accessed | tf_op | source)
XLA Modules:
  0.0 364.3 jit_solution(14798179431097502333)
XLA Ops:
  4.3 6.9 %kv_kernel.1 = bf16[112,128,128]{2,1,0:T(8,128)(2,1)} custom-call(bf16[512,768]{1,0:T(8,128)(2,1)} %tok.7, bf16[768,2304]{1,0:T(8,128)(2,1)} %w_value.1, bf16[768,2304]{1,0:T(8,128)(2,1)} %w_value.1, bf16[768]{0:T(1024)(128)(2,1)} %b_value.1, s32[1,12,512]{2,1,0:T(8,128)} %copy.68.perm, s32[16,7]{1,0:T(8,128)} %copy.74.chosen_in), custom_call_target="tpu_custom_call" | custom-call | tf_op jit(solution)/shard_map/kv_kernel/pallas_call | solution.py:678
  11.2 7.6 %all-to-all-start = ((bf16[16,7,128,128]{3,2,1,0:T(8,128)(2,1)}), bf16[16,7,128,128]{3,2,1,0:T(8,128)(2,1)}, u32[]{:S(2)}, u32[]{:S(2)}) async-start(bf16[16,7,128,128]{3,2,1,0:T(8,128)(2,1)} %bitcast.17), calls=%async_computation | async-start | bytes 7340032 | tf_op jit(solution)/shard_map/all_to_all | solution.py:693
  21.4 5.7 %q_kernel.1.queries = bf16[12,512,128]{2,1,0:T(8,128)(2,1)} custom-call(bf16[512,768]{1,0:T(8,128)(2,1)} %tok.7, bf16[768,2304]{1,0:T(8,128)(2,1)} %w_value.1, bf16[768]{0:T(1024)(128)(2,1)} %b_query.1, s32[1,12,512]{2,1,0:T(8,128)} %copy.68.perm), custom_call_target="tpu_custom_call" | custom-call | tf_op jit(solution)/shard_map/q_kernel/pallas_call | solution.py:702
  28.6 58.9 %all-to-all-done = bf16[16,7,128,128]{3,2,1,0:T(8,128)(2,1)} async-done(((bf16[16,7,128,128]{3,2,1,0:T(8,128)(2,1)}), bf16[16,7,128,128]{3,2,1,0:T(8,128)(2,1)}, u32[]{:S(2)}, u32[]{:S(2)}) %all-to-all-start) | async-done | bytes 3670048 | tf_op jit(solution)/shard_map/all_to_all | solution.py:693
  87.4 36.9 %mid_kernel.1 = (bf16[112,128,128]{2,1,0:T(8,128)(2,1)}, bf16[12,512,128]{2,1,0:T(8,128)(2,1)}, bf16[512,768]{1,0:T(8,128)(2,1)}, bf16[512,768]{1,0:T(8,128)(2,1...) custom-call(s32[96]{0:T(128)} %multiply_add_fusion.fetch, ...), custom_call_target="tpu_custom_call" | custom-call | tf_op jit(solution)/shard_map/mid_kernel/pallas_call | solution.py:729
  124.3 17.6 %all-to-all-start.1 = ((bf16[16,7,128,128]{3,2,1,0:T(8,128)(2,1)}), bf16[16,7,128,128]{3,2,1,0:T(8,128)(2,1)}, u32[]{:S(2)}, u32[]{:S(2)}) async-start(bf16[16,7,128,128]{3,2,1,0:T(8,128)(2,1)} %bitcast.18), calls=%async_computation.1 | async-start | bytes 7340032 | tf_op jit(solution)/shard_map/all_to_all | solution.py:773
  142.6 6.2 %up_kernel.1 = (bf16[768,1536]{1,0:T(8,128)(2,1)}, bf16[768,1536]{1,0:T(8,128)(2,1)}) custom-call(s32[41]{0:T(128)} %concatenate.25.info, bf16[512,768]{1,0:T(8,128)(2,1)} %get-tuple-element.93.z_low, bf16[512,3072]{1,0:T(8,128)(2,1)} %get-tuple-element.94.grad), custom_call_target="tpu_custom_call" | custom-call | flops 1 | bytes 1 | tf_op jit(solution)/shard_map/up_kernel/pallas_call | solution.py:784
  149.2 6.4 %down_kernel.1 = (bf16[768,1536]{1,0:T(8,128)(2,1)}, bf16[768,1536]{1,0:T(8,128)(2,1)}) custom-call(s32[41]{0:T(128)} %concatenate.25.info, bf16[512,3072]{1,0:T(8,128)(2,1)} %get-tuple-element.100.active, bf16[512,768]{1,0:T(8,128)(2,1)} %get-tuple-element.101.grad), custom_call_target="tpu_custom_call" | custom-call | flops 1 | bytes 1 | tf_op jit(solution)/shard_map/down_kernel/pallas_call | solution.py:784
  159.0 7.5 %out_q_kernel.1 = (bf16[768,896]{1,0:T(8,128)(2,1)}, bf16[768,896]{1,0:T(8,128)(2,1)}, bf16[512,768]{1,0:T(8,128)(2,1)}) custom-call(s32[41]{0:T(128)} %concatenate.25.info, bf16[512,768]{1,0:T(8,128)(2,1)} %get-tuple-element.106.attn, bf16[512,768]{1,0:T(8,128)(2,1)} %get-tuple-element.107.db, bf16[512,768]{1,0:T(8,128)(2,1)} %tok.7, ...), custom_call_target="tpu_custom_call" | custom-call | flops 1 | bytes 1 | tf_op jit(solution)/shard_map/out_q_kernel/pallas_call | solution.py:784
  169.0 17.4 %collective-permute-done.1 = bf16[384,1536]{1,0:T(8,128)(2,1)} collective-permute-done((bf16[384,1536]{1,0:T(8,128)(2,1)S(1)}, bf16[384,1536]{1,0:T(8,128)(2,1)}, u32[]{:S(2)}, u32[]{:S(2)}) %collective-permute-start.1) | collective-permute-done | bytes 1179680 | tf_op jit(solution)/shard_map/ppermute | solution.py:558
  191.7 20.3 %collective-permute-done.2 = bf16[192,1536]{1,0:T(8,128)(2,1)S(1)} collective-permute-done((bf16[192,1536]{1,0:T(8,128)(2,1)S(1)}, bf16[192,1536]{1,0:T(8,128)(2,1)S(1)}, u32[]{:S(2)}, u32[]{:S(2)}) %collective-permute-start.2) | collective-permute-done | bytes 589856 | tf_op jit(solution)/shard_map/ppermute | solution.py:558
  217.4 8.3 %collective-permute-done.6 = bf16[384,896]{1,0:T(8,128)(2,1)S(1)} collective-permute-done((bf16[384,896]{1,0:T(8,128)(2,1)S(1)}, bf16[384,896]{1,0:T(8,128)(2,1)S(1)}, u32[]{:S(2)}, u32[]{:S(2)}) %collective-permute-start.6) | collective-permute-done | bytes 688160 | tf_op jit(solution)/shard_map/ppermute | solution.py:558
  231.6 8.4 %key_value_kernel.1 = (bf16[768,384]{1,0:T(8,128)(2,1)}, bf16[768,384]{1,0:T(8,128)(2,1)}, bf16[768,384]{1,0:T(8,128)(2,1)}, bf16[768,384]{1,0:T(8,128)(2,1)}, bf16[512,1536]{1,0:T(8,128)(2,1)}) custom-call(s32[41]{0:T(128)} %concatenate.25.info, s32[112]{0:T(128)} %select_n.184.segment, bf16[112,128,128]{2,1,0:T(8,128)(2,1)} %bitcast.8.returned_hbm, ...), custom_call_target="tpu_custom_call" | custom-call | tf_op jit(solution)/shard_map/key_value_kernel/pallas_call | solution.py:825
  254.0 9.1 %collective-permute-done.8 = bf16[96,1536]{1,0:T(8,128)(2,1)S(1)} collective-permute-done((bf16[96,1536]{1,0:T(8,128)(2,1)S(1)}, bf16[96,1536]{1,0:T(8,128)(2,1)S(1)}, u32[]{:S(2)}, u32[]{:S(2)}) %collective-permute-start.8) | collective-permute-done | bytes 294944 | tf_op jit(solution)/shard_map/ppermute | solution.py:558
  266.7 3.5 collective-permute-done.18
  275.5 3.2 collective-permute-done.22
  287.3 9.1 %collective-permute-done.12 = bf16[96,1536]{1,0:T(8,128)(2,1)S(1)} collective-permute-done((bf16[96,1536]{1,0:T(8,128)(2,1)S(1)}, bf16[96,1536]{1,0:T(8,128)(2,1)S(1)}, u32[]{:S(2)}, u32[]{:S(2)}) %collective-permute-start.12) | collective-permute-done | bytes 294944 | tf_op jit(solution)/shard_map/ppermute | solution.py:558
  299.5 3.7 %collective-permute-done.13 = bf16[96,1536]{1,0:T(8,128)(2,1)S(1)} collective-permute-done((bf16[96,1536]{1,0:T(8,128)(2,1)S(1)}, bf16[96,1536]{1,0:T(8,128)(2,1)S(1)}, u32[]{:S(2)}, u32[]{:S(2)}) %collective-permute-start.13) | collective-permute-done | bytes 294944 | tf_op jit(solution)/shard_map/ppermute | solution.py:558
  309.5 8.4 %collective-permute-done.32.refs_0_ = bf16[192,1536]{1,0:T(8,128)(2,1)S(1)} collective-permute-done((bf16[192,1536]{1,0:T(8,128)(2,1)S(1)}, bf16[192,1536]{1,0:T(8,128)(2,1)S(1)}, u32[]{:S(2)}, u32[]{:S(2)}) %collective-permute-start.32) | collective-permute-done | bytes 589856 | tf_op jit(solution)/shard_map/ppermute | solution.py:558
  323.1 3.5 spread.2
  329.5 5.5 %collective-permute-done.26.refs_6_ = bf16[192,1536]{1,0:T(8,128)(2,1)S(1)} collective-permute-done((bf16[192,1536]{1,0:T(8,128)(2,1)S(1)}, bf16[192,1536]{1,0:T(8,128)(2,1)S(1)}, u32[]{:S(2)}, u32[]{:S(2)}) %collective-permute-start.26) | collective-permute-done | bytes 589856 | tf_op jit(solution)/shard_map/ppermute | solution.py:558
  342.4 5.6 %spread.3 = (f32[768,3072]{1,0:T(8,128)}, f32[4,768,768]{2,1,0:T(8,128)}, f32[768,768]{1,0:T(8,128)}, f32[768,2304]{1,0:T(8,128)}) custom-call(s32[41]{0:T(128)S(1)} %copy-done, bf16[192,1536]{1,0:T(8,128)(2,1)S(1)} %collective-permute-done.32.refs_0_, ...), custom_call_target="tpu_custom_call", output_to_operand_aliasing={{0}: (13, {}), {1}: (14, {}), {2}: (15, {}), {3}: (16, {})} | custom-call | tf_op jit(solution)/shard_map/spread/pallas_call | solution.py:878
  348.0 7.1 %collective-permute-done.35.refs_0_ = bf16[192,1536]{1,0:T(8,128)(2,1)S(1)} collective-permute-done((bf16[192,1536]{1,0:T(8,128)(2,1)S(1)}, bf16[192,1536]{1,0:T(8,128)(2,1)S(1)}, u32[]{:S(2)}, u32[]{:S(2)}) %collective-permute-start.35) | collective-permute-done | bytes 589856 | tf_op jit(solution)/shard_map/ppermute | solution.py:558
  359.7 4.2 %spread_last.1 = (f32[768,3072]{1,0:T(8,128)}, f32[4,768,768]{2,1,0:T(8,128)}, f32[768,768]{1,0:T(8,128)}, f32[768,2304]{1,0:T(8,128)}, f32[768]{0:T(1024)}, /*i...) custom-call(s32[41]{0:T(128)S(1)} %copy-done, ...), custom_call_target="tpu_custom_call", output_to_operand_aliasing={{0}: (11, {}), {1}: (12, {}), {2}: (13, {}), {3}: (14, {})} | custom-call | tf_op jit(solution)/shard_map/spread_last/pallas_call | solution.py:904
  (176 shorter events, 91.7 us)
Async XLA Ops:
  11.2 76.2 %all-to-all-start = ((bf16[16,7,128,128]{3,2,1,0:T(8,128)(2,1)}), bf16[16,7,128,128]{3,2,1,0:T(8,128)(2,1)}, u32[]{:S(2)}, u32[]{:S(2)}) async-start(bf16[16,7,128,128]{3,2,1,0:T(8,128)(2,1)} %bitcast.17), calls=%async_computation | async-start | bytes 7340032 | tf_op jit(solution)/shard_map/all_to_all | solution.py:693
  124.3 101.3 %all-to-all-start.1 = ((bf16[16,7,128,128]{3,2,1,0:T(8,128)(2,1)}), bf16[16,7,128,128]{3,2,1,0:T(8,128)(2,1)}, u32[]{:S(2)}, u32[]{:S(2)}) async-start(bf16[16,7,128,128]{3,2,1,0:T(8,128)(2,1)} %bitcast.18), calls=%async_computation.1 | async-start | bytes 7340032 | tf_op jit(solution)/shard_map/all_to_all | solution.py:773
  157.4 29.0 %collective-permute-start.1 = (bf16[384,1536]{1,0:T(8,128)(2,1)S(1)}, bf16[384,1536]{1,0:T(8,128)(2,1)}, u32[]{:S(2)}, u32[]{:S(2)}) collective-permute-start(bf16[384,1536]{1,0:T(8,128)(2,1)S(1)} %add_convert_fusion.1), channel_id=1, source_target_pairs={{0,16},{16,0},{1,17},{17,1},{2,18},{18,2},{3,19},{19,3},{4,20},{20... | collective-permute-start | bytes 3538952 | tf_op jit(solution)/shard_map/ppermute | solution.py:558
  166.5 23.5 %collective-permute-start.5 = (bf16[768,896]{1,0:T(8,128)(2,1)}, bf16[768,896]{1,0:T(8,128)(2,1)S(1)}, u32[]{:S(2)}, u32[]{:S(2)}) collective-permute-start(bf16[768,896]{1,0:T(8,128)(2,1)} %get-tuple-element.111), channel_id=1, source_target_pairs={{0,1},{1,0},{2,3},{3,2},{4,5},{5,4},{6,7},{7,6},{8,9},{9,8},{10,11... | collective-permute-start | bytes 4128776 | tf_op jit(solution)/shard_map/ppermute | solution.py:558
  168.2 46.0 %collective-permute-start.4 = (bf16[384,1536]{1,0:T(8,128)(2,1)S(1)}, bf16[384,1536]{1,0:T(8,128)(2,1)S(1)}, u32[]{:S(2)}, u32[]{:S(2)}) collective-permute-start(bf16[384,1536]{1,0:T(8,128)(2,1)S(1)} %add_convert_fusion), channel_id=1, source_target_pairs={{0,16},{16,0},{1,17},{17,1},{2,18},{18,2},{3,19},{19,3},{4,20},{20... | collective-permute-start | bytes 3538952 | tf_op jit(solution)/shard_map/ppermute | solution.py:558
  188.0 24.0 %collective-permute-start.2 = (bf16[192,1536]{1,0:T(8,128)(2,1)S(1)}, bf16[192,1536]{1,0:T(8,128)(2,1)S(1)}, u32[]{:S(2)}, u32[]{:S(2)}) collective-permute-start(bf16[192,1536]{1,0:T(8,128)(2,1)S(1)} %add_convert_fusion.5), channel_id=1, source_target_pairs={{0,2},{1,3},{2,0},{3,1},{4,6},{5,7},{6,4},{7,5},{8,10},{9,11},{10,... | collective-permute-start | bytes 1769480 | tf_op jit(solution)/shard_map/ppermute | solution.py:558
  190.2 35.5 %collective-permute-start.6 = (bf16[384,896]{1,0:T(8,128)(2,1)S(1)}, bf16[384,896]{1,0:T(8,128)(2,1)S(1)}, u32[]{:S(2)}, u32[]{:S(2)}) collective-permute-start(bf16[384,896]{1,0:T(8,128)(2,1)S(1)} %add_convert_fusion.3), channel_id=1, source_target_pairs={{0,16},{16,0},{1,17},{17,1},{2,18},{18,2},{3,19},{19,3},{4,20},{20... | collective-permute-start | bytes 2064392 | tf_op jit(solution)/shard_map/ppermute | solution.py:558
  226.9 13.1 %collective-permute-start.14 = (bf16[192,896]{1,0:T(8,128)(2,1)S(1)}, bf16[192,896]{1,0:T(8,128)(2,1)}, u32[]{:S(2)}, u32[]{:S(2)}) collective-permute-start(bf16[192,896]{1,0:T(8,128)(2,1)S(1)} %add_convert_fusion.6), channel_id=1, source_target_pairs={{0,2},{1,3},{2,0},{3,1},{4,6},{5,7},{6,4},{7,5},{8,10},{9,11},{10,... | collective-permute-start | bytes 1032200 | tf_op jit(solution)/shard_map/ppermute | solution.py:558
  228.8 13.0 %collective-permute-start.7 = (bf16[96,1536]{1,0:T(8,128)(2,1)}, bf16[96,1536]{1,0:T(8,128)(2,1)}, u32[]{:S(2)}, u32[]{:S(2)}) collective-permute-start(bf16[96,1536]{1,0:T(8,128)(2,1)} %add_convert_fusion.14), channel_id=1, source_target_pairs={{0,4},{1,5},{2,6},{3,7},{4,0},{5,1},{6,2},{7,3},{8,12},{9,13},{10,... | collective-permute-start | bytes 884744 | tf_op jit(solution)/shard_map/ppermute | solution.py:558
  231.0 21.2 %collective-permute-start.10 = (bf16[192,1536]{1,0:T(8,128)(2,1)}, bf16[192,1536]{1,0:T(8,128)(2,1)}, u32[]{:S(2)}, u32[]{:S(2)}) collective-permute-start(bf16[192,1536]{1,0:T(8,128)(2,1)} %add_convert_fusion.4), channel_id=1, source_target_pairs={{0,2},{1,3},{2,0},{3,1},{4,6},{5,7},{6,4},{7,5},{8,10},{9,11},{10,... | collective-permute-start | bytes 1769480 | tf_op jit(solution)/shard_map/ppermute | solution.py:558
  243.3 19.8 %collective-permute-start.8 = (bf16[96,1536]{1,0:T(8,128)(2,1)S(1)}, bf16[96,1536]{1,0:T(8,128)(2,1)S(1)}, u32[]{:S(2)}, u32[]{:S(2)}) collective-permute-start(bf16[96,1536]{1,0:T(8,128)(2,1)S(1)} %add_convert_fusion.13), channel_id=1, source_target_pairs={{0,8},{1,9},{2,10},{3,11},{4,12},{5,13},{6,14},{7,15},{8,0},{9,1},... | collective-permute-start | bytes 884744 | tf_op jit(solution)/shard_map/ppermute | solution.py:558
  249.6 17.0 %collective-permute-start.16 = (bf16[96,896]{1,0:T(8,128)(2,1)S(1)}, bf16[96,896]{1,0:T(8,128)(2,1)S(1)}, u32[]{:S(2)}, u32[]{:S(2)}) collective-permute-start(bf16[96,896]{1,0:T(8,128)(2,1)S(1)} %add_convert_fusion.16), channel_id=1, source_target_pairs={{0,8},{1,9},{2,10},{3,11},{4,12},{5,13},{6,14},{7,15},{8,0},{9,1},... | collective-permute-start | bytes 516104 | tf_op jit(solution)/shard_map/ppermute | solution.py:558
  253.9 26.8 %collective-permute-start.11 = (bf16[96,1536]{1,0:T(8,128)(2,1)S(1)}, bf16[96,1536]{1,0:T(8,128)(2,1)S(1)}, u32[]{:S(2)}, u32[]{:S(2)}) collective-permute-start(bf16[96,1536]{1,0:T(8,128)(2,1)S(1)} %add_convert_fusion.11), channel_id=1, source_target_pairs={{0,4},{1,5},{2,6},{3,7},{4,0},{5,1},{6,2},{7,3},{8,12},{9,13},{10,... | collective-permute-start | bytes 884744 | tf_op jit(solution)/shard_map/ppermute | solution.py:558
  263.2 36.3 %collective-permute-start.9 = (bf16[96,1536]{1,0:T(8,128)(2,1)S(1)}, bf16[96,1536]{1,0:T(8,128)(2,1)S(1)}, u32[]{:S(2)}, u32[]{:S(2)}) collective-permute-start(bf16[96,1536]{1,0:T(8,128)(2,1)S(1)} %add_convert_fusion.12), channel_id=1, source_target_pairs={{0,4},{1,5},{2,6},{3,7},{4,0},{5,1},{6,2},{7,3},{8,12},{9,13},{10,... | collective-permute-start | bytes 884744 | tf_op jit(solution)/shard_map/ppermute | solution.py:558
  282.0 14.4 %collective-permute-start.12 = (bf16[96,1536]{1,0:T(8,128)(2,1)S(1)}, bf16[96,1536]{1,0:T(8,128)(2,1)S(1)}, u32[]{:S(2)}, u32[]{:S(2)}) collective-permute-start(bf16[96,1536]{1,0:T(8,128)(2,1)S(1)} %add_convert_fusion.10), channel_id=1, source_target_pairs={{0,8},{1,9},{2,10},{3,11},{4,12},{5,13},{6,14},{7,15},{8,0},{9,1},... | collective-permute-start | bytes 884744 | tf_op jit(solution)/shard_map/ppermute | solution.py:558
  284.8 13.3 %collective-permute-start.24 = (bf16[96,768]{1,0:T(8,128)(2,1)S(1)}, bf16[96,768]{1,0:T(8,128)(2,1)S(1)}, u32[]{:S(2)}, u32[]{:S(2)}) collective-permute-start(bf16[96,768]{1,0:T(8,128)(2,1)S(1)} %pad_maximum_fusion.5), channel_id=1, source_target_pairs={{0,8},{1,9},{2,10},{3,11},{4,12},{5,13},{6,14},{7,15},{8,0},{9,1},... | collective-permute-start | bytes 442376 | tf_op jit(solution)/shard_map/ppermute | solution.py:558
  307.5 14.7 %collective-permute-start.34 = (bf16[192,1664]{1,0:T(8,128)(2,1)S(1)}, bf16[192,1664]{1,0:T(8,128)(2,1)S(1)}, u32[]{:S(2)}, u32[]{:S(2)}) collective-permute-start(bf16[192,1664]{1,0:T(8,128)(2,1)S(1)} %pad_maximum_fusion.refs_4_.refs_6_), channel_id=1, source_target_pairs={{0,16},{16,0},{1,17},{17,1},{2,18},{18,2},{3,19},{19,3},{4,20},{20... | collective-permute-start | bytes 1916936 | tf_op jit(solution)/shard_map/ppermute | solution.py:558
  309.0 14.1 %collective-permute-start.31 = (bf16[192,1664]{1,0:T(8,128)(2,1)S(1)}, bf16[192,1664]{1,0:T(8,128)(2,1)S(1)}, u32[]{:S(2)}, u32[]{:S(2)}) collective-permute-start(bf16[192,1664]{1,0:T(8,128)(2,1)S(1)} %pad_maximum_fusion.refs_4_.refs_6_), channel_id=1, source_target_pairs={{0,1},{1,0},{2,3},{3,2},{4,5},{5,4},{6,7},{7,6},{8,9},{9,8},{10,11... | collective-permute-start | bytes 1916936 | tf_op jit(solution)/shard_map/ppermute | solution.py:558
  319.7 16.3 %collective-permute-start.28 = (bf16[192,1664]{1,0:T(8,128)(2,1)S(1)}, bf16[192,1664]{1,0:T(8,128)(2,1)S(1)}, u32[]{:S(2)}, u32[]{:S(2)}) collective-permute-start(bf16[192,1664]{1,0:T(8,128)(2,1)S(1)} %pad_maximum_fusion.refs_4_.refs_6_), channel_id=1, source_target_pairs={{0,4},{1,5},{2,6},{3,7},{4,0},{5,1},{6,2},{7,3},{8,12},{9,13},{10,... | collective-permute-start | bytes 1916936 | tf_op jit(solution)/shard_map/ppermute | solution.py:558
  321.3 13.7 %collective-permute-start.26 = (bf16[192,1536]{1,0:T(8,128)(2,1)S(1)}, bf16[192,1536]{1,0:T(8,128)(2,1)S(1)}, u32[]{:S(2)}, u32[]{:S(2)}) collective-permute-start(bf16[192,1536]{1,0:T(8,128)(2,1)S(1)} %pad_maximum_fusion.1.refs_0_), channel_id=1, source_target_pairs={{0,16},{16,0},{1,17},{17,1},{2,18},{18,2},{3,19},{19,3},{4,20},{20... | collective-permute-start | bytes 1769480 | tf_op jit(solution)/shard_map/ppermute | solution.py:558
  322.2 13.8 %collective-permute-start.27 = (bf16[192,1536]{1,0:T(8,128)(2,1)S(1)}, bf16[192,1536]{1,0:T(8,128)(2,1)S(1)}, u32[]{:S(2)}, u32[]{:S(2)}) collective-permute-start(bf16[192,1536]{1,0:T(8,128)(2,1)S(1)} %pad_maximum_fusion.2.refs_2_), channel_id=1, source_target_pairs={{0,2},{1,3},{2,0},{3,1},{4,6},{5,7},{6,4},{7,5},{8,10},{9,11},{10,... | collective-permute-start | bytes 1769480 | tf_op jit(solution)/shard_map/ppermute | solution.py:558
  338.8 17.1 %collective-permute-start.37 = (bf16[192,1664]{1,0:T(8,128)(2,1)S(1)}, bf16[192,1664]{1,0:T(8,128)(2,1)S(1)}, u32[]{:S(2)}, u32[]{:S(2)}) collective-permute-start(bf16[192,1664]{1,0:T(8,128)(2,1)S(1)} %collective-permute-done.34.refs_4_.refs_7_), channel_id=1, source_target_pairs={{0,4},{1,5},{2,6},{3,7},{4,0},{5,1},{6,2},{7,3},{8,12},{9,13},{10,... | collective-permute-start | bytes 1916936 | tf_op jit(solution)/shard_map/ppermute | solution.py:558
  340.0 15.1 %collective-permute-start.35 = (bf16[192,1536]{1,0:T(8,128)(2,1)S(1)}, bf16[192,1536]{1,0:T(8,128)(2,1)S(1)}, u32[]{:S(2)}, u32[]{:S(2)}) collective-permute-start(bf16[192,1536]{1,0:T(8,128)(2,1)S(1)} %collective-permute-done.32.refs_0_), channel_id=1, source_target_pairs={{0,16},{16,0},{1,17},{17,1},{2,18},{18,2},{3,19},{19,3},{4,20},{20... | collective-permute-start | bytes 1769480 | tf_op jit(solution)/shard_map/ppermute | solution.py:558
  340.5 15.4 %collective-permute-start.36 = (bf16[192,1536]{1,0:T(8,128)(2,1)S(1)}, bf16[192,1536]{1,0:T(8,128)(2,1)S(1)}, u32[]{:S(2)}, u32[]{:S(2)}) collective-permute-start(bf16[192,1536]{1,0:T(8,128)(2,1)S(1)} %collective-permute-done.33.refs_2_), channel_id=1, source_target_pairs={{0,2},{1,3},{2,0},{3,1},{4,6},{5,7},{6,4},{7,5},{8,10},{9,11},{10,... | collective-permute-start | bytes 1769480 | tf_op jit(solution)/shard_map/ppermute | solution.py:558
  (42 other events, 457.7 us)

commit v7 on v6

--- a/solution.py
+++ b/solution.py
@@ -47,15 +47,15 @@
 
 
 def columns_of(perm, rows):
-    local = lax.rem(perm, rows)
-    return jnp.concatenate([local, local[: 16 - HEADS]]).T
+    every = [perm[head] for head in range(HEADS)] + [perm[0]] * (16 - HEADS)
+    return lax.rem(jnp.concatenate(every), rows).T
 
 
 def kv_kernel(tok, w_key, w_value, b_value, perm, chosen_in, out, blocks, chosen, chosen_sem, sem):
     fetch = pltpu.make_async_copy(chosen_in, chosen, chosen_sem)
     fetch.start()
     rows = tok.shape[0]
-    order = columns_of(perm[0], rows)
+    order = columns_of(perm, rows)
     per_dev = rows // CLUS
     place = lax.broadcasted_iota(jnp.int32, (rows, rows), 1)
     left = left_half((rows, 2 * HEAD_DIM))
@@ -90,7 +90,7 @@
 
 def q_kernel(tok, w_query, b_query, perm, out):
     rows = tok.shape[0]
-    order = columns_of(perm[0], rows)
+    order = columns_of(perm, rows)
     place = lax.broadcasted_iota(jnp.int32, (rows, rows), 1)
     left = left_half((rows, 2 * HEAD_DIM))
     inputs = tok[...]
@@ -118,7 +118,7 @@
     fetch, queries, arrived, order, inverse, tok_hbm, cot_hbm,
     b_out, gain_one, shift_one, b_up, b_down, gain_two, shift_two, w_out_hbm, w_up_hbm, w_down_hbm,
     back, dq_out, attn_out, z_out, active_out, du_out, df_out, db_out, dh1_out, layer_out, sums,
-    kv, probs, attn, mixed, w_out, w_up, w_down, hidden, z_full, n_one, r_one, z_low, active, slope,
+    kv, probs, attn, mixed, w_out, w_up, w_down, hidden, n_one, r_one, z_low, active, slope,
     dh2, df, db, d_out, dh1, final, dq, tok, cot, kv_sem, w_sem, out_sem, back_sem,
 ):
     rows = tok_hbm.shape[0]
@@ -193,7 +193,6 @@
         n_one[at, :] = unit
         r_one[at, :] = scale
         z_low[at, :] = z.astype(LOW)
-        z_full[at, :] = z
         hidden[at, :] = z + as_row(b_down)
 
     store(z_low, z_out)
@@ -647,6 +646,7 @@
     slots = count_blk * capacity
     pair_width = 2 * HEAD_DIM
     ff = w_up.shape[1]
+    perm = cluster_perm.reshape(HEADS, 1, rows)
     local_order = cluster_perm[0] - my_index * rows
     order_rows = local_order[:, None, :]
 
@@ -689,7 +689,7 @@
         ],
         compiler_params=params(),
         name="kv_kernel",
-    )(tokens, w_qkv, w_qkv, b_value, cluster_perm, chosen)
+    )(tokens, w_qkv, w_qkv, b_value, perm, chosen)
     arrived = lax.all_to_all(
         outgoing.reshape(count_blk, capacity, CLUS, pair_width),
         "blk",
@@ -707,7 +707,7 @@
         out_specs=vmem,
         compiler_params=params(),
         name="q_kernel",
-    )(tokens, w_qkv, b_query, cluster_perm)
+    )(tokens, w_qkv, b_query, perm)
     filled = jnp.any(matches, axis=1)
     segment = jnp.where(filled, chosen, blocks).reshape(-1)
     my_source = lax.dynamic_index_in_dim(wanted, my_index, 0, keepdims=False) // per_dev
@@ -743,7 +743,6 @@
             pltpu.VMEM((D, D), LOW),
             pltpu.VMEM((D, ff), LOW),
             pltpu.VMEM((ff, D), LOW),
-            pltpu.VMEM((rows, D), F32),
             pltpu.VMEM((rows, D), F32),
             pltpu.VMEM((rows, D), F32),
             pltpu.VMEM((rows, 1), F32),

time: 368 us -> 367 us (level)
  no operation moved by 1% of the time
where the time goes in v7:
time: 367 us; the launch traced here: 363 us
  waiting for transfers between devices  173 us (47%)
  Pallas kernels  91.3 us (25%)
  starting transfers between devices  66.9 us (18%)
  other arithmetic  21.9 us (6%)
  local copies, waits for them, and re-layouts  4.69 us (1%)
    ppermute x47, waiting for transfers between devices, swap(): return lax.ppermute(value, axis, [(i, i ^ distance) for i in range(size)])  114 us
    all_to_all x1, waiting for transfers between devices, per_device(): lax.all_to_all(outgoing.reshape(count_blk, capacity, CLUS, pair_width), '...  58.8 us
    ppermute x47, starting transfers between devices, swap(): return lax.ppermute(value, axis, [(i, i ^ distance) for i in range(size)])  41.7 us
    pallas_call x1, Pallas kernels, per_device(): pl.pallas_call(mid_kernel, out_shape=(low(slots, CLUS, pair_width), low(H...  36.9 us
    pallas_call x3, Pallas kernels, halves(): pl.pallas_call(kernel, out_shape=(low(D, columns), low(D, columns)) + mor...  20.1 us
    all_to_all x1, starting transfers between devices, per_device(): lax.all_to_all(back.reshape(count_blk, capacity, CLUS, pair_width), 'blk'...  17.6 us
    convert_element_type x15, other arithmetic, to_send(): return sum_rows(terms, rows // 2, rows).astype(LOW)  13.4 us
    pallas_call x2, Pallas kernels, spread(): pl.pallas_call(partial(spread_kernel, groups), out_shape=weights, in_spec...  9.1 us
  transfers between devices with their start and end apart: 49, of which 25 were waited for; matrix products, arithmetic and copies ran while one was open for 7% of the time, Pallas kernels for 12%

profile of v7, /device:TPU:0, one launch (start us, length us, event | category | flops | bytes accessed | tf_op | source)
XLA Modules:
  0.0 362.8 jit_solution(4217785798819410621)
XLA Ops:
  2.9 6.9 %kv_kernel.1 = bf16[112,128,128]{2,1,0:T(8,128)(2,1)} custom-call(bf16[512,768]{1,0:T(8,128)(2,1)} %tok.7, bf16[768,2304]{1,0:T(8,128)(2,1)} %w_value.1, bf16[768,2304]{1,0:T(8,128)(2,1)} %w_value.1, bf16[768]{0:T(1024)(128)(2,1)} %b_value.1, s32[12,1,512]{2,1,0:T(1,128)} %bitcast.21, s32[16,7]{1,0:T(8,128)} %copy.64.chosen_in), custom_call_target="tpu_custom_call" | custom-call | tf_op jit(solution)/shard_map/kv_kernel/pallas_call | solution.py:678
  9.9 7.6 %all-to-all-start = ((bf16[16,7,128,128]{3,2,1,0:T(8,128)(2,1)}), bf16[16,7,128,128]{3,2,1,0:T(8,128)(2,1)}, u32[]{:S(2)}, u32[]{:S(2)}) async-start(bf16[16,7,128,128]{3,2,1,0:T(8,128)(2,1)} %bitcast.17), calls=%async_computation | async-start | bytes 7340032 | tf_op jit(solution)/shard_map/all_to_all | solution.py:693
  20.0 5.8 %q_kernel.1.queries = bf16[12,512,128]{2,1,0:T(8,128)(2,1)} custom-call(bf16[512,768]{1,0:T(8,128)(2,1)} %tok.7, bf16[768,2304]{1,0:T(8,128)(2,1)} %w_value.1, bf16[768]{0:T(1024)(128)(2,1)} %b_query.1, s32[12,1,512]{2,1,0:T(1,128)} %bitcast.22), custom_call_target="tpu_custom_call" | custom-call | tf_op jit(solution)/shard_map/q_kernel/pallas_call | solution.py:702
  27.3 58.8 %all-to-all-done = bf16[16,7,128,128]{3,2,1,0:T(8,128)(2,1)} async-done(((bf16[16,7,128,128]{3,2,1,0:T(8,128)(2,1)}), bf16[16,7,128,128]{3,2,1,0:T(8,128)(2,1)}, u32[]{:S(2)}, u32[]{:S(2)}) %all-to-all-start) | async-done | bytes 3670048 | tf_op jit(solution)/shard_map/all_to_all | solution.py:693
  86.1 36.9 %mid_kernel.1 = (bf16[112,128,128]{2,1,0:T(8,128)(2,1)}, bf16[12,512,128]{2,1,0:T(8,128)(2,1)}, bf16[512,768]{1,0:T(8,128)(2,1)}, bf16[512,768]{1,0:T(8,128)(2,1...) custom-call(s32[96]{0:T(128)} %multiply_add_fusion.fetch, ...), custom_call_target="tpu_custom_call" | custom-call | tf_op jit(solution)/shard_map/mid_kernel/pallas_call | solution.py:729
  123.0 17.6 %all-to-all-start.1 = ((bf16[16,7,128,128]{3,2,1,0:T(8,128)(2,1)}), bf16[16,7,128,128]{3,2,1,0:T(8,128)(2,1)}, u32[]{:S(2)}, u32[]{:S(2)}) async-start(bf16[16,7,128,128]{3,2,1,0:T(8,128)(2,1)} %bitcast.18), calls=%async_computation.1 | async-start | bytes 7340032 | tf_op jit(solution)/shard_map/all_to_all | solution.py:772
  141.3 6.2 %up_kernel.1 = (bf16[768,1536]{1,0:T(8,128)(2,1)}, bf16[768,1536]{1,0:T(8,128)(2,1)}) custom-call(s32[41]{0:T(128)} %concatenate.25.info, bf16[512,768]{1,0:T(8,128)(2,1)} %get-tuple-element.93.z_low, bf16[512,3072]{1,0:T(8,128)(2,1)} %get-tuple-element.94.grad), custom_call_target="tpu_custom_call" | custom-call | flops 1 | bytes 1 | tf_op jit(solution)/shard_map/up_kernel/pallas_call | solution.py:783
  147.9 6.4 %down_kernel.1 = (bf16[768,1536]{1,0:T(8,128)(2,1)}, bf16[768,1536]{1,0:T(8,128)(2,1)}) custom-call(s32[41]{0:T(128)} %concatenate.25.info, bf16[512,3072]{1,0:T(8,128)(2,1)} %get-tuple-element.100.active, bf16[512,768]{1,0:T(8,128)(2,1)} %get-tuple-element.101.grad), custom_call_target="tpu_custom_call" | custom-call | flops 1 | bytes 1 | tf_op jit(solution)/shard_map/down_kernel/pallas_call | solution.py:783
  157.6 7.5 %out_q_kernel.1 = (bf16[768,896]{1,0:T(8,128)(2,1)}, bf16[768,896]{1,0:T(8,128)(2,1)}, bf16[512,768]{1,0:T(8,128)(2,1)}) custom-call(s32[41]{0:T(128)} %concatenate.25.info, bf16[512,768]{1,0:T(8,128)(2,1)} %get-tuple-element.106.attn, bf16[512,768]{1,0:T(8,128)(2,1)} %get-tuple-element.107.db, bf16[512,768]{1,0:T(8,128)(2,1)} %tok.7, ...), custom_call_target="tpu_custom_call" | custom-call | flops 1 | bytes 1 | tf_op jit(solution)/shard_map/out_q_kernel/pallas_call | solution.py:783
  167.7 17.4 %collective-permute-done.1 = bf16[384,1536]{1,0:T(8,128)(2,1)} collective-permute-done((bf16[384,1536]{1,0:T(8,128)(2,1)S(1)}, bf16[384,1536]{1,0:T(8,128)(2,1)}, u32[]{:S(2)}, u32[]{:S(2)}) %collective-permute-start.1) | collective-permute-done | bytes 1179680 | tf_op jit(solution)/shard_map/ppermute | solution.py:557
  190.4 20.3 %collective-permute-done.2 = bf16[192,1536]{1,0:T(8,128)(2,1)S(1)} collective-permute-done((bf16[192,1536]{1,0:T(8,128)(2,1)S(1)}, bf16[192,1536]{1,0:T(8,128)(2,1)S(1)}, u32[]{:S(2)}, u32[]{:S(2)}) %collective-permute-start.2) | collective-permute-done | bytes 589856 | tf_op jit(solution)/shard_map/ppermute | solution.py:557
  216.0 8.3 %collective-permute-done.6 = bf16[384,896]{1,0:T(8,128)(2,1)S(1)} collective-permute-done((bf16[384,896]{1,0:T(8,128)(2,1)S(1)}, bf16[384,896]{1,0:T(8,128)(2,1)S(1)}, u32[]{:S(2)}, u32[]{:S(2)}) %collective-permute-start.6) | collective-permute-done | bytes 688160 | tf_op jit(solution)/shard_map/ppermute | solution.py:557
  230.2 8.4 %key_value_kernel.1 = (bf16[768,384]{1,0:T(8,128)(2,1)}, bf16[768,384]{1,0:T(8,128)(2,1)}, bf16[768,384]{1,0:T(8,128)(2,1)}, bf16[768,384]{1,0:T(8,128)(2,1)}, bf16[512,1536]{1,0:T(8,128)(2,1)}) custom-call(s32[41]{0:T(128)} %concatenate.25.info, s32[112]{0:T(128)} %select_n.184.segment, bf16[112,128,128]{2,1,0:T(8,128)(2,1)} %bitcast.8.returned_hbm, ...), custom_call_target="tpu_custom_call" | custom-call | tf_op jit(solution)/shard_map/key_value_kernel/pallas_call | solution.py:824
  252.8 8.9 %collective-permute-done.8 = bf16[96,1536]{1,0:T(8,128)(2,1)S(1)} collective-permute-done((bf16[96,1536]{1,0:T(8,128)(2,1)S(1)}, bf16[96,1536]{1,0:T(8,128)(2,1)S(1)}, u32[]{:S(2)}, u32[]{:S(2)}) %collective-permute-start.8) | collective-permute-done | bytes 294944 | tf_op jit(solution)/shard_map/ppermute | solution.py:557
  265.3 3.5 collective-permute-done.18
  274.2 3.0 collective-permute-done.22
  285.9 9.2 %collective-permute-done.12 = bf16[96,1536]{1,0:T(8,128)(2,1)S(1)} collective-permute-done((bf16[96,1536]{1,0:T(8,128)(2,1)S(1)}, bf16[96,1536]{1,0:T(8,128)(2,1)S(1)}, u32[]{:S(2)}, u32[]{:S(2)}) %collective-permute-start.12) | collective-permute-done | bytes 294944 | tf_op jit(solution)/shard_map/ppermute | solution.py:557
  298.3 3.7 %collective-permute-done.13 = bf16[96,1536]{1,0:T(8,128)(2,1)S(1)} collective-permute-done((bf16[96,1536]{1,0:T(8,128)(2,1)S(1)}, bf16[96,1536]{1,0:T(8,128)(2,1)S(1)}, u32[]{:S(2)}, u32[]{:S(2)}) %collective-permute-start.13) | collective-permute-done | bytes 294944 | tf_op jit(solution)/shard_map/ppermute | solution.py:557
  308.1 8.5 %collective-permute-done.32.refs_0_ = bf16[192,1536]{1,0:T(8,128)(2,1)S(1)} collective-permute-done((bf16[192,1536]{1,0:T(8,128)(2,1)S(1)}, bf16[192,1536]{1,0:T(8,128)(2,1)S(1)}, u32[]{:S(2)}, u32[]{:S(2)}) %collective-permute-start.32) | collective-permute-done | bytes 589856 | tf_op jit(solution)/shard_map/ppermute | solution.py:557
  321.8 3.5 spread.2
  328.2 5.5 %collective-permute-done.26.refs_6_ = bf16[192,1536]{1,0:T(8,128)(2,1)S(1)} collective-permute-done((bf16[192,1536]{1,0:T(8,128)(2,1)S(1)}, bf16[192,1536]{1,0:T(8,128)(2,1)S(1)}, u32[]{:S(2)}, u32[]{:S(2)}) %collective-permute-start.26) | collective-permute-done | bytes 589856 | tf_op jit(solution)/shard_map/ppermute | solution.py:557
  340.9 5.6 %spread.3 = (f32[768,3072]{1,0:T(8,128)}, f32[4,768,768]{2,1,0:T(8,128)}, f32[768,768]{1,0:T(8,128)}, f32[768,2304]{1,0:T(8,128)}) custom-call(s32[41]{0:T(128)S(1)} %copy-done, bf16[192,1536]{1,0:T(8,128)(2,1)S(1)} %collective-permute-done.32.refs_0_, ...), custom_call_target="tpu_custom_call", output_to_operand_aliasing={{0}: (13, {}), {1}: (14, {}), {2}: (15, {}), {3}: (16, {})} | custom-call | tf_op jit(solution)/shard_map/spread/pallas_call | solution.py:877
  346.5 7.5 %collective-permute-done.35.refs_0_ = bf16[192,1536]{1,0:T(8,128)(2,1)S(1)} collective-permute-done((bf16[192,1536]{1,0:T(8,128)(2,1)S(1)}, bf16[192,1536]{1,0:T(8,128)(2,1)S(1)}, u32[]{:S(2)}, u32[]{:S(2)}) %collective-permute-start.35) | collective-permute-done | bytes 589856 | tf_op jit(solution)/shard_map/ppermute | solution.py:557
  358.2 4.2 %spread_last.1 = (f32[768,3072]{1,0:T(8,128)}, f32[4,768,768]{2,1,0:T(8,128)}, f32[768,768]{1,0:T(8,128)}, f32[768,2304]{1,0:T(8,128)}, f32[768]{0:T(1024)}, /*i...) custom-call(s32[41]{0:T(128)S(1)} %copy-done, ...), custom_call_target="tpu_custom_call", output_to_operand_aliasing={{0}: (11, {}), {1}: (12, {}), {2}: (13, {}), {3}: (14, {})} | custom-call | tf_op jit(solution)/shard_map/spread_last/pallas_call | solution.py:903
  (177 shorter events, 90.0 us)
Async XLA Ops:
  9.9 76.2 %all-to-all-start = ((bf16[16,7,128,128]{3,2,1,0:T(8,128)(2,1)}), bf16[16,7,128,128]{3,2,1,0:T(8,128)(2,1)}, u32[]{:S(2)}, u32[]{:S(2)}) async-start(bf16[16,7,128,128]{3,2,1,0:T(8,128)(2,1)} %bitcast.17), calls=%async_computation | async-start | bytes 7340032 | tf_op jit(solution)/shard_map/all_to_all | solution.py:693
  123.0 101.4 %all-to-all-start.1 = ((bf16[16,7,128,128]{3,2,1,0:T(8,128)(2,1)}), bf16[16,7,128,128]{3,2,1,0:T(8,128)(2,1)}, u32[]{:S(2)}, u32[]{:S(2)}) async-start(bf16[16,7,128,128]{3,2,1,0:T(8,128)(2,1)} %bitcast.18), calls=%async_computation.1 | async-start | bytes 7340032 | tf_op jit(solution)/shard_map/all_to_all | solution.py:772
  156.1 29.0 %collective-permute-start.1 = (bf16[384,1536]{1,0:T(8,128)(2,1)S(1)}, bf16[384,1536]{1,0:T(8,128)(2,1)}, u32[]{:S(2)}, u32[]{:S(2)}) collective-permute-start(bf16[384,1536]{1,0:T(8,128)(2,1)S(1)} %add_convert_fusion.1), channel_id=1, source_target_pairs={{0,16},{16,0},{1,17},{17,1},{2,18},{18,2},{3,19},{19,3},{4,20},{20... | collective-permute-start | bytes 3538952 | tf_op jit(solution)/shard_map/ppermute | solution.py:557
  165.1 23.5 %collective-permute-start.5 = (bf16[768,896]{1,0:T(8,128)(2,1)}, bf16[768,896]{1,0:T(8,128)(2,1)S(1)}, u32[]{:S(2)}, u32[]{:S(2)}) collective-permute-start(bf16[768,896]{1,0:T(8,128)(2,1)} %get-tuple-element.111), channel_id=1, source_target_pairs={{0,1},{1,0},{2,3},{3,2},{4,5},{5,4},{6,7},{7,6},{8,9},{9,8},{10,11... | collective-permute-start | bytes 4128776 | tf_op jit(solution)/shard_map/ppermute | solution.py:557
  166.9 46.0 %collective-permute-start.4 = (bf16[384,1536]{1,0:T(8,128)(2,1)S(1)}, bf16[384,1536]{1,0:T(8,128)(2,1)S(1)}, u32[]{:S(2)}, u32[]{:S(2)}) collective-permute-start(bf16[384,1536]{1,0:T(8,128)(2,1)S(1)} %add_convert_fusion), channel_id=1, source_target_pairs={{0,16},{16,0},{1,17},{17,1},{2,18},{18,2},{3,19},{19,3},{4,20},{20... | collective-permute-start | bytes 3538952 | tf_op jit(solution)/shard_map/ppermute | solution.py:557
  186.6 24.0 %collective-permute-start.2 = (bf16[192,1536]{1,0:T(8,128)(2,1)S(1)}, bf16[192,1536]{1,0:T(8,128)(2,1)S(1)}, u32[]{:S(2)}, u32[]{:S(2)}) collective-permute-start(bf16[192,1536]{1,0:T(8,128)(2,1)S(1)} %add_convert_fusion.5), channel_id=1, source_target_pairs={{0,2},{1,3},{2,0},{3,1},{4,6},{5,7},{6,4},{7,5},{8,10},{9,11},{10,... | collective-permute-start | bytes 1769480 | tf_op jit(solution)/shard_map/ppermute | solution.py:557
  188.8 35.5 %collective-permute-start.6 = (bf16[384,896]{1,0:T(8,128)(2,1)S(1)}, bf16[384,896]{1,0:T(8,128)(2,1)S(1)}, u32[]{:S(2)}, u32[]{:S(2)}) collective-permute-start(bf16[384,896]{1,0:T(8,128)(2,1)S(1)} %add_convert_fusion.3), channel_id=1, source_target_pairs={{0,16},{16,0},{1,17},{17,1},{2,18},{18,2},{3,19},{19,3},{4,20},{20... | collective-permute-start | bytes 2064392 | tf_op jit(solution)/shard_map/ppermute | solution.py:557
  225.6 13.0 %collective-permute-start.14 = (bf16[192,896]{1,0:T(8,128)(2,1)S(1)}, bf16[192,896]{1,0:T(8,128)(2,1)}, u32[]{:S(2)}, u32[]{:S(2)}) collective-permute-start(bf16[192,896]{1,0:T(8,128)(2,1)S(1)} %add_convert_fusion.6), channel_id=1, source_target_pairs={{0,2},{1,3},{2,0},{3,1},{4,6},{5,7},{6,4},{7,5},{8,10},{9,11},{10,... | collective-permute-start | bytes 1032200 | tf_op jit(solution)/shard_map/ppermute | solution.py:557
  227.4 13.0 %collective-permute-start.7 = (bf16[96,1536]{1,0:T(8,128)(2,1)}, bf16[96,1536]{1,0:T(8,128)(2,1)}, u32[]{:S(2)}, u32[]{:S(2)}) collective-permute-start(bf16[96,1536]{1,0:T(8,128)(2,1)} %add_convert_fusion.14), channel_id=1, source_target_pairs={{0,4},{1,5},{2,6},{3,7},{4,0},{5,1},{6,2},{7,3},{8,12},{9,13},{10,... | collective-permute-start | bytes 884744 | tf_op jit(solution)/shard_map/ppermute | solution.py:557
  229.7 21.3 %collective-permute-start.10 = (bf16[192,1536]{1,0:T(8,128)(2,1)}, bf16[192,1536]{1,0:T(8,128)(2,1)}, u32[]{:S(2)}, u32[]{:S(2)}) collective-permute-start(bf16[192,1536]{1,0:T(8,128)(2,1)} %add_convert_fusion.4), channel_id=1, source_target_pairs={{0,2},{1,3},{2,0},{3,1},{4,6},{5,7},{6,4},{7,5},{8,10},{9,11},{10,... | collective-permute-start | bytes 1769480 | tf_op jit(solution)/shard_map/ppermute | solution.py:557
  242.0 19.7 %collective-permute-start.8 = (bf16[96,1536]{1,0:T(8,128)(2,1)S(1)}, bf16[96,1536]{1,0:T(8,128)(2,1)S(1)}, u32[]{:S(2)}, u32[]{:S(2)}) collective-permute-start(bf16[96,1536]{1,0:T(8,128)(2,1)S(1)} %add_convert_fusion.13), channel_id=1, source_target_pairs={{0,8},{1,9},{2,10},{3,11},{4,12},{5,13},{6,14},{7,15},{8,0},{9,1},... | collective-permute-start | bytes 884744 | tf_op jit(solution)/shard_map/ppermute | solution.py:557
  248.0 17.3 %collective-permute-start.16 = (bf16[96,896]{1,0:T(8,128)(2,1)S(1)}, bf16[96,896]{1,0:T(8,128)(2,1)S(1)}, u32[]{:S(2)}, u32[]{:S(2)}) collective-permute-start(bf16[96,896]{1,0:T(8,128)(2,1)S(1)} %add_convert_fusion.16), channel_id=1, source_target_pairs={{0,8},{1,9},{2,10},{3,11},{4,12},{5,13},{6,14},{7,15},{8,0},{9,1},... | collective-permute-start | bytes 516104 | tf_op jit(solution)/shard_map/ppermute | solution.py:557
  252.7 26.6 %collective-permute-start.11 = (bf16[96,1536]{1,0:T(8,128)(2,1)S(1)}, bf16[96,1536]{1,0:T(8,128)(2,1)S(1)}, u32[]{:S(2)}, u32[]{:S(2)}) collective-permute-start(bf16[96,1536]{1,0:T(8,128)(2,1)S(1)} %add_convert_fusion.11), channel_id=1, source_target_pairs={{0,4},{1,5},{2,6},{3,7},{4,0},{5,1},{6,2},{7,3},{8,12},{9,13},{10,... | collective-permute-start | bytes 884744 | tf_op jit(solution)/shard_map/ppermute | solution.py:557
  261.7 36.5 %collective-permute-start.9 = (bf16[96,1536]{1,0:T(8,128)(2,1)S(1)}, bf16[96,1536]{1,0:T(8,128)(2,1)S(1)}, u32[]{:S(2)}, u32[]{:S(2)}) collective-permute-start(bf16[96,1536]{1,0:T(8,128)(2,1)S(1)} %add_convert_fusion.12), channel_id=1, source_target_pairs={{0,4},{1,5},{2,6},{3,7},{4,0},{5,1},{6,2},{7,3},{8,12},{9,13},{10,... | collective-permute-start | bytes 884744 | tf_op jit(solution)/shard_map/ppermute | solution.py:557
  280.6 14.5 %collective-permute-start.12 = (bf16[96,1536]{1,0:T(8,128)(2,1)S(1)}, bf16[96,1536]{1,0:T(8,128)(2,1)S(1)}, u32[]{:S(2)}, u32[]{:S(2)}) collective-permute-start(bf16[96,1536]{1,0:T(8,128)(2,1)S(1)} %add_convert_fusion.10), channel_id=1, source_target_pairs={{0,8},{1,9},{2,10},{3,11},{4,12},{5,13},{6,14},{7,15},{8,0},{9,1},... | collective-permute-start | bytes 884744 | tf_op jit(solution)/shard_map/ppermute | solution.py:557
  283.4 13.4 %collective-permute-start.24 = (bf16[96,768]{1,0:T(8,128)(2,1)S(1)}, bf16[96,768]{1,0:T(8,128)(2,1)S(1)}, u32[]{:S(2)}, u32[]{:S(2)}) collective-permute-start(bf16[96,768]{1,0:T(8,128)(2,1)S(1)} %pad_maximum_fusion.5), channel_id=1, source_target_pairs={{0,8},{1,9},{2,10},{3,11},{4,12},{5,13},{6,14},{7,15},{8,0},{9,1},... | collective-permute-start | bytes 442376 | tf_op jit(solution)/shard_map/ppermute | solution.py:557
  306.1 15.1 %collective-permute-start.34 = (bf16[192,1664]{1,0:T(8,128)(2,1)S(1)}, bf16[192,1664]{1,0:T(8,128)(2,1)S(1)}, u32[]{:S(2)}, u32[]{:S(2)}) collective-permute-start(bf16[192,1664]{1,0:T(8,128)(2,1)S(1)} %pad_maximum_fusion.refs_4_.refs_6_), channel_id=1, source_target_pairs={{0,16},{16,0},{1,17},{17,1},{2,18},{18,2},{3,19},{19,3},{4,20},{20... | collective-permute-start | bytes 1916936 | tf_op jit(solution)/shard_map/ppermute | solution.py:557
  307.6 14.2 %collective-permute-start.31 = (bf16[192,1664]{1,0:T(8,128)(2,1)S(1)}, bf16[192,1664]{1,0:T(8,128)(2,1)S(1)}, u32[]{:S(2)}, u32[]{:S(2)}) collective-permute-start(bf16[192,1664]{1,0:T(8,128)(2,1)S(1)} %pad_maximum_fusion.refs_4_.refs_6_), channel_id=1, source_target_pairs={{0,1},{1,0},{2,3},{3,2},{4,5},{5,4},{6,7},{7,6},{8,9},{9,8},{10,11... | collective-permute-start | bytes 1916936 | tf_op jit(solution)/shard_map/ppermute | solution.py:557
  318.6 15.9 %collective-permute-start.28 = (bf16[192,1664]{1,0:T(8,128)(2,1)S(1)}, bf16[192,1664]{1,0:T(8,128)(2,1)S(1)}, u32[]{:S(2)}, u32[]{:S(2)}) collective-permute-start(bf16[192,1664]{1,0:T(8,128)(2,1)S(1)} %pad_maximum_fusion.refs_4_.refs_6_), channel_id=1, source_target_pairs={{0,4},{1,5},{2,6},{3,7},{4,0},{5,1},{6,2},{7,3},{8,12},{9,13},{10,... | collective-permute-start | bytes 1916936 | tf_op jit(solution)/shard_map/ppermute | solution.py:557
  319.9 13.9 %collective-permute-start.26 = (bf16[192,1536]{1,0:T(8,128)(2,1)S(1)}, bf16[192,1536]{1,0:T(8,128)(2,1)S(1)}, u32[]{:S(2)}, u32[]{:S(2)}) collective-permute-start(bf16[192,1536]{1,0:T(8,128)(2,1)S(1)} %pad_maximum_fusion.1.refs_0_), channel_id=1, source_target_pairs={{0,16},{16,0},{1,17},{17,1},{2,18},{18,2},{3,19},{19,3},{4,20},{20... | collective-permute-start | bytes 1769480 | tf_op jit(solution)/shard_map/ppermute | solution.py:557
  321.1 13.4 %collective-permute-start.27 = (bf16[192,1536]{1,0:T(8,128)(2,1)S(1)}, bf16[192,1536]{1,0:T(8,128)(2,1)S(1)}, u32[]{:S(2)}, u32[]{:S(2)}) collective-permute-start(bf16[192,1536]{1,0:T(8,128)(2,1)S(1)} %pad_maximum_fusion.2.refs_2_), channel_id=1, source_target_pairs={{0,2},{1,3},{2,0},{3,1},{4,6},{5,7},{6,4},{7,5},{8,10},{9,11},{10,... | collective-permute-start | bytes 1769480 | tf_op jit(solution)/shard_map/ppermute | solution.py:557
  337.3 17.1 %collective-permute-start.37 = (bf16[192,1664]{1,0:T(8,128)(2,1)S(1)}, bf16[192,1664]{1,0:T(8,128)(2,1)S(1)}, u32[]{:S(2)}, u32[]{:S(2)}) collective-permute-start(bf16[192,1664]{1,0:T(8,128)(2,1)S(1)} %collective-permute-done.34.refs_4_.refs_7_), channel_id=1, source_target_pairs={{0,4},{1,5},{2,6},{3,7},{4,0},{5,1},{6,2},{7,3},{8,12},{9,13},{10,... | collective-permute-start | bytes 1916936 | tf_op jit(solution)/shard_map/ppermute | solution.py:557
  338.9 15.1 %collective-permute-start.35 = (bf16[192,1536]{1,0:T(8,128)(2,1)S(1)}, bf16[192,1536]{1,0:T(8,128)(2,1)S(1)}, u32[]{:S(2)}, u32[]{:S(2)}) collective-permute-start(bf16[192,1536]{1,0:T(8,128)(2,1)S(1)} %collective-permute-done.32.refs_0_), channel_id=1, source_target_pairs={{0,16},{16,0},{1,17},{17,1},{2,18},{18,2},{3,19},{19,3},{4,20},{20... | collective-permute-start | bytes 1769480 | tf_op jit(solution)/shard_map/ppermute | solution.py:557
  339.3 15.1 %collective-permute-start.36 = (bf16[192,1536]{1,0:T(8,128)(2,1)S(1)}, bf16[192,1536]{1,0:T(8,128)(2,1)S(1)}, u32[]{:S(2)}, u32[]{:S(2)}) collective-permute-start(bf16[192,1536]{1,0:T(8,128)(2,1)S(1)} %collective-permute-done.33.refs_2_), channel_id=1, source_target_pairs={{0,2},{1,3},{2,0},{3,1},{4,6},{5,7},{6,4},{7,5},{8,10},{9,11},{10,... | collective-permute-start | bytes 1769480 | tf_op jit(solution)/shard_map/ppermute | solution.py:557
  (43 other events, 465.7 us)
